TPU v7x, 32 devices: a whole 2x2x4 slice. The times are simulated.
32 devices in a mesh: table: 4 (over x, core), tensor: 2 (over y), dp: 4 (over z).
Axes of the slice: x: 2, y: 2, z: 4, core: 2. Of those that a mesh axis runs over, the one named last changes fastest.
Arguments:
- lookup_ids: int32 [2048, 4, 16], P('dp', 'table'), may hold values from 0 to 4095
- bag_lengths: int32 [2048, 4], P('dp', 'table'), may hold values from 1 to 16
- feature_widths: int32 [4], replicated, may hold values from 32 to 256, as said below
- tables: bfloat16 [4, 4096, 256], P('table', None, 'tensor'), may hold values from -6 to 6
- w_in: bfloat16 [1024, 16384], P(None, ('table', 'tensor')), may hold values from -0.5 to 0.5
- w_out: bfloat16 [16384, 4096], P(('table', 'tensor')), may hold values from -0.125 to 0.125
- cotangent: bfloat16 [2048, 4096], P('dp', ('table', 'tensor')), may hold values from -6 to 6
Outputs:
- mixed_out: bfloat16 [2048, 4096], P('dp', ('table', 'tensor'))
- grad_in: float32 [1024, 16384], P('dp', ('table', 'tensor'))
- grad_out: float32 [16384, 4096], P(('table', 'tensor', 'dp'))
Inputs may be any that keep to these rules, and one draw needn't show every extreme that they name: `feature_widths`: multiples of 32; one feature has exactly 256, another exactly 32.
All inputs are finite; a program needn't handle non-finite values.
Results may differ from a plain program's by a relative error of at most 0.0056.
Values may be sent and summed in bfloat16 or wider, within the bound.
No kernel may reach another device: no remote copies, remote signals or barrier semaphores. Data moves between devices by JAX's collectives and lax.ppermute only.
A program may use at most 128 MiB of HBM per device.

v0:
```python
import jax
import jax.numpy as jnp
from jax import lax
from jax.sharding import PartitionSpec as P


def silu_slope(preact):
    sigmoid_part = jax.nn.sigmoid(preact)
    return sigmoid_part * (1.0 + preact * (1.0 - sigmoid_part))


def pool_local(lookup, lengths, embedding):
    samples, bag_size = lookup.shape
    vocab, half_width = embedding.shape
    vocab_block = min(vocab, 512)
    in_bag = jnp.arange(bag_size)[None, :] < lengths[:, None]
    masked = jnp.where(in_bag, lookup, -1)

    def add_block(running, first_row):
        local_ids = first_row + jnp.arange(vocab_block)
        counts = jnp.sum(masked[:, :, None] == local_ids[None, None, :], axis=1).astype(
            jnp.bfloat16
        )
        table_rows = lax.dynamic_slice_in_dim(embedding, first_row, vocab_block, 0)
        return (running + jnp.dot(counts, table_rows, preferred_element_type=jnp.float32), None)

    starts = jnp.arange(vocab // vocab_block) * vocab_block
    summed, unused = lax.scan(add_block, jnp.zeros((samples, half_width), jnp.float32), starts)
    return summed / lengths[:, None].astype(jnp.float32)


def shards(lookup_ids, bag_lengths, feature_widths, tables, w_in, w_out, cotangent):
    embedding = tables[0]
    half_width = embedding.shape[1]
    summed = pool_local(lookup_ids[:, 0, :], bag_lengths[:, 0], embedding)
    own_width = lax.dynamic_index_in_dim(feature_widths, lax.axis_index("table"), 0, keepdims=False)
    positions = lax.axis_index("tensor") * half_width + jnp.arange(half_width)
    pooled = jnp.where(positions[None, :] < own_width, summed, jnp.zeros_like(summed)).astype(
        jnp.bfloat16
    )
    features = lax.all_gather(pooled, ("table", "tensor"), axis=1, tiled=True)
    preact = jnp.dot(features, w_in, preferred_element_type=jnp.float32)
    hidden = jax.nn.silu(preact).astype(jnp.bfloat16)
    partial_out = jnp.dot(hidden, w_out, preferred_element_type=jnp.float32)
    reduced = lax.psum_scatter(partial_out, ("table", "tensor"), scatter_dimension=1, tiled=True)
    mixed_out = reduced.astype(jnp.bfloat16)
    whole_grad = lax.all_gather(cotangent, ("table", "tensor"), axis=1, tiled=True)
    contract_rows = (((0,), (0,)), ((), ()))
    contract_cols = (((1,), (1,)), ((), ()))
    grad_hidden = lax.dot_general(
        whole_grad, w_out, contract_cols, preferred_element_type=jnp.float32
    )
    grad_preact = (grad_hidden * silu_slope(preact)).astype(jnp.bfloat16)
    term_in = lax.dot_general(
        features, grad_preact, contract_rows, preferred_element_type=jnp.float32
    )
    term_out = lax.dot_general(
        hidden, whole_grad, contract_rows, preferred_element_type=jnp.float32
    )
    grad_in, grad_out = (
        lax.psum_scatter(term_in, "dp", scatter_dimension=0, tiled=True),
        lax.psum_scatter(term_out, "dp", scatter_dimension=0, tiled=True),
    )
    return (mixed_out, grad_in, grad_out)


def solution(mesh):
    return jax.shard_map(
        shards,
        mesh=mesh,
        in_specs=(
            P("dp", "table", None),
            P("dp", "table"),
            P(),
            P("table", None, "tensor"),
            P(None, ("table", "tensor")),
            P(("table", "tensor"), None),
            P("dp", ("table", "tensor")),
        ),
        out_specs=(
            P("dp", ("table", "tensor")),
            P("dp", ("table", "tensor")),
            P(("table", "tensor", "dp"), None),
        ),
        check_vma=False,
    )
```

profile of v0, /device:TPU:0, one launch (start us, length us, event | category | flops | bytes accessed | tf_op | source)
XLA Modules:
  0.0 926.6 jit_solution(2555965209635707534)
XLA Ops:
  7.2 0.0 all-gather.3.cloned.1.call-start
  7.2 0.7 convert_element_type.21
  7.9 0.9 copy.11
  8.8 0.8 bitcast_select_fusion
  9.6 0.0 copy-start.1
  9.6 64.6 %while.11 = (s32[]{:T(128)}, f32[512,128]{1,0:T(8,128)S(1)}, s32[512,16]{1,0:T(8,128)S(1)}, s32[8]{0:T(128)S(1)}, bf16[4096,128]{1,0:T(8,128)(2,1)}, /*index=5*/s32[]{:T(128)}, s32[]{:T(128)}, s32[]{:T(128)}) while((s32[]{:T(128)}, f32[512,128]{1,0:T(8,128)S(1)}, s32[512,16]{1,0:T(8,128)S(1)}, s32[8]{0:T(128)S(1)}, ...), condition=%wide.region_2.3_spmd.clone, body=%wide.region_0.2_spmd.clone.sunk | while | flops 79823368 | bytes 2789533 | solution.py:28
  9.7 0.6 dynamic_slice.19
  12.2 0.6 iota_add_fusion.2
  12.8 3.6 convert_reduce_fusion.2
  16.5 1.2 convolution_add_fusion.2
  17.7 0.6 dynamic_slice.19
  20.3 0.6 iota_add_fusion.2
  20.9 3.6 convert_reduce_fusion.2
  24.6 1.2 convolution_add_fusion.2
  25.8 0.6 dynamic_slice.19
  28.4 0.6 iota_add_fusion.2
  29.0 3.6 convert_reduce_fusion.2
  32.6 1.2 convolution_add_fusion.2
  33.9 0.6 dynamic_slice.19
  36.4 0.6 iota_add_fusion.2
  37.1 3.6 convert_reduce_fusion.2
  40.7 1.2 convolution_add_fusion.2
  42.0 0.6 dynamic_slice.19
  44.5 0.6 iota_add_fusion.2
  45.2 3.6 convert_reduce_fusion.2
  48.8 1.2 convolution_add_fusion.2
  50.1 0.6 dynamic_slice.19
  52.6 0.6 iota_add_fusion.2
  53.2 3.6 convert_reduce_fusion.2
  56.9 1.2 convolution_add_fusion.2
  58.1 0.6 dynamic_slice.19
  60.7 0.6 iota_add_fusion.2
  61.3 3.6 convert_reduce_fusion.2
  65.0 1.2 convolution_add_fusion.2
  66.2 0.6 dynamic_slice.19
  68.7 0.6 iota_add_fusion.2
  69.4 3.6 convert_reduce_fusion.2
  73.0 1.2 convolution_add_fusion.2
  74.3 0.0 copy-done.1
  74.3 0.6 dynamic_slice.11
  74.9 0.7 add_compare_fusion
  75.5 0.8 select_convert_fusion
  76.3 0.0 all-gather.3.cloned.1.call-update
  76.4 0.0 all-gather.5.cloned.1.call-start
  76.4 0.7 all-gather.5.cloned.1.call-update
  77.1 0.0 reduce-scatter.4.cloned.1.call-start
  77.2 25.6 %all-gather.3.cloned.1.call-done = bf16[512,1024]{1,0:T(8,128)(2,1)} async-done(((bf16[512,128]{1,0:T(8,128)(2,1)}), bf16[512,1024]{1,0:T(8,128)(2,1)}) %all-gather.3.cloned.1.call-update) | async-done | bytes 1048592 | tf_op jit(solution)/shard_map/all_gather | solution.py:41
  102.8 4.8 fusion.7
  107.6 0.0 copy-start.2
  107.7 2.0 copy-done.2
  109.7 14.8 %fusion.6 = f32[512,4096]{1,0:T(8,128)} fusion(bf16[2048,4096]{1,0:T(8,128)(2,1)} %param.14, f32[512,2048]{1,0:T(8,128)S(1)} %fusion.7), kind=kOutput, calls=%fused_computation.17 | convolution fusion | flops 8595177472 | bytes 29360128 | tf_op jit(solution)/shard_map/dot_general | solution.py:44
  124.5 0.0 reduce-scatter.4.cloned.1.call-update
  124.5 0.0 reduce-scatter.6.cloned.1.call-start
  124.6 17.6 %all-gather.5.cloned.1.call-done = bf16[512,4096]{1,0:T(8,128)(2,1)} async-done(((bf16[512,512]{1,0:T(8,128)(2,1)}), bf16[512,4096]{1,0:T(8,128)(2,1)}) %all-gather.5.cloned.1.call-update) | async-done | bytes 4194320 | tf_op jit(solution)/shard_map/all_gather | solution.py:47
  142.1 0.0 copy-done
  142.1 19.1 %fusion.3 = f32[1024,2048]{1,0:T(8,128)} fusion(bf16[512,1024]{1,0:T(8,128)(2,1)S(1)} %copy-done, f32[512,2048]{1,0:T(8,128)} %copy-done.2, bf16[512,4096]{1,0:T(8,128)(2,1)} %all-gather.5.cloned.1.call-done, bf16[2048,4096]{1,0:T(8,128)(2,1)} %param.14), kind=kOutput, calls=%fused_computation.9 | convolution fusion | flops 10746855424 | bytes 34603008 | tf_op jit(solution)/shard_map/dot_general | solution.py:54
  161.2 0.0 reduce-scatter.6.cloned.1.call-update
  161.2 0.2 reduce-scatter.8.cloned.1.call-start
  161.5 19.5 %fusion.5 = f32[2048,4096]{1,0:T(8,128)} fusion(bf16[512,4096]{1,0:T(8,128)(2,1)} %all-gather.5.cloned.1.call-done, f32[512,2048]{1,0:T(8,128)} %copy-done.2), kind=kOutput, calls=%fused_computation.16 | convolution fusion | flops 8595177472 | bytes 41943040 | tf_op jit(solution)/shard_map/dot_general | solution.py:57
  180.9 0.0 reduce-scatter.8.cloned.1.call-update
  180.9 36.0 %reduce-scatter.4.cloned.1.call-done = f32[512,512]{1,0:T(8,128)} async-done(((f32[512,4096]{1,0:T(8,128)}), f32[512,512]{1,0:T(8,128)}) %reduce-scatter.4.cloned.1.call-update) | async-done | bytes 1048592 | tf_op jit(solution)/shard_map/reduce_scatter | solution.py:45
  216.9 2.1 convert_element_type.24
  219.0 145.3 %reduce-scatter.6.cloned.1.call-done = f32[256,2048]{1,0:T(8,128)} async-done(((f32[1024,2048]{1,0:T(8,128)}), f32[256,2048]{1,0:T(8,128)}) %reduce-scatter.6.cloned.1.call-update) | async-done | bytes 2097168 | tf_op jit(solution)/shard_map/reduce_scatter | solution.py:61
  364.3 555.7 %reduce-scatter.8.cloned.1.call-done = f32[512,4096]{1,0:T(8,128)} async-done(((f32[2048,4096]{1,0:T(8,128)}), f32[512,4096]{1,0:T(8,128)}) %reduce-scatter.8.cloned.1.call-update) | async-done | bytes 8388624 | tf_op jit(solution)/shard_map/reduce_scatter | solution.py:62
  (3 shorter events, 0.0 us)
Async XLA Ops:
  7.2 95.6 %all-gather.3.cloned.1.call-start = ((), (), s32[]{:S(2)}) async-start(), calls=%async_computation.3 | async-start | bytes 1179648 | tf_op jit(solution)/shard_map/all_gather | solution.py:41
  9.6 64.7 %copy-start.1 = (s32[4]{0:T(128)S(1)}, s32[4]{0:T(128)}, u32[]{:S(2)}) copy-start(s32[4]{0:T(128)} %param.11) | copy-start | bytes 52
  76.4 65.8 %all-gather.5.cloned.1.call-start = ((), (), s32[]{:S(2)}) async-start(), calls=%async_computation.5 | async-start | bytes 4718592 | tf_op jit(solution)/shard_map/all_gather | solution.py:47
  77.1 139.8 %reduce-scatter.4.cloned.1.call-start = ((), (), s32[]{:S(2)}) async-start(), calls=%async_computation.4 | async-start | bytes 9437184 | tf_op jit(solution)/shard_map/reduce_scatter | solution.py:45
  107.6 2.0 copy-start.2
  124.5 17.6 %copy-start = (bf16[512,1024]{1,0:T(8,128)(2,1)S(1)}, bf16[512,1024]{1,0:T(8,128)(2,1)}, u32[]{:S(2)}) copy-start(bf16[512,1024]{1,0:T(8,128)(2,1)} %all-gather.3.cloned.1.call-done) | copy-start | bytes 3145732
  124.5 239.8 %reduce-scatter.6.cloned.1.call-start = ((), (), s32[]{:S(2)}) async-start(), calls=%async_computation.6 | async-start | bytes 10485760 | tf_op jit(solution)/shard_map/reduce_scatter | solution.py:61
  161.2 758.8 %reduce-scatter.8.cloned.1.call-start = ((), (), s32[]{:S(2)}) async-start(), calls=%async_computation.7 | async-start | bytes 41943040 | tf_op jit(solution)/shard_map/reduce_scatter | solution.py:62
Sparse Core Ops, SparseCore 0:
  76.5 26.2 all-gather.2
  104.7 37.4 all-gather.4
  145.6 71.2 reduce-scatter.3
  219.8 144.4 reduce-scatter.5
  367.2 552.7 reduce-scatter.7
where the time goes:
time: 927 us
  waiting for transfers between devices  781 us (84%)
  matrix products  68.1 us (7%)
  other arithmetic  39.2 us (4%)
  loops' own time  15.9 us (2%)
  between operations  13.9 us (1%)
    reduce_scatter x1, waiting for transfers between devices, shards(): lax.psum_scatter(term_out, 'dp', scatter_dimension=0, tiled=True)  556 us
    reduce_scatter x1, waiting for transfers between devices, shards(): lax.psum_scatter(term_in, 'dp', scatter_dimension=0, tiled=True)  145 us
    reduce_scatter x1, waiting for transfers between devices, shards(): lax.psum_scatter(partial_out, ('table', 'tensor'), scatter_dimension=1, t...  36 us
    reduce_sum x8, other arithmetic, add_block(): jnp.sum(masked[:, :, None] == local_ids[None, None, :], axis=1)  29 us
    all_gather x1, waiting for transfers between devices, shards(): features = lax.all_gather(pooled, ('table', 'tensor'), axis=1, tiled=True)  25.6 us
    dot_general x1, matrix products, shards(): lax.dot_general(hidden, whole_grad, contract_rows, preferred_element_type...  19.5 us
    dot_general x1, matrix products, shards(): lax.dot_general(features, grad_preact, contract_rows, preferred_element_t...  19.1 us
  transfers between devices with their start and end apart: 5, of which 5 were waited for; matrix products, arithmetic and copies ran while one was open for 7% of the time, Pallas kernels for 0%

commit v1 on v0

v1 whole, which is shorter than its diff:
```python
import functools

import jax
import jax.numpy as jnp
from jax import lax
from jax.experimental import pallas as pl
from jax.experimental.pallas import tpu as pltpu
from jax.sharding import PartitionSpec as P

F32 = jnp.float32
BF16 = jnp.bfloat16
PLANE = ("table", "tensor")
ROWS_TN = (((0,), (0,)), ((), ()))
COLS_NT = (((1,), (1,)), ((), ()))


def silu_slope(preact):
    sigmoid_part = jax.nn.sigmoid(preact)
    return sigmoid_part * (1.0 + preact * (1.0 - sigmoid_part))


def params(mib):
    return pltpu.CompilerParams(vmem_limit_bytes=mib * 1024 * 1024)


def pool_kernel(width_ref, hi_ref, lo_ref, len_ref, table_ref, out_ref, counts_ref, *, group, low):
    samples = out_ref.shape[0]
    slots = hi_ref.shape[1]
    high = table_ref.shape[0] // low
    rows = lax.broadcasted_iota(jnp.int32, (high * group, slots), 0)
    low_rows = lax.broadcasted_iota(jnp.int32, (low, slots), 0)

    def one_group(g, carry):
        hit_high = (rows == hi_ref[pl.ds(g, 1), :]).astype(BF16)
        hit_low = (low_rows == lo_ref[pl.ds(g, 1), :]).astype(BF16)
        counts = lax.dot_general(hit_high, hit_low, COLS_NT, preferred_element_type=F32).astype(BF16)
        first = pl.multiple_of(g * group, group)
        for h in range(high):
            counts_ref[h, pl.ds(first, group), :] = counts[h * group : (h + 1) * group, :]
        return carry

    lax.fori_loop(0, samples // group, one_group, 0)
    total = jnp.zeros(out_ref.shape, F32)
    for h in range(high):
        total += jnp.dot(
            counts_ref[h], table_ref[h * low : (h + 1) * low, :], preferred_element_type=F32
        )
    pooled = total / len_ref[...].astype(F32)
    columns = width_ref[1] + lax.broadcasted_iota(jnp.int32, pooled.shape, 1)
    out_ref[...] = jnp.where(columns < width_ref[0], pooled, 0.0).astype(BF16)


def pool_local(lookup, lengths, embedding, own_width, first_column):
    samples, bag = lookup.shape
    vocab, columns = embedding.shape
    low, group = 256, 16
    high = vocab // low
    in_bag = jnp.arange(bag)[None, :] < lengths[:, None]
    sample_in_group = (jnp.arange(samples) % group)[:, None]
    hi_key = jnp.where(in_bag, (lookup // low) * group + sample_in_group, -1)
    lo_key = lookup % low
    return pl.pallas_call(
        functools.partial(pool_kernel, group=group, low=low),
        out_shape=jax.ShapeDtypeStruct((samples, columns), BF16),
        in_specs=[pl.BlockSpec(memory_space=pltpu.SMEM)] + [pl.BlockSpec(memory_space=pltpu.VMEM)] * 4,
        out_specs=pl.BlockSpec(memory_space=pltpu.VMEM),
        scratch_shapes=[pltpu.VMEM((high, samples, low), BF16)],
        compiler_params=params(48),
        name="pool",
    )(
        jnp.stack([own_width, first_column]).astype(jnp.int32),
        hi_key.reshape(samples // group, group * bag),
        lo_key.reshape(samples // group, group * bag),
        lengths[:, None],
        embedding,
    )


def place_kernel(place_ref, own_ref, other_ref, out_ref):
    j = pl.program_id(1)
    half = pl.num_programs(1) // 2

    @pl.when(j < half)
    def _():
        out_ref[...] = own_ref[0]

    @pl.when(j >= half)
    def _():
        out_ref[...] = other_ref[0]


def place_features(place, own, other):
    half, chunks, samples, columns = own.shape
    slots = 2 * half
    return pl.pallas_call(
        place_kernel,
        out_shape=jax.ShapeDtypeStruct((chunks, samples, slots * columns), BF16),
        grid_spec=pltpu.PrefetchScalarGridSpec(
            num_scalar_prefetch=1,
            grid=(chunks, slots),
            in_specs=[
                pl.BlockSpec((1, 1, samples, columns), lambda k, j, p: (jnp.minimum(j, half - 1), k, 0, 0)),
                pl.BlockSpec((1, 1, samples, columns), lambda k, j, p: (jnp.maximum(j - half, 0), k, 0, 0)),
            ],
            out_specs=pl.BlockSpec((1, samples, columns), lambda k, j, p: (k, 0, p[j])),
        ),
        compiler_params=params(32),
        name="place_features",
    )(place, own, other)


def hidden_kernel(feat_ref, w_ref, out_ref):
    preact = jnp.dot(feat_ref[...], w_ref[...], preferred_element_type=F32)
    out_ref[...] = jax.nn.silu(preact).astype(BF16)


def hidden_of(feat, w_in):
    samples, depth = feat.shape
    units = w_in.shape[1]
    wide = min(units, 512)
    return pl.pallas_call(
        hidden_kernel,
        out_shape=jax.ShapeDtypeStruct((samples, units), BF16),
        grid=(units // wide,),
        in_specs=[
            pl.BlockSpec((samples, depth), lambda i: (0, 0)),
            pl.BlockSpec((depth, wide), lambda i: (0, i)),
        ],
        out_specs=pl.BlockSpec((samples, wide), lambda i: (0, i)),
        compiler_params=params(48),
        name="hidden",
    )(feat, w_in)


def mixed_kernel(place_ref, hidden_ref, w_ref, out_ref):
    product = jnp.dot(hidden_ref[...], w_ref[...], preferred_element_type=F32)
    out_ref[0] = product.astype(out_ref.dtype)


def mixed_blocks(place, hidden, w_out, wide, dtype):
    samples, units = hidden.shape
    slots = place.shape[0]
    return pl.pallas_call(
        mixed_kernel,
        out_shape=jax.ShapeDtypeStruct((slots, samples, wide), dtype),
        grid_spec=pltpu.PrefetchScalarGridSpec(
            num_scalar_prefetch=1,
            grid=(slots,),
            in_specs=[
                pl.BlockSpec((samples, units), lambda j, p: (0, 0)),
                pl.BlockSpec((units, wide), lambda j, p: (0, p[j])),
            ],
            out_specs=pl.BlockSpec((1, samples, wide), lambda j, p: (j, 0, 0)),
        ),
        compiler_params=params(48),
        name="mixed",
    )(place, hidden, w_out)


def chunk_kernel(
    place_ref, own_ref, other_ref, w_out_ref, feat_ref, w_in_ref, sum_ref,
    hidden_ref, grad_in_ref, grad_hidden_ref,
):
    j = pl.program_id(0)
    slots = pl.num_programs(0)
    half = slots // 2

    @pl.when(j == 0)
    def _():
        grad_hidden_ref[...] = jnp.zeros_like(grad_hidden_ref)

    @pl.when(j < half)
    def _():
        grad_hidden_ref[...] += lax.dot_general(
            own_ref[0], w_out_ref[...], COLS_NT, preferred_element_type=F32
        )

    @pl.when(j >= half)
    def _():
        grad_hidden_ref[...] += lax.dot_general(
            other_ref[0], w_out_ref[...], COLS_NT, preferred_element_type=F32
        )

    @pl.when(j == slots - 1)
    def _():
        preact = jnp.dot(feat_ref[0], w_in_ref[...], preferred_element_type=F32)
        hidden_ref[...] = jax.nn.silu(preact).astype(BF16)
        grad_preact = (grad_hidden_ref[...] * silu_slope(preact)).astype(BF16)
        grad_in_ref[...] = sum_ref[...] + lax.dot_general(
            feat_ref[0], grad_preact, ROWS_TN, preferred_element_type=F32
        )


def chunk_backward(place, own, other, w_out, features, w_in, chunk, running, units):
    half, samples, wide = own.shape
    slots = 2 * half
    depth = w_in.shape[0]
    return pl.pallas_call(
        chunk_kernel,
        out_shape=(
            jax.ShapeDtypeStruct((samples, units), BF16),
            jax.ShapeDtypeStruct((depth, units), F32),
        ),
        grid_spec=pltpu.PrefetchScalarGridSpec(
            num_scalar_prefetch=1,
            grid=(slots,),
            in_specs=[
                pl.BlockSpec((1, samples, wide), lambda j, p: (jnp.minimum(j, half - 1), 0, 0)),
                pl.BlockSpec((1, samples, wide), lambda j, p: (jnp.maximum(j - half, 0), 0, 0)),
                pl.BlockSpec((units, wide), lambda j, p: (p[slots], p[j])),
                pl.BlockSpec((1, samples, depth), lambda j, p: (chunk, 0, 0)),
                pl.BlockSpec((depth, units), lambda j, p: (0, p[slots])),
                pl.BlockSpec((depth, units), lambda j, p: (0, 0)),
            ],
            out_specs=[
                pl.BlockSpec((samples, units), lambda j, p: (0, 0)),
                pl.BlockSpec((depth, units), lambda j, p: (0, 0)),
            ],
            scratch_shapes=[pltpu.VMEM((samples, units), F32)],
        ),
        compiler_params=params(48),
        name="chunk_backward",
    )(place, own, other, w_out, features, w_in, running)


def grad_out_kernel(place_ref, *refs):
    chunks = (len(refs) - 2) // 3
    hidden, own, other = refs[:chunks], refs[chunks : 2 * chunks], refs[2 * chunks : 3 * chunks]
    out_ref, turned_ref = refs[3 * chunks :]
    j = pl.program_id(0)
    half = pl.num_programs(0) // 2
    samples = hidden[0].shape[0]

    @pl.when(j == 0)
    def _():
        for k in range(chunks):
            turned_ref[:, k * samples : (k + 1) * samples] = hidden[k][...].T

    def product(blocks):
        total = None
        for k in range(chunks):
            term = jnp.dot(
                turned_ref[:, k * samples : (k + 1) * samples], blocks[k][0], preferred_element_type=F32
            )
            total = term if total is None else total + term
        out_ref[...] = total

    @pl.when(j < half)
    def _():
        product(own)

    @pl.when(j >= half)
    def _():
        product(other)


def grad_out_of(place, hidden, own, other):
    chunks = len(hidden)
    samples, units = hidden[0].shape
    half, unused, wide = own[0].shape
    slots = 2 * half
    return pl.pallas_call(
        grad_out_kernel,
        out_shape=jax.ShapeDtypeStruct((units, slots * wide), F32),
        grid_spec=pltpu.PrefetchScalarGridSpec(
            num_scalar_prefetch=1,
            grid=(slots,),
            in_specs=[pl.BlockSpec((samples, units), lambda j, p: (0, 0))] * chunks
            + [pl.BlockSpec((1, samples, wide), lambda j, p: (jnp.minimum(j, half - 1), 0, 0))] * chunks
            + [pl.BlockSpec((1, samples, wide), lambda j, p: (jnp.maximum(j - half, 0), 0, 0))] * chunks,
            out_specs=pl.BlockSpec((units, wide), lambda j, p: (0, p[j])),
            scratch_shapes=[pltpu.VMEM((units, chunks * samples), BF16)],
        ),
        compiler_params=params(56),
        name="grad_out",
    )(place, *hidden, *own, *other)


def plane_perms():
    first, second = [], []
    for t in range(4):
        for y in range(2):
            along_x, along_y = (t ^ 2) * 2 + y, t * 2 + (y ^ 1)
            first.append((t * 2 + y, along_x if t % 2 == 0 else along_y))
            second.append((t * 2 + y, along_y if t % 2 == 0 else along_x))
    return first, second


PERM_A, PERM_B = plane_perms()


def move_a(v):
    return lax.ppermute(v, PLANE, PERM_A)


def move_b(v):
    return lax.ppermute(v, PLANE, PERM_B)


def swap(v):
    return lax.ppermute(v, "table", [(t, t ^ 1) for t in range(4)])


def move_z(v, k):
    return lax.ppermute(v, "dp", [(z, z ^ k) for z in range(4)])


def plane_blocks():
    t, y = lax.axis_index("table"), lax.axis_index("tensor")
    x, core = t // 2, t % 2
    blocks = []
    for dc in range(2):
        c = core ^ dc
        a_x, a_y = jnp.where(c == 0, 1, 0), jnp.where(c == 0, 0, 1)
        for dx, dy in ((0, 0), (a_x, a_y), (a_y, a_x), (1, 1)):
            blocks.append(((x ^ dx) * 2 + c) * 2 + (y ^ dy))
    return jnp.stack(blocks).astype(jnp.int32)


def spread_shards(lookup_ids, bag_lengths, feature_widths, tables, w_in, w_out, cotangent):
    embedding = tables[0]
    half_width = embedding.shape[1]
    z = lax.axis_index("dp")
    samples, wide = cotangent.shape
    units = w_in.shape[1] // 4
    blocks = plane_blocks()
    place = jnp.concatenate([blocks, z[None].astype(jnp.int32)])

    s0 = cotangent
    a0, b0 = move_a(s0), move_b(s0)
    s2 = move_z(s0, 2)

    own_width = lax.dynamic_index_in_dim(feature_widths, lax.axis_index("table"), 0, keepdims=False)
    pooled = pool_local(
        lookup_ids[:, 0, :], bag_lengths[:, 0], embedding, own_width, lax.axis_index("tensor") * half_width
    )
    p_all = jnp.stack([pooled] + [move_z(pooled, k) for k in (1, 2, 3)])
    pa, pb = move_a(p_all), move_b(p_all)
    pd = move_b(pa)
    own_feat = jnp.stack([p_all, pa, pb, pd])
    features = place_features(blocks, own_feat, swap(own_feat))

    d0 = move_b(a0)
    own0 = jnp.stack([s0, a0, b0, d0])
    own1 = move_z(own0, 1)
    a2, b2 = move_a(s2), move_b(s2)
    own2 = jnp.stack([s2, a2, b2, move_b(a2)])
    s3 = move_z(s0, 3)
    a3, b3 = move_a(s3), move_b(s3)
    own3 = jnp.stack([s3, a3, b3, move_b(a3)])
    own = [own0, own1, own2, own3]
    other = [swap(v) for v in own]

    hidden_here = hidden_of(features[0], w_in)
    away = mixed_blocks(blocks[4:], hidden_here, w_out, wide, BF16)
    near = mixed_blocks(blocks[:4], hidden_here, w_out, wide, F32)
    near = near + swap(away).astype(F32)
    to_a = near[1] + move_b(near[3].astype(BF16)).astype(F32)
    mixed_out = near[0] + move_b(near[2].astype(BF16)).astype(F32)
    mixed_out = (mixed_out + move_a(to_a.astype(BF16)).astype(F32)).astype(BF16)

    hidden = [None] * 4
    running = jnp.zeros((w_in.shape[0], units), F32)
    for k in (0, 2, 1, 3):
        hidden[k], running = chunk_backward(
            place, own[k], other[k], w_out, features, w_in, k, running, units
        )
    rows = w_in.shape[0] // 4
    grad_in = jnp.zeros((rows, 4 * units), F32)
    for k in range(4):
        part = lax.dynamic_slice_in_dim(running, (z ^ k) * rows, rows, 0)
        part = part if k == 0 else move_z(part.astype(BF16), k).astype(F32)
        grad_in = lax.dynamic_update_slice_in_dim(grad_in, part, (z ^ k) * units, 1)
    grad_out = grad_out_of(blocks, hidden, own, other)
    return (mixed_out, grad_in, grad_out)


def summed_shards(lookup_ids, bag_lengths, feature_widths, tables, w_in, w_out, cotangent):
    embedding = tables[0]
    half_width = embedding.shape[1]
    own_width = lax.dynamic_index_in_dim(feature_widths, lax.axis_index("table"), 0, keepdims=False)
    pooled = pool_local(
        lookup_ids[:, 0, :], bag_lengths[:, 0], embedding, own_width, lax.axis_index("tensor") * half_width
    )
    features = lax.all_gather(pooled, PLANE, axis=1, tiled=True)
    preact = jnp.dot(features, w_in, preferred_element_type=F32)
    hidden = jax.nn.silu(preact).astype(BF16)
    partial_out = jnp.dot(hidden, w_out, preferred_element_type=F32)
    reduced = lax.psum_scatter(partial_out, PLANE, scatter_dimension=1, tiled=True)
    mixed_out = reduced.astype(BF16)
    whole_grad = lax.all_gather(cotangent, PLANE, axis=1, tiled=True)
    grad_hidden = lax.dot_general(whole_grad, w_out, COLS_NT, preferred_element_type=F32)
    grad_preact = (grad_hidden * silu_slope(preact)).astype(BF16)
    term_in = lax.dot_general(features, grad_preact, ROWS_TN, preferred_element_type=F32)
    term_out = lax.dot_general(hidden, whole_grad, ROWS_TN, preferred_element_type=F32)
    grad_in = lax.psum_scatter(term_in, "dp", scatter_dimension=0, tiled=True)
    grad_out = lax.psum_scatter(term_out, "dp", scatter_dimension=0, tiled=True)
    return (mixed_out, grad_in, grad_out)


def solution(mesh):
    sizes = (mesh.shape["table"], mesh.shape["tensor"], mesh.shape["dp"])
    return jax.shard_map(
        spread_shards if sizes == (4, 2, 4) else summed_shards,
        mesh=mesh,
        in_specs=(
            P("dp", "table", None),
            P("dp", "table"),
            P(),
            P("table", None, "tensor"),
            P(None, PLANE),
            P(PLANE, None),
            P("dp", PLANE),
        ),
        out_specs=(
            P("dp", PLANE),
            P("dp", PLANE),
            P(("table", "tensor", "dp"), None),
        ),
        check_vma=False,
    )
```

time: 927 us -> 309 us (0.33)
  waiting for transfers between devices: 781 us -> 130 us
  Pallas kernels: 0 us -> 110 us
  matrix products: 68.1 us -> 0 us
  starting transfers between devices: 0.38 us -> 31.5 us
  other arithmetic: 39.2 us -> 18.7 us
  loops' own time: 15.9 us -> 0 us
  between operations: 13.9 us -> 0.97 us
    reduce_scatter x3 -> x0, waiting for transfers between devices: 737 us -> none  [the longest x1 556 us: shards(): lax.psum_scatter(term_out, 'dp', scatter_dimension=0, tiled=True)]
    ppermute x0 -> x30, waiting for transfers between devices: none -> 130 us  [the longest x9 74.1 us: move_z(): return lax.ppermute(v, 'dp', [(z, z ^ k) for z in range(4)])]
    pallas_call x0 -> x10, Pallas kernels: none -> 110 us  [the longest x4 45.1 us: chunk_backward(): pl.pallas_call(chunk_kernel, out_shape=(jax.ShapeDtypeStruct((samples, un...]
    dot_general x12 -> x0, matrix products: 68.1 us -> none  [the longest x1 19.5 us: shards(): lax.dot_general(hidden, whole_grad, contract_rows, preferred_element_type...]
    all_gather x2 -> x0, waiting for transfers between devices: 43.2 us -> none  [the longest x1 25.6 us: shards(): features = lax.all_gather(pooled, ('table', 'tensor'), axis=1, tiled=True)]
    ppermute x0 -> x30, starting transfers between devices: none -> 31.5 us  [the longest x9 14.6 us: move_z(): return lax.ppermute(v, 'dp', [(z, z ^ k) for z in range(4)])]
    reduce_sum x8 -> x0, other arithmetic: 29 us -> none  [add_block(): jnp.sum(masked[:, :, None] == local_ids[None, None, :], axis=1)]
    another operation x1 -> x0, loops' own time: 15.9 us -> none  [pool_local(): lax.scan(add_block, jnp.zeros((samples, half_width), jnp.float32), starts)]
  transfers between devices with their start and end apart: 5 -> 30, of which waited for: 5 -> 12; matrix products, arithmetic and copies ran while one was open for 7% -> 6% of each run, Pallas kernels for 0% -> 33%
where the time goes in v1:
time: 309 us; the launch traced here: 308 us
  waiting for transfers between devices  130 us (42%)
  Pallas kernels  110 us (36%)
  starting transfers between devices  31.5 us (10%)
  other arithmetic  18.7 us (6%)
  local copies, waits for them, and re-layouts  16.5 us (5%)
    ppermute x9, waiting for transfers between devices, move_z(): return lax.ppermute(v, 'dp', [(z, z ^ k) for z in range(4)])  74.1 us
    pallas_call x4, Pallas kernels, chunk_backward(): pl.pallas_call(chunk_kernel, out_shape=(jax.ShapeDtypeStruct((samples, un...  45.1 us
    ppermute x10, waiting for transfers between devices, move_b(): return lax.ppermute(v, PLANE, PERM_B)  44.1 us
    pallas_call x1, Pallas kernels, grad_out_of(): pl.pallas_call(grad_out_kernel, out_shape=jax.ShapeDtypeStruct((units, sl...  18.2 us
    pallas_call x2, Pallas kernels, mixed_blocks(): pl.pallas_call(mixed_kernel, out_shape=jax.ShapeDtypeStruct((slots, sampl...  16.7 us
    pallas_call x1, Pallas kernels, place_features(): pl.pallas_call(place_kernel, out_shape=jax.ShapeDtypeStruct((chunks, samp...  16.4 us
    ppermute x9, starting transfers between devices, move_z(): return lax.ppermute(v, 'dp', [(z, z ^ k) for z in range(4)])  14.6 us
    ppermute x5, waiting for transfers between devices, move_a(): return lax.ppermute(v, PLANE, PERM_A)  11.7 us
  transfers between devices with their start and end apart: 30, of which 12 were waited for; matrix products, arithmetic and copies ran while one was open for 6% of the time, Pallas kernels for 33%

profile of v1, /device:TPU:0, one launch (start us, length us, event | category | flops | bytes accessed | tf_op | source)
XLA Modules:
  0.0 307.8 jit_solution(15326044478119422009)
XLA Ops:
  0.7 1.0 copy.14
  1.9 0.9 copy.16.len_ref
  2.8 0.5 broadcast.63
  3.3 1.3 reduce.3
  5.0 1.2 dynamic_slice.16
  6.2 0.7 pad_add_fusion.1.width_ref
  7.0 9.1 %pool.1 = bf16[512,128]{1,0:T(8,128)(2,1)S(1)} custom-call(s32[2]{0:T(128)S(1)} %pad_add_fusion.1.width_ref, s32[32,256]{1,0:T(8,128)S(1)} %get-tuple-element.29.hi_ref, s32[32,256]{1,0:T(8,128)S(1)} %get-tuple-element.28.lo_ref, s32[512,1]{1,0:T(8,128)S(1)} %copy.16.len_ref, bf16[4096,128]{1,0:T(8,128)(2,1)S(1)} %bitcast.57), custom_call_target="tpu_custom_call" | custom-call | tf_op jit(solution)/shard_map/pool/pallas_call | solution.py:62
  16.0 5.1 %collective-permute-start.2 = (bf16[512,128]{1,0:T(8,128)(2,1)S(1)}, bf16[512,128]{1,0:T(8,128)(2,1)S(1)}, u32[]{:S(2)}, u32[]{:S(2)}) collective-permute-start(bf16[512,128]{1,0:T(8,128)(2,1)S(1)} %pool.1), channel_id=1, source_target_pairs={{0,3},{1,2},{2,1},{3,0},{4,7},{5,6},{6,5},{7,4},{8,11},{9,10},{10,... | collective-permute-start | bytes 393224 | tf_op jit(solution)/shard_map/ppermute | solution.py:305
  21.2 0.6 collective-permute-start
  21.8 3.8 %collective-permute-done.2 = bf16[512,128]{1,0:T(8,128)(2,1)S(1)} collective-permute-done((bf16[512,128]{1,0:T(8,128)(2,1)S(1)}, bf16[512,128]{1,0:T(8,128)(2,1)S(1)}, u32[]{:S(2)}, u32[]{:S(2)}) %collective-permute-start.2) | collective-permute-done | bytes 131104 | tf_op jit(solution)/shard_map/ppermute | solution.py:305
  25.6 6.6 %collective-permute-done.1 = bf16[512,128]{1,0:T(8,128)(2,1)S(1)} collective-permute-done((bf16[512,128]{1,0:T(8,128)(2,1)S(1)}, bf16[512,128]{1,0:T(8,128)(2,1)S(1)}, u32[]{:S(2)}, u32[]{:S(2)}) %collective-permute-start.1) | collective-permute-done | bytes 131104 | tf_op jit(solution)/shard_map/ppermute | solution.py:305
  32.3 1.6 collective-permute-start.3
  33.9 1.5 collective-permute-start.4
  35.4 11.7 %collective-permute-done.3 = bf16[4,512,128]{2,1,0:T(8,128)(2,1)S(1)} collective-permute-done((bf16[4,512,128]{2,1,0:T(8,128)(2,1)S(1)}, bf16[4,512,128]{2,1,0:T(8,128)(2,1)S(1)}, u32[]{:S(2)}, u32[]{:S(2)}) %collective-permute-start.3) | collective-permute-done | bytes 524320 | tf_op jit(solution)/shard_map/ppermute | solution.py:293
  47.3 1.4 collective-permute-start.16
  48.7 9.4 %collective-permute-done.5 = bf16[4,512,128]{2,1,0:T(8,128)(2,1)S(1)} collective-permute-done((bf16[4,512,128]{2,1,0:T(8,128)(2,1)S(1)}, bf16[4,512,128]{2,1,0:T(8,128)(2,1)S(1)}, u32[]{:S(2)}, u32[]{:S(2)}) %collective-permute-start.5) | collective-permute-done | bytes 524320 | tf_op jit(solution)/shard_map/ppermute | solution.py:297
  58.1 1.6 pad_maximum_fusion.own_ref
  59.7 1.5 collective-permute-start.17
  61.7 7.2 %collective-permute-done.17 = bf16[512,512]{1,0:T(8,128)(2,1)S(1)} collective-permute-done((bf16[512,512]{1,0:T(8,128)(2,1)S(1)}, bf16[512,512]{1,0:T(8,128)(2,1)S(1)}, u32[]{:S(2)}, u32[]{:S(2)}) %collective-permute-start.17) | collective-permute-done | bytes 524320 | tf_op jit(solution)/shard_map/ppermute | solution.py:297
  68.9 5.6 %collective-permute-done.18 = bf16[512,512]{1,0:T(8,128)(2,1)S(1)} collective-permute-done((bf16[512,512]{1,0:T(8,128)(2,1)S(1)}, bf16[512,512]{1,0:T(8,128)(2,1)S(1)}, u32[]{:S(2)}, u32[]{:S(2)}) %collective-permute-start.18) | collective-permute-done | bytes 524320 | tf_op jit(solution)/shard_map/ppermute | solution.py:297
  74.8 2.7 collective-permute-start.21
  77.5 1.7 collective-permute-start.11
  79.3 52.8 %collective-permute-done.21 = bf16[512,512]{1,0:T(8,128)(2,1)} collective-permute-done((bf16[512,512]{1,0:T(8,128)(2,1)S(1)}, bf16[512,512]{1,0:T(8,128)(2,1)}, u32[]{:S(2)}, u32[]{:S(2)}) %collective-permute-start.21) | collective-permute-done | bytes 524320 | tf_op jit(solution)/shard_map/ppermute | solution.py:305
  132.5 1.5 collective-permute-start.23
  134.0 10.9 %collective-permute-done.11 = bf16[512,512]{1,0:T(8,128)(2,1)S(1)} collective-permute-done((bf16[512,512]{1,0:T(8,128)(2,1)S(1)}, bf16[512,512]{1,0:T(8,128)(2,1)S(1)}, u32[]{:S(2)}, u32[]{:S(2)}) %collective-permute-start.11) | collective-permute-done | bytes 524320 | tf_op jit(solution)/shard_map/ppermute | solution.py:305
  145.2 16.4 %place_features.1.feat_ref = bf16[4,512,1024]{2,1,0:T(8,128)(2,1)S(1)} custom-call(s32[8]{0:T(128)S(1)} %stack.122.place_ref, bf16[4,4,512,128]{3,2,1,0:T(8,128)(2,1)} %pad_maximum_fusion.own_ref, bf16[4,4,512,128]{3,2,1,0:T(8,128)(2,1)} %collective-permute-done.6.other_ref), custom_call_target="tpu_custom_call" | custom-call | tf_op jit(solution)/shard_map/place_features/pallas_call | solution.py:95
  161.6 2.0 copy-done
  163.7 4.8 %hidden.1.hidden_ref = bf16[512,2048]{1,0:T(8,128)(2,1)S(1)} custom-call(bf16[512,1024]{1,0:T(8,128)(2,1)S(1)} %slice_bitcast_fusion.2.feat_ref, bf16[1024,2048]{1,0:T(8,128)(2,1)} %w_in_ref.7), custom_call_target="tpu_custom_call" | custom-call | tf_op jit(solution)/shard_map/hidden/pallas_call | solution.py:121
  168.5 7.6 %mixed.3 = bf16[4,512,512]{2,1,0:T(8,128)(2,1)S(1)} custom-call(s32[4]{0:T(128)S(1)} %pad_add_fusion.2.place_ref, bf16[512,2048]{1,0:T(8,128)(2,1)S(1)} %hidden.1.hidden_ref, bf16[2048,4096]{1,0:T(8,128)(2,1)} %w_out_ref.7), custom_call_target="tpu_custom_call" | custom-call | tf_op jit(solution)/shard_map/mixed/pallas_call | solution.py:143
  176.2 1.6 collective-permute-start.24
  177.8 0.5 collective-permute-start.13
  178.3 1.5 collective-permute-start.14
  179.8 5.6 %collective-permute-done.24 = bf16[512,512]{1,0:T(8,128)(2,1)S(1)} collective-permute-done((bf16[512,512]{1,0:T(8,128)(2,1)S(1)}, bf16[512,512]{1,0:T(8,128)(2,1)S(1)}, u32[]{:S(2)}, u32[]{:S(2)}) %collective-permute-start.24) | collective-permute-done | bytes 524320 | tf_op jit(solution)/shard_map/ppermute | solution.py:297
  185.5 2.6 pad_maximum_fusion.3.own_ref.refs_6_
  188.1 3.0 collective-permute-done.13
  191.6 5.1 %collective-permute-done.14 = bf16[512,512]{1,0:T(8,128)(2,1)S(1)} collective-permute-done((bf16[512,512]{1,0:T(8,128)(2,1)S(1)}, bf16[512,512]{1,0:T(8,128)(2,1)S(1)}, u32[]{:S(2)}, u32[]{:S(2)}) %collective-permute-start.14) | collective-permute-done | bytes 524320 | tf_op jit(solution)/shard_map/ppermute | solution.py:297
  196.7 1.6 pad_maximum_fusion.1.own_ref.refs_7_
  198.3 9.0 %mixed.2 = f32[4,512,512]{2,1,0:T(8,128)} custom-call(s32[4]{0:T(128)S(1)} %pad_add_fusion.place_ref, bf16[512,2048]{1,0:T(8,128)(2,1)S(1)} %hidden.1.hidden_ref, bf16[2048,4096]{1,0:T(8,128)(2,1)} %w_out_ref.7), custom_call_target="tpu_custom_call" | custom-call | tf_op jit(solution)/shard_map/mixed/pallas_call | solution.py:143
  207.4 5.1 %fusion.14 = (bf16[4,512,512]{2,1,0:T(8,128)(2,1)S(1)}, f32[4,512,512]{2,1,0:T(8,128)}) fusion(f32[4,512,512]{2,1,0:T(8,128)} %mixed.2, bf16[4,512,512]{2,1,0:T(8,128)(2,1)S(1)} %collective-permute-done.7), kind=kLoop, calls=%fused_computation.43 | loop fusion | flops 3145728 | bytes 12582912 | tf_op jit(solution)/shard_map/convert.1
  212.5 1.6 collective-permute-start.9
  214.2 1.6 broadcast_in_dim.15.sum_ref
  215.8 10.9 %chunk_backward.4 = (bf16[512,512]{1,0:T(8,128)(2,1)S(1)}, f32[1024,512]{1,0:T(8,128)S(1)}) custom-call(s32[9]{0:T(128)S(1)} %concatenate.6.place_ref, bf16[4,512,512]{2,1,0:T(8,128)(2,1)S(1)} %pad_maximum_fusion.2.own_ref.refs_4_, bf16[4,512,512]{2,1,0:T(8,128)(2,1)} %collective-permute-done.26.other_ref.refs_8_, bf16[2048,4096]{1,0:T(8,128)(2,1)} %w_out_ref.7, ...), custom_call_target="tpu_custom_call" | custom-call | tf_op jit(solution)/shard_map/chunk_backward/pallas_call | solution.py:198
  226.8 1.3 copy-done.3
  228.1 0.8 copy-done.6
  228.9 11.3 %chunk_backward.5 = (bf16[512,512]{1,0:T(8,128)(2,1)S(1)}, f32[1024,512]{1,0:T(8,128)S(1)}) custom-call(s32[9]{0:T(128)S(1)} %concatenate.6.place_ref, bf16[4,512,512]{2,1,0:T(8,128)(2,1)} %pad_maximum_fusion.3.own_ref.refs_6_, bf16[4,512,512]{2,1,0:T(8,128)(2,1)} %collective-permute-done.25.other_ref.refs_10_, bf16[2048,4096]{1,0:T(8,128)(2,1)} %w_out_ref.7, ...), custom_call_target="tpu_custom_call" | custom-call | tf_op jit(solution)/shard_map/chunk_backward/pallas_call | solution.py:198
  240.2 1.3 copy-done.4
  241.5 0.8 copy-done.7
  242.4 11.5 %chunk_backward.6 = (bf16[512,512]{1,0:T(8,128)(2,1)S(1)}, f32[1024,512]{1,0:T(8,128)S(1)}) custom-call(s32[9]{0:T(128)S(1)} %concatenate.6.place_ref, bf16[4,512,512]{2,1,0:T(8,128)(2,1)} %collective-permute-done.19.own_ref.refs_5_, bf16[4,512,512]{2,1,0:T(8,128)(2,1)} %collective-permute-done.20.other_ref.refs_9_, bf16[2048,4096]{1,0:T(8,128)(2,1)} %w_out_ref.7, ...), custom_call_target="tpu_custom_call" | custom-call | tf_op jit(solution)/shard_map/chunk_backward/pallas_call | solution.py:198
  253.9 1.3 copy-done.2
  255.2 0.8 copy-done.8
  256.0 11.3 %chunk_backward.7 = (bf16[512,512]{1,0:T(8,128)(2,1)S(1)}, f32[1024,512]{1,0:T(8,128)S(1)}) custom-call(s32[9]{0:T(128)S(1)} %concatenate.6.place_ref, bf16[4,512,512]{2,1,0:T(8,128)(2,1)} %pad_maximum_fusion.1.own_ref.refs_7_, bf16[4,512,512]{2,1,0:T(8,128)(2,1)} %collective-permute-done.15.other_ref.refs_11_, bf16[2048,4096]{1,0:T(8,128)(2,1)} %w_out_ref.7, ...), custom_call_target="tpu_custom_call" | custom-call | tf_op jit(solution)/shard_map/chunk_backward/pallas_call | solution.py:198
  267.3 0.8 copy-done.9
  268.1 0.9 dynamic-slice_convert_fusion
  269.1 2.3 collective-permute-start.28
  271.4 2.1 collective-permute-start.29
  273.4 18.2 %grad_out.1 = f32[512,4096]{1,0:T(8,128)} custom-call(s32[8]{0:T(128)} %copy-done.10, bf16[512,512]{1,0:T(8,128)(2,1)} %copy-done.6, bf16[512,512]{1,0:T(8,128)(2,1)} %copy-done.8, bf16[512,512]{1,0:T(8,128)(2,1)} %copy-done.7, bf16[512,512]{1,0:T(8,128)(2,1)} %copy-done.9, bf16[4,512,512]{2,1,0:T(8,128)(2,1)} %copy-done.1, ...), custom_call_target="tpu_custom_call" | custom-call | tf_op jit(solution)/shard_map/grad_out/pallas_call | solution.py:262
  291.9 0.6 collective-permute-start.8
  292.5 1.2 fusion.1
  293.7 1.8 collective-permute-start.10
  295.5 1.0 convert_dynamic-update-slice_fusion.2
  296.5 1.0 convert_dynamic-update-slice_fusion.1
  297.5 1.0 convert_dynamic-update-slice_fusion
  298.6 8.2 %collective-permute-done.8 = bf16[512,512]{1,0:T(8,128)(2,1)S(1)} collective-permute-done((bf16[512,512]{1,0:T(8,128)(2,1)S(1)}, bf16[512,512]{1,0:T(8,128)(2,1)S(1)}, u32[]{:S(2)}, u32[]{:S(2)}) %collective-permute-start.8) | collective-permute-done | bytes 524320 | tf_op jit(solution)/shard_map/ppermute | solution.py:297
  306.7 1.0 fusion.4
  (72 shorter events, 3.6 us)
Async XLA Ops:
  0.6 6.3 %copy-start.5 = (bf16[1,4096,128]{2,1,0:T(8,128)(2,1)S(1)}, bf16[1,4096,128]{2,1,0:T(8,128)(2,1)}, u32[]{:S(2)}) copy-start(bf16[1,4096,128]{2,1,0:T(8,128)(2,1)} %param.10) | copy-start | bytes 3145732
  1.8 45.5 %copy-start.13 = (bf16[512,512]{1,0:T(8,128)(2,1)S(1)}, bf16[512,512]{1,0:T(8,128)(2,1)}, u32[]{:S(2)}) copy-start(bf16[512,512]{1,0:T(8,128)(2,1)} %param.13) | copy-start | bytes 1572868
  16.0 9.5 %collective-permute-start.2 = (bf16[512,128]{1,0:T(8,128)(2,1)S(1)}, bf16[512,128]{1,0:T(8,128)(2,1)S(1)}, u32[]{:S(2)}, u32[]{:S(2)}) collective-permute-start(bf16[512,128]{1,0:T(8,128)(2,1)S(1)} %pool.1), channel_id=1, source_target_pairs={{0,3},{1,2},{2,1},{3,0},{4,7},{5,6},{6,5},{7,4},{8,11},{9,10},{10,... | collective-permute-start | bytes 393224 | tf_op jit(solution)/shard_map/ppermute | solution.py:305
  21.2 11.1 %collective-permute-start.1 = (bf16[512,128]{1,0:T(8,128)(2,1)S(1)}, bf16[512,128]{1,0:T(8,128)(2,1)S(1)}, u32[]{:S(2)}, u32[]{:S(2)}) collective-permute-start(bf16[512,128]{1,0:T(8,128)(2,1)S(1)} %pool.1), channel_id=1, source_target_pairs={{0,2},{1,3},{2,0},{3,1},{4,6},{5,7},{6,4},{7,5},{8,10},{9,11},{10,... | collective-permute-start | bytes 393224 | tf_op jit(solution)/shard_map/ppermute | solution.py:305
  21.2 11.1 %collective-permute-start = (bf16[512,128]{1,0:T(8,128)(2,1)S(1)}, bf16[512,128]{1,0:T(8,128)(2,1)S(1)}, u32[]{:S(2)}, u32[]{:S(2)}) collective-permute-start(bf16[512,128]{1,0:T(8,128)(2,1)S(1)} %pool.1), channel_id=1, source_target_pairs={{0,1},{1,0},{2,3},{3,2},{4,5},{5,4},{6,7},{7,6},{8,9},{9,8},{10,11... | collective-permute-start | bytes 393224 | tf_op jit(solution)/shard_map/ppermute | solution.py:305
  32.3 14.8 %collective-permute-start.3 = (bf16[4,512,128]{2,1,0:T(8,128)(2,1)S(1)}, bf16[4,512,128]{2,1,0:T(8,128)(2,1)S(1)}, u32[]{:S(2)}, u32[]{:S(2)}) collective-permute-start(bf16[4,512,128]{2,1,0:T(8,128)(2,1)S(1)} %get-tuple-element.27), channel_id=1, source_target_pairs={{0,16},{4,20},{8,12},{12,8},{16,0},{20,4},{24,28},{28,24},{1,17},{... | collective-permute-start | bytes 1572872 | tf_op jit(solution)/shard_map/ppermute | solution.py:293
  33.9 14.7 %collective-permute-start.4 = (bf16[4,512,128]{2,1,0:T(8,128)(2,1)S(1)}, bf16[4,512,128]{2,1,0:T(8,128)(2,1)S(1)}, u32[]{:S(2)}, u32[]{:S(2)}) collective-permute-start(bf16[4,512,128]{2,1,0:T(8,128)(2,1)S(1)} %get-tuple-element.27), channel_id=1, source_target_pairs={{0,4},{4,0},{8,24},{12,28},{16,20},{20,16},{24,8},{28,12},{1,5},{5... | collective-permute-start | bytes 1572872 | tf_op jit(solution)/shard_map/ppermute | solution.py:297
  47.1 11.0 %collective-permute-start.5 = (bf16[4,512,128]{2,1,0:T(8,128)(2,1)S(1)}, bf16[4,512,128]{2,1,0:T(8,128)(2,1)S(1)}, u32[]{:S(2)}, u32[]{:S(2)}) collective-permute-start(bf16[4,512,128]{2,1,0:T(8,128)(2,1)S(1)} %collective-permute-done.3), channel_id=1, source_target_pairs={{0,4},{4,0},{8,24},{12,28},{16,20},{20,16},{24,8},{28,12},{1,5},{5... | collective-permute-start | bytes 1572872 | tf_op jit(solution)/shard_map/ppermute | solution.py:297
  47.3 14.0 %collective-permute-start.16 = (bf16[512,512]{1,0:T(8,128)(2,1)S(1)}, bf16[512,512]{1,0:T(8,128)(2,1)S(1)}, u32[]{:S(2)}, u32[]{:S(2)}) collective-permute-start(bf16[512,512]{1,0:T(8,128)(2,1)S(1)} %copy-done.13), channel_id=1, source_target_pairs={{0,16},{4,20},{8,12},{12,8},{16,0},{20,4},{24,28},{28,24},{1,17},{... | collective-permute-start | bytes 1572872 | tf_op jit(solution)/shard_map/ppermute | solution.py:293
  59.7 85.5 %collective-permute-start.6 = (bf16[4,4,512,128]{3,2,1,0:T(8,128)(2,1)}, bf16[4,4,512,128]{3,2,1,0:T(8,128)(2,1)}, u32[]{:S(2)}, u32[]{:S(2)}) collective-permute-start(bf16[4,4,512,128]{3,2,1,0:T(8,128)(2,1)} %pad_maximum_fusion.own_ref), channel_id=1, source_target_pairs={{0,8},{8,0},{16,24},{24,16},{1,9},{9,1},{17,25},{25,17},{2,10},{10... | collective-permute-start | bytes 6291464 | tf_op jit(solution)/shard_map/ppermute | solution.py:301
  59.7 9.2 %collective-permute-start.17 = (bf16[512,512]{1,0:T(8,128)(2,1)S(1)}, bf16[512,512]{1,0:T(8,128)(2,1)S(1)}, u32[]{:S(2)}, u32[]{:S(2)}) collective-permute-start(bf16[512,512]{1,0:T(8,128)(2,1)S(1)} %copy-done.13), channel_id=1, source_target_pairs={{0,4},{4,0},{8,24},{12,28},{16,20},{20,16},{24,8},{28,12},{1,5},{5... | collective-permute-start | bytes 1572872 | tf_op jit(solution)/shard_map/ppermute | solution.py:297
  61.2 13.3 %collective-permute-start.18 = (bf16[512,512]{1,0:T(8,128)(2,1)S(1)}, bf16[512,512]{1,0:T(8,128)(2,1)S(1)}, u32[]{:S(2)}, u32[]{:S(2)}) collective-permute-start(bf16[512,512]{1,0:T(8,128)(2,1)S(1)} %collective-permute-done.16), channel_id=1, source_target_pairs={{0,4},{4,0},{8,24},{12,28},{16,20},{20,16},{24,8},{28,12},{1,5},{5... | collective-permute-start | bytes 1572872 | tf_op jit(solution)/shard_map/ppermute | solution.py:297
  74.8 141.0 %copy-start.1 = (bf16[4,512,512]{2,1,0:T(8,128)(2,1)}, bf16[4,512,512]{2,1,0:T(8,128)(2,1)S(1)}, u32[]{:S(2)}) copy-start(bf16[4,512,512]{2,1,0:T(8,128)(2,1)S(1)} %pad_maximum_fusion.2.own_ref.refs_4_) | copy-start | bytes 6291460
  74.8 116.3 %collective-permute-start.19 = (bf16[4,512,512]{2,1,0:T(8,128)(2,1)S(1)}, bf16[4,512,512]{2,1,0:T(8,128)(2,1)}, u32[]{:S(2)}, u32[]{:S(2)}) collective-permute-start(bf16[4,512,512]{2,1,0:T(8,128)(2,1)S(1)} %pad_maximum_fusion.2.own_ref.refs_4_), channel_id=1, source_target_pairs={{0,1},{1,0},{2,3},{3,2},{4,5},{5,4},{6,7},{7,6},{8,9},{9,8},{10,11... | collective-permute-start | bytes 6291464 | tf_op jit(solution)/shard_map/ppermute | solution.py:305
  74.8 57.3 %collective-permute-start.21 = (bf16[512,512]{1,0:T(8,128)(2,1)S(1)}, bf16[512,512]{1,0:T(8,128)(2,1)}, u32[]{:S(2)}, u32[]{:S(2)}) collective-permute-start(bf16[512,512]{1,0:T(8,128)(2,1)S(1)} %copy-done.13), channel_id=1, source_target_pairs={{0,2},{1,3},{2,0},{3,1},{4,6},{5,7},{6,4},{7,5},{8,10},{9,11},{10,... | collective-permute-start | bytes 1572872 | tf_op jit(solution)/shard_map/ppermute | solution.py:305
  77.5 67.4 %collective-permute-start.11 = (bf16[512,512]{1,0:T(8,128)(2,1)S(1)}, bf16[512,512]{1,0:T(8,128)(2,1)S(1)}, u32[]{:S(2)}, u32[]{:S(2)}) collective-permute-start(bf16[512,512]{1,0:T(8,128)(2,1)S(1)} %copy-done.13), channel_id=1, source_target_pairs={{0,3},{1,2},{2,1},{3,0},{4,7},{5,6},{6,5},{7,4},{8,11},{9,10},{10,... | collective-permute-start | bytes 1572872 | tf_op jit(solution)/shard_map/ppermute | solution.py:305
  79.3 82.3 %copy-start.10 = (s32[8]{0:T(128)}, s32[8]{0:T(128)S(1)}, u32[]{:S(2)}) copy-start(s32[8]{0:T(128)S(1)} %stack.122.place_ref) | copy-start | bytes 100
  132.1 44.1 %collective-permute-start.22 = (bf16[512,512]{1,0:T(8,128)(2,1)}, bf16[512,512]{1,0:T(8,128)(2,1)S(1)}, u32[]{:S(2)}, u32[]{:S(2)}) collective-permute-start(bf16[512,512]{1,0:T(8,128)(2,1)} %collective-permute-done.21), channel_id=1, source_target_pairs={{0,16},{4,20},{8,12},{12,8},{16,0},{20,4},{24,28},{28,24},{1,17},{... | collective-permute-start | bytes 1572872 | tf_op jit(solution)/shard_map/ppermute | solution.py:293
  132.5 45.8 %collective-permute-start.23 = (bf16[512,512]{1,0:T(8,128)(2,1)}, bf16[512,512]{1,0:T(8,128)(2,1)S(1)}, u32[]{:S(2)}, u32[]{:S(2)}) collective-permute-start(bf16[512,512]{1,0:T(8,128)(2,1)} %collective-permute-done.21), channel_id=1, source_target_pairs={{0,4},{4,0},{8,24},{12,28},{16,20},{20,16},{24,8},{28,12},{1,5},{5... | collective-permute-start | bytes 1572872 | tf_op jit(solution)/shard_map/ppermute | solution.py:297
  144.9 32.9 %collective-permute-start.12 = (bf16[512,512]{1,0:T(8,128)(2,1)S(1)}, bf16[512,512]{1,0:T(8,128)(2,1)S(1)}, u32[]{:S(2)}, u32[]{:S(2)}) collective-permute-start(bf16[512,512]{1,0:T(8,128)(2,1)S(1)} %collective-permute-done.11), channel_id=1, source_target_pairs={{0,16},{4,20},{8,12},{12,8},{16,0},{20,4},{24,28},{28,24},{1,17},{... | collective-permute-start | bytes 1572872 | tf_op jit(solution)/shard_map/ppermute | solution.py:293
  161.6 2.0 copy-start
  176.1 31.3 %collective-permute-start.7 = (bf16[4,512,512]{2,1,0:T(8,128)(2,1)S(1)}, bf16[4,512,512]{2,1,0:T(8,128)(2,1)S(1)}, u32[]{:S(2)}, u32[]{:S(2)}) collective-permute-start(bf16[4,512,512]{2,1,0:T(8,128)(2,1)S(1)} %mixed.3), channel_id=1, source_target_pairs={{0,8},{8,0},{16,24},{24,16},{1,9},{9,1},{17,25},{25,17},{2,10},{10... | collective-permute-start | bytes 6291464 | tf_op jit(solution)/shard_map/ppermute | solution.py:301
  176.2 9.2 %collective-permute-start.24 = (bf16[512,512]{1,0:T(8,128)(2,1)S(1)}, bf16[512,512]{1,0:T(8,128)(2,1)S(1)}, u32[]{:S(2)}, u32[]{:S(2)}) collective-permute-start(bf16[512,512]{1,0:T(8,128)(2,1)S(1)} %collective-permute-done.22), channel_id=1, source_target_pairs={{0,4},{4,0},{8,24},{12,28},{16,20},{20,16},{24,8},{28,12},{1,5},{5... | collective-permute-start | bytes 1572872 | tf_op jit(solution)/shard_map/ppermute | solution.py:297
  177.8 13.3 %collective-permute-start.13 = (bf16[512,512]{1,0:T(8,128)(2,1)S(1)}, bf16[512,512]{1,0:T(8,128)(2,1)S(1)}, u32[]{:S(2)}, u32[]{:S(2)}) collective-permute-start(bf16[512,512]{1,0:T(8,128)(2,1)S(1)} %collective-permute-done.11), channel_id=1, source_target_pairs={{0,4},{4,0},{8,24},{12,28},{16,20},{20,16},{24,8},{28,12},{1,5},{5... | collective-permute-start | bytes 1572872 | tf_op jit(solution)/shard_map/ppermute | solution.py:297
  178.3 18.4 %collective-permute-start.14 = (bf16[512,512]{1,0:T(8,128)(2,1)S(1)}, bf16[512,512]{1,0:T(8,128)(2,1)S(1)}, u32[]{:S(2)}, u32[]{:S(2)}) collective-permute-start(bf16[512,512]{1,0:T(8,128)(2,1)S(1)} %collective-permute-done.12), channel_id=1, source_target_pairs={{0,4},{4,0},{8,24},{12,28},{16,20},{20,16},{24,8},{28,12},{1,5},{5... | collective-permute-start | bytes 1572872 | tf_op jit(solution)/shard_map/ppermute | solution.py:297
  185.5 28.8 %collective-permute-start.26 = (bf16[4,512,512]{2,1,0:T(8,128)(2,1)S(1)}, bf16[4,512,512]{2,1,0:T(8,128)(2,1)}, u32[]{:S(2)}, u32[]{:S(2)}) collective-permute-start(bf16[4,512,512]{2,1,0:T(8,128)(2,1)S(1)} %pad_maximum_fusion.2.own_ref.refs_4_), channel_id=1, source_target_pairs={{0,8},{8,0},{16,24},{24,16},{1,9},{9,1},{17,25},{25,17},{2,10},{10... | collective-permute-start | bytes 6291464 | tf_op jit(solution)/shard_map/ppermute | solution.py:301
  191.1 37.8 %collective-permute-start.25 = (bf16[4,512,512]{2,1,0:T(8,128)(2,1)}, bf16[4,512,512]{2,1,0:T(8,128)(2,1)}, u32[]{:S(2)}, u32[]{:S(2)}) collective-permute-start(bf16[4,512,512]{2,1,0:T(8,128)(2,1)} %pad_maximum_fusion.3.own_ref.refs_6_), channel_id=1, source_target_pairs={{0,8},{8,0},{16,24},{24,16},{1,9},{9,1},{17,25},{25,17},{2,10},{10... | collective-permute-start | bytes 6291464 | tf_op jit(solution)/shard_map/ppermute | solution.py:301
  191.1 51.3 %collective-permute-start.20 = (bf16[4,512,512]{2,1,0:T(8,128)(2,1)}, bf16[4,512,512]{2,1,0:T(8,128)(2,1)}, u32[]{:S(2)}, u32[]{:S(2)}) collective-permute-start(bf16[4,512,512]{2,1,0:T(8,128)(2,1)} %collective-permute-done.19.own_ref.refs_5_), channel_id=1, source_target_pairs={{0,8},{8,0},{16,24},{24,16},{1,9},{9,1},{17,25},{25,17},{2,10},{10... | collective-permute-start | bytes 6291464 | tf_op jit(solution)/shard_map/ppermute | solution.py:301
  198.3 57.7 %collective-permute-start.15 = (bf16[4,512,512]{2,1,0:T(8,128)(2,1)}, bf16[4,512,512]{2,1,0:T(8,128)(2,1)}, u32[]{:S(2)}, u32[]{:S(2)}) collective-permute-start(bf16[4,512,512]{2,1,0:T(8,128)(2,1)} %pad_maximum_fusion.1.own_ref.refs_7_), channel_id=1, source_target_pairs={{0,8},{8,0},{16,24},{24,16},{1,9},{9,1},{17,25},{25,17},{2,10},{10... | collective-permute-start | bytes 6291464 | tf_op jit(solution)/shard_map/ppermute | solution.py:301
  212.5 79.9 %collective-permute-start.9 = (bf16[512,512]{1,0:T(8,128)(2,1)S(1)}, bf16[512,512]{1,0:T(8,128)(2,1)}, u32[]{:S(2)}, u32[]{:S(2)}) collective-permute-start(bf16[512,512]{1,0:T(8,128)(2,1)S(1)} %get-tuple-element.25), channel_id=1, source_target_pairs={{0,4},{4,0},{8,24},{12,28},{16,20},{20,16},{24,8},{28,12},{1,5},{5... | collective-permute-start | bytes 1572872 | tf_op jit(solution)/shard_map/ppermute | solution.py:297
  226.7 1.3 copy-start.3
  228.1 0.8 copy-start.6
  240.2 1.3 copy-start.4
  241.5 0.8 copy-start.7
  253.9 1.3 copy-start.2
  255.2 0.8 copy-start.8
  267.3 0.8 copy-start.9
  269.1 26.4 %collective-permute-start.27 = (bf16[256,512]{1,0:T(8,128)(2,1)}, bf16[256,512]{1,0:T(8,128)(2,1)}, u32[]{:S(2)}, u32[]{:S(2)}) collective-permute-start(bf16[256,512]{1,0:T(8,128)(2,1)} %get-tuple-element.23), channel_id=1, source_target_pairs={{0,1},{1,0},{2,3},{3,2},{4,5},{5,4},{6,7},{7,6},{8,9},{9,8},{10,11... | collective-permute-start | bytes 786440 | tf_op jit(solution)/shard_map/ppermute | solution.py:305
  269.1 27.5 %collective-permute-start.28 = (bf16[256,512]{1,0:T(8,128)(2,1)}, bf16[256,512]{1,0:T(8,128)(2,1)}, u32[]{:S(2)}, u32[]{:S(2)}) collective-permute-start(bf16[256,512]{1,0:T(8,128)(2,1)} %get-tuple-element.22), channel_id=1, source_target_pairs={{0,2},{1,3},{2,0},{3,1},{4,6},{5,7},{6,4},{7,5},{8,10},{9,11},{10,... | collective-permute-start | bytes 786440 | tf_op jit(solution)/shard_map/ppermute | solution.py:305
  271.4 26.2 %collective-permute-start.29 = (bf16[256,512]{1,0:T(8,128)(2,1)S(1)}, bf16[256,512]{1,0:T(8,128)(2,1)}, u32[]{:S(2)}, u32[]{:S(2)}) collective-permute-start(bf16[256,512]{1,0:T(8,128)(2,1)S(1)} %get-tuple-element.21), channel_id=1, source_target_pairs={{0,3},{1,2},{2,1},{3,0},{4,7},{5,6},{6,5},{7,4},{8,11},{9,10},{10,... | collective-permute-start | bytes 786440 | tf_op jit(solution)/shard_map/ppermute | solution.py:305
  273.4 19.0 %copy-start.11 = (f32[4,512,512]{2,1,0:T(8,128)S(1)}, f32[4,512,512]{2,1,0:T(8,128)}, u32[]{:S(2)}) copy-start(f32[4,512,512]{2,1,0:T(8,128)} %get-tuple-element.20) | copy-start | bytes 12582916
  291.9 14.9 %collective-permute-start.8 = (bf16[512,512]{1,0:T(8,128)(2,1)S(1)}, bf16[512,512]{1,0:T(8,128)(2,1)S(1)}, u32[]{:S(2)}, u32[]{:S(2)}) collective-permute-start(bf16[512,512]{1,0:T(8,128)(2,1)S(1)} %get-tuple-element.24), channel_id=1, source_target_pairs={{0,4},{4,0},{8,24},{12,28},{16,20},{20,16},{24,8},{28,12},{1,5},{5... | collective-permute-start | bytes 1572872 | tf_op jit(solution)/shard_map/ppermute | solution.py:297
  293.7 13.1 %collective-permute-start.10 = (bf16[512,512]{1,0:T(8,128)(2,1)S(1)}, bf16[512,512]{1,0:T(8,128)(2,1)S(1)}, u32[]{:S(2)}, u32[]{:S(2)}) collective-permute-start(bf16[512,512]{1,0:T(8,128)(2,1)S(1)} %fusion.1), channel_id=1, source_target_pairs={{0,16},{4,20},{8,12},{12,8},{16,0},{20,4},{24,28},{28,24},{1,17},{... | collective-permute-start | bytes 1572872 | tf_op jit(solution)/shard_map/ppermute | solution.py:293
  298.6 9.2 %copy-start.12 = (f32[256,2048]{1,0:T(8,128)}, f32[256,2048]{1,0:T(8,128)S(1)}, u32[]{:S(2)}) copy-start(f32[256,2048]{1,0:T(8,128)S(1)} %convert_dynamic-update-slice_fusion) | copy-start | bytes 6291460

commit v2 on v0

v2 whole, which is shorter than its diff:
```python
import functools

import jax
import jax.numpy as jnp
from jax import lax
from jax.experimental import pallas as pl
from jax.experimental.pallas import tpu as pltpu
from jax.sharding import PartitionSpec as P

F32 = jnp.float32
BF16 = jnp.bfloat16
PLANE = ("table", "tensor")
ROWS_TN = (((0,), (0,)), ((), ()))
COLS_NT = (((1,), (1,)), ((), ()))


def silu_slope(preact):
    sigmoid_part = jax.nn.sigmoid(preact)
    return sigmoid_part * (1.0 + preact * (1.0 - sigmoid_part))


def cost(flops, bytes_accessed, transcendentals):
    return pl.CostEstimate(flops=flops, bytes_accessed=bytes_accessed, transcendentals=transcendentals)


def params(mib):
    return pltpu.CompilerParams(vmem_limit_bytes=mib * 1024 * 1024)


def pool_kernel(key_ref, len_ref, width_ref, table_ref, out_ref, counts_ref, *, group, low):
    samples, columns = out_ref.shape
    slots = key_ref.shape[1]
    bag = slots // group
    high = table_ref.shape[0] // low
    rows = lax.broadcasted_iota(jnp.int32, (high * group, slots), 0)
    low_rows = lax.broadcasted_iota(jnp.int32, (low, slots), 0)
    lane = lax.broadcasted_iota(jnp.int32, (1, slots), 1)
    member, slot = lane // bag, lax.rem(lane, bag)
    group_rows = lax.broadcasted_iota(jnp.int32, (group, slots), 0)

    def one_group(g, carry):
        first = pl.multiple_of(g * group, group)
        lengths = jnp.where(group_rows == member, len_ref[pl.ds(first, group), :], 0)
        in_bag = slot < jnp.sum(lengths, axis=0, keepdims=True)
        key = key_ref[pl.ds(g, 1), :]
        hit_high = (rows == jnp.where(in_bag, (key // low) * group + member, -1)).astype(BF16)
        hit_low = (low_rows == lax.rem(key, low)).astype(BF16)
        counts = lax.dot_general(hit_high, hit_low, COLS_NT, preferred_element_type=F32).astype(BF16)
        for h in range(high):
            counts_ref[h, pl.ds(first, group), :] = counts[h * group : (h + 1) * group, :]
        return carry

    lax.fori_loop(0, samples // group, one_group, 0, unroll=4)
    total = jnp.zeros(out_ref.shape, F32)
    for h in range(high):
        total += jnp.dot(
            counts_ref[h], table_ref[h * low : (h + 1) * low, :], preferred_element_type=F32
        )
    pooled = total / len_ref[...].astype(F32)
    position = lax.axis_index("tensor") * columns + lax.broadcasted_iota(jnp.int32, pooled.shape, 1)
    out_ref[...] = jnp.where(position < width_ref[lax.axis_index("table")], pooled, 0.0).astype(BF16)


def pool_local(lookup_ids, bag_lengths, feature_widths, embedding):
    samples, unused, bag = lookup_ids.shape
    vocab, columns = embedding.shape
    low, group = 256, 16
    high = vocab // low
    return pl.pallas_call(
        functools.partial(pool_kernel, group=group, low=low),
        out_shape=jax.ShapeDtypeStruct((samples, columns), BF16),
        in_specs=[
            pl.BlockSpec(memory_space=pltpu.VMEM),
            pl.BlockSpec(memory_space=pltpu.VMEM),
            pl.BlockSpec(memory_space=pltpu.SMEM),
            pl.BlockSpec(memory_space=pltpu.VMEM),
        ],
        out_specs=pl.BlockSpec(memory_space=pltpu.VMEM),
        scratch_shapes=[pltpu.VMEM((high, samples, low), BF16)],
        compiler_params=params(56),
        cost_estimate=cost(4 * samples * vocab * columns, 2 * vocab * columns, 0),
        name="pool",
    )(lookup_ids.reshape(samples // group, group * bag), bag_lengths, feature_widths, embedding)


def block_copies(place_ref, refs, first, width, buffer, sem, in_place):
    copies = []
    each = 8 // len(refs)
    for j in range(8):
        to = pl.multiple_of(place_ref[j] * width, width) if in_place else j * width
        source = refs[j // each].at[j % each, :, pl.ds(first, width)]
        copies.append(pltpu.make_async_copy(source, buffer.at[:, pl.ds(to, width)], sem.at[j]))
    return copies


def start_all(copies):
    for c in copies:
        c.start()


def wait_all(copies):
    for c in copies:
        c.wait()


def hidden_kernel(place_ref, blocks_ref, w_in_ref, hidden_ref, feat_ref, sem, *, step):
    copies = block_copies(place_ref, [blocks_ref], 0, blocks_ref.shape[2], feat_ref, sem, True)
    start_all(copies)
    wait_all(copies)
    for i in range(hidden_ref.shape[1] // step):
        here = slice(i * step, (i + 1) * step)
        preact = jnp.dot(feat_ref[...], w_in_ref[:, here], preferred_element_type=F32)
        hidden_ref[:, here] = jax.nn.silu(preact).astype(BF16)


def hidden_of(place, feat_blocks, w_in):
    samples = feat_blocks.shape[1]
    depth, units = w_in.shape
    in_vmem = pl.BlockSpec(memory_space=pltpu.VMEM)
    return pl.pallas_call(
        functools.partial(hidden_kernel, step=512),
        out_shape=jax.ShapeDtypeStruct((samples, units), BF16),
        in_specs=[pl.BlockSpec(memory_space=pltpu.SMEM), pl.BlockSpec(memory_space=pl.ANY), in_vmem],
        out_specs=in_vmem,
        scratch_shapes=[pltpu.VMEM((samples, depth), BF16), pltpu.SemaphoreType.DMA((8,))],
        compiler_params=params(56),
        cost_estimate=cost(2 * samples * units * depth, 2 * units * depth, samples * units),
        name="hidden",
    )(place, feat_blocks, w_in)


def mixed_kernel(place_ref, hidden_ref, w_ref, out_ref):
    out_ref[0] = jnp.dot(hidden_ref[...], w_ref[...], preferred_element_type=F32).astype(out_ref.dtype)


def mixed_blocks(place, hidden, w_out, wide, dtype):
    samples, units = hidden.shape
    slots = place.shape[0]
    return pl.pallas_call(
        mixed_kernel,
        out_shape=jax.ShapeDtypeStruct((slots, samples, wide), dtype),
        grid_spec=pltpu.PrefetchScalarGridSpec(
            num_scalar_prefetch=1,
            grid=(slots,),
            in_specs=[
                pl.BlockSpec((samples, units), lambda j, p: (0, 0)),
                pl.BlockSpec((units, wide), lambda j, p: (0, p[j])),
            ],
            out_specs=pl.BlockSpec((1, samples, wide), lambda j, p: (j, 0, 0)),
        ),
        compiler_params=params(56),
        cost_estimate=cost(2 * samples * units * slots * wide, 2 * units * slots * wide, 0),
        name="mixed",
    )(place, hidden, w_out)


def chunk_kernel(place_ref, *refs, wide, first, feats):
    cot_refs, feat_refs = refs[:4], refs[4 : 4 + feats]
    w_out_ref, w_in_ref, sum_ref, hidden_ref, grad_in_ref = refs[4 + feats : 9 + feats]
    cot_buf, w_out_buf, feat_buf, w_in_buf, sum_buf, cot_sem, w_sem, feat_sem, sem = refs[9 + feats :]
    units = hidden_ref.shape[0]
    row = pl.ds(pl.multiple_of(place_ref[8] * units, units), units)
    cot_copies = block_copies(place_ref, cot_refs, 0, wide, cot_buf, cot_sem, False)
    w_copies = []
    for j in range(8):
        column = pl.ds(pl.multiple_of(place_ref[j] * wide, wide), wide)
        w_copies.append(
            pltpu.make_async_copy(w_out_ref.at[row, column], w_out_buf.at[:, pl.ds(j * wide, wide)], w_sem.at[j])
        )
    feat_copies = block_copies(place_ref, feat_refs, first, feat_buf.shape[1] // 8, feat_buf, feat_sem, True)
    w_in_copy = pltpu.make_async_copy(w_in_ref.at[:, row], w_in_buf, sem.at[0])
    sum_copy = pltpu.make_async_copy(sum_ref, sum_buf, sem.at[1])
    start_all(feat_copies)
    w_in_copy.start()
    start_all(cot_copies[:4] + w_copies[:4])
    start_all(cot_copies[4:] + w_copies[4:])
    sum_copy.start()

    wait_all(feat_copies)
    w_in_copy.wait()
    preact = jnp.dot(feat_buf[...], w_in_buf[...], preferred_element_type=F32)
    hidden_ref[...] = jax.nn.silu(preact).astype(BF16).T
    slope = silu_slope(preact)
    middle = 4 * wide
    wait_all(cot_copies[:4] + w_copies[:4])
    grad_hidden = lax.dot_general(
        cot_buf[:, :middle], w_out_buf[:, :middle], COLS_NT, preferred_element_type=F32
    )
    wait_all(cot_copies[4:] + w_copies[4:])
    grad_hidden += lax.dot_general(
        cot_buf[:, middle:], w_out_buf[:, middle:], COLS_NT, preferred_element_type=F32
    )
    grad_preact = (grad_hidden * slope).astype(BF16)
    sum_copy.wait()
    grad_in_ref[...] = sum_buf[...] + lax.dot_general(
        feat_buf[...], grad_preact, ROWS_TN, preferred_element_type=F32
    )


def chunk_backward(place, cot_blocks, feat_blocks, first, w_out, w_in, running, wide):
    samples = cot_blocks[0].shape[1]
    depth, units = running.shape
    any_space = pl.BlockSpec(memory_space=pl.ANY)
    in_vmem = pl.BlockSpec(memory_space=pltpu.VMEM)
    return pl.pallas_call(
        functools.partial(chunk_kernel, wide=wide, first=first, feats=len(feat_blocks)),
        out_shape=(
            jax.ShapeDtypeStruct((units, samples), BF16),
            jax.ShapeDtypeStruct((depth, units), F32),
        ),
        in_specs=[pl.BlockSpec(memory_space=pltpu.SMEM)] + [any_space] * (7 + len(feat_blocks)),
        out_specs=(in_vmem, in_vmem),
        scratch_shapes=[
            pltpu.VMEM((samples, 8 * wide), BF16),
            pltpu.VMEM((units, 8 * wide), BF16),
            pltpu.VMEM((samples, depth), BF16),
            pltpu.VMEM((depth, units), BF16),
            pltpu.VMEM((depth, units), F32),
            pltpu.SemaphoreType.DMA((8,)),
            pltpu.SemaphoreType.DMA((8,)),
            pltpu.SemaphoreType.DMA((8,)),
            pltpu.SemaphoreType.DMA((2,)),
        ],
        compiler_params=params(56),
        cost_estimate=cost(
            2 * samples * units * (8 * wide + 2 * depth),
            2 * (samples + units) * (8 * wide + depth) + 8 * depth * units,
            2 * samples * units,
        ),
        name="chunk_backward",
    )(place, *cot_blocks, *feat_blocks, w_out, w_in, running)


def grad_out_kernel(place_ref, *refs, chunks):
    hidden, blocks = refs[:chunks], refs[chunks : 5 * chunks]
    out_ref, hidden_buf, cot_buf, hidden_sem, cot_sem = refs[5 * chunks :]
    samples, wide = hidden[0].shape[1], out_ref.shape[1]
    j = pl.program_id(0)
    rows = [slice(k * samples, (k + 1) * samples) for k in range(chunks)]

    def fetch(slot, action):
        buffer = lax.rem(slot, 2)
        for i in range(4):

            @pl.when(slot // 2 == i)
            def _():
                for k in range(chunks):
                    source = blocks[4 * k + i].at[lax.rem(slot, 2), :, pl.ds(0, wide)]
                    action(pltpu.make_async_copy(source, cot_buf.at[buffer, rows[k]], cot_sem.at[buffer, k]))

    hidden_copies = [
        pltpu.make_async_copy(hidden[k], hidden_buf.at[:, rows[k]], hidden_sem.at[k]) for k in range(chunks)
    ]

    @pl.when(j == 0)
    def _():
        start_all(hidden_copies)
        fetch(j, lambda c: c.start())

    @pl.when(j + 1 < pl.num_programs(0))
    def _():
        fetch(j + 1, lambda c: c.start())

    @pl.when(j == 0)
    def _():
        wait_all(hidden_copies)

    fetch(j, lambda c: c.wait())
    out_ref[...] = jnp.dot(hidden_buf[...], cot_buf[lax.rem(j, 2)], preferred_element_type=F32)


def grad_out_of(place, hidden, cot_blocks, wide):
    chunks = len(hidden)
    units, samples = hidden[0].shape
    flat = [array for blocks in cot_blocks for array in blocks]
    return pl.pallas_call(
        functools.partial(grad_out_kernel, chunks=chunks),
        out_shape=jax.ShapeDtypeStruct((units, 8 * wide), F32),
        grid_spec=pltpu.PrefetchScalarGridSpec(
            num_scalar_prefetch=1,
            grid=(8,),
            in_specs=[pl.BlockSpec(memory_space=pl.ANY)] * (5 * chunks),
            out_specs=pl.BlockSpec((units, wide), lambda j, p: (0, p[j])),
            scratch_shapes=[
                pltpu.VMEM((units, chunks * samples), BF16),
                pltpu.VMEM((2, chunks * samples, wide), BF16),
                pltpu.SemaphoreType.DMA((chunks,)),
                pltpu.SemaphoreType.DMA((2, chunks)),
            ],
        ),
        compiler_params=params(56),
        cost_estimate=cost(
            2 * units * chunks * samples * 8 * wide,
            2 * chunks * samples * (8 * wide + units) + 4 * units * 8 * wide,
            0,
        ),
        name="grad_out",
    )(place, *hidden, *flat)


def plane_perms():
    first, second = [], []
    for t in range(4):
        for y in range(2):
            along_x, along_y = (t ^ 2) * 2 + y, t * 2 + (y ^ 1)
            first.append((t * 2 + y, along_x if t % 2 == 0 else along_y))
            second.append((t * 2 + y, along_y if t % 2 == 0 else along_x))
    return first, second


PERM_A, PERM_B = plane_perms()


def move_a(v):
    return lax.ppermute(v, PLANE, PERM_A)


def move_b(v):
    return lax.ppermute(v, PLANE, PERM_B)


def swap(v):
    return lax.ppermute(v, "table", [(t, t ^ 1) for t in range(4)])


def move_z(v, k):
    return lax.ppermute(v, "dp", [(z, z ^ k) for z in range(4)])


def plane_blocks():
    t, y = lax.axis_index("table"), lax.axis_index("tensor")
    x, core = t // 2, t % 2
    blocks = []
    for dc in range(2):
        c = core ^ dc
        a_x, a_y = jnp.where(c == 0, 1, 0), jnp.where(c == 0, 0, 1)
        for dx, dy in ((0, 0), (a_x, a_y), (a_y, a_x), (1, 1)):
            blocks.append(((x ^ dx) * 2 + c) * 2 + (y ^ dy))
    return jnp.stack(blocks).astype(jnp.int32)


def after(v, *earlier):
    return lax.optimization_barrier((v,) + earlier)[0]


def spread_shards(lookup_ids, bag_lengths, feature_widths, tables, w_in, w_out, cotangent):
    z = lax.axis_index("dp")
    wide = cotangent.shape[1]
    units = w_in.shape[1] // 4
    blocks = plane_blocks()
    place = jnp.concatenate([blocks, z[None].astype(jnp.int32)])

    def backward(cot, feat, first, running):
        return chunk_backward(place, cot, feat, first, w_out, w_in, running, wide)

    s0 = cotangent
    a0 = move_a(s0)
    s1, s2 = move_z(s0, 1), move_z(s0, 2)
    pair0 = jnp.stack([s0, a0])
    both0 = move_b(pair0)
    pair0_ = swap(pair0)
    pooled = pool_local(lookup_ids, bag_lengths, after(feature_widths, pair0), tables[0])
    pa = move_a(pooled)
    pooled1, pooled2 = move_z(pooled, 1), move_z(pooled, 2)
    feat_pair = jnp.stack([pooled, after(pa, both0)])
    both0_ = swap(both0)
    feat_both = move_b(feat_pair)

    e1 = jnp.concatenate([after(s1, feat_pair), after(pooled1, feat_pair)], axis=1)
    a1 = move_a(e1)
    e2 = jnp.concatenate([after(s2, e1), after(pooled2, e1)], axis=1)
    e3 = move_z(e2, 1)
    feat0 = jnp.concatenate([feat_pair, feat_both, swap(feat_pair), swap(feat_both)])
    hidden_here = hidden_of(blocks, after(feat0, e2), w_in)

    pair1 = jnp.stack([e1, after(a1, hidden_here)])
    both1, a2 = move_b(pair1), move_a(after(e2, pair1))
    pair1_ = swap(pair1)
    away = mixed_blocks(blocks[4:], after(hidden_here, pair1, both0_), w_out, wide, BF16)
    got = swap(away)
    near = mixed_blocks(blocks[:4], after(hidden_here, away), w_out, wide, F32)

    pair2 = jnp.stack([e2, after(a2, near)])
    both1 = after(both1, pair2)
    both1_ = swap(both1)
    both2, a3 = move_b(pair2), move_a(after(e3, pair2))
    pair2_ = swap(pair2)
    running = jnp.zeros((w_in.shape[0], units), F32)
    cot0 = [pair0, both0, pair0_, both0_]
    hidden0, running = backward(cot0, [feat0], 0, after(running, pair2))
    cot1 = [pair1, both1, pair1_, both1_]
    hidden1, running = backward(cot1, cot1, wide, running)

    pair3 = jnp.stack([e3, after(a3, running)])
    both2 = after(both2, pair3)
    both2_ = swap(both2)
    both3 = move_b(pair3)
    pair3_ = swap(pair3)
    near = near + after(got, pair3).astype(F32)
    cot2 = [pair2, both2, pair2_, both2_]
    hidden2, running = backward(cot2, cot2, wide, after(running, near))

    both3 = after(both3, running)
    both3_ = swap(both3)
    moved = move_b(after(near, both3)[2:].astype(BF16))
    cot3 = [pair3, both3, pair3_, both3_]
    hidden3, running = backward(cot3, cot3, wide, running)
    moved = after(moved, running).astype(F32)
    last = move_a((near[1] + moved[1]).astype(BF16))

    rows = w_in.shape[0] // 4
    grad_in = jnp.zeros((rows, 4 * units), F32)
    for k in range(4):
        part = lax.dynamic_slice_in_dim(running, (z ^ k) * rows, rows, 0)
        part = part if k == 0 else move_z(part.astype(BF16), k).astype(F32)
        grad_in = lax.dynamic_update_slice_in_dim(grad_in, part, (z ^ k) * units, 1)
    grad_out = grad_out_of(blocks, [hidden0, hidden1, hidden2, hidden3], [cot0, cot1, cot2, cot3], wide)
    mixed_out = (near[0] + moved[0] + after(last, grad_out).astype(F32)).astype(BF16)
    return (mixed_out, grad_in, grad_out)


def summed_shards(lookup_ids, bag_lengths, feature_widths, tables, w_in, w_out, cotangent):
    pooled = pool_local(lookup_ids, bag_lengths, feature_widths, tables[0])
    features = lax.all_gather(pooled, PLANE, axis=1, tiled=True)
    preact = jnp.dot(features, w_in, preferred_element_type=F32)
    hidden = jax.nn.silu(preact).astype(BF16)
    partial_out = jnp.dot(hidden, w_out, preferred_element_type=F32)
    reduced = lax.psum_scatter(partial_out, PLANE, scatter_dimension=1, tiled=True)
    mixed_out = reduced.astype(BF16)
    whole_grad = lax.all_gather(cotangent, PLANE, axis=1, tiled=True)
    grad_hidden = lax.dot_general(whole_grad, w_out, COLS_NT, preferred_element_type=F32)
    grad_preact = (grad_hidden * silu_slope(preact)).astype(BF16)
    term_in = lax.dot_general(features, grad_preact, ROWS_TN, preferred_element_type=F32)
    term_out = lax.dot_general(hidden, whole_grad, ROWS_TN, preferred_element_type=F32)
    grad_in = lax.psum_scatter(term_in, "dp", scatter_dimension=0, tiled=True)
    grad_out = lax.psum_scatter(term_out, "dp", scatter_dimension=0, tiled=True)
    return (mixed_out, grad_in, grad_out)


def solution(mesh):
    sizes = (mesh.shape["table"], mesh.shape["tensor"], mesh.shape["dp"])
    return jax.shard_map(
        spread_shards if sizes == (4, 2, 4) else summed_shards,
        mesh=mesh,
        in_specs=(
            P("dp", "table", None),
            P("dp", "table"),
            P(),
            P("table", None, "tensor"),
            P(None, PLANE),
            P(PLANE, None),
            P("dp", PLANE),
        ),
        out_specs=(
            P("dp", PLANE),
            P("dp", PLANE),
            P(("table", "tensor", "dp"), None),
        ),
        check_vma=False,
    )
```

time: 927 us -> 175 us (0.19)
  waiting for transfers between devices: 781 us -> 24.4 us
  Pallas kernels: 0 us -> 91 us
  matrix products: 68.1 us -> 0 us
  starting transfers between devices: 0.38 us -> 26.9 us
  other arithmetic: 39.2 us -> 16.3 us
  loops' own time: 15.9 us -> 0 us
  between operations: 13.9 us -> 1.04 us
    reduce_scatter x3 -> x0, waiting for transfers between devices: 737 us -> none  [the longest x1 556 us: shards(): lax.psum_scatter(term_out, 'dp', scatter_dimension=0, tiled=True)]
    pallas_call x0 -> x9, Pallas kernels: none -> 91 us  [the longest x4 42 us: chunk_backward(): pl.pallas_call(functools.partial(chunk_kernel, wide=wide, first=first, fe...]
    dot_general x12 -> x0, matrix products: 68.1 us -> none  [the longest x1 19.5 us: shards(): lax.dot_general(hidden, whole_grad, contract_rows, preferred_element_type...]
    all_gather x2 -> x0, waiting for transfers between devices: 43.2 us -> none  [the longest x1 25.6 us: shards(): features = lax.all_gather(pooled, ('table', 'tensor'), axis=1, tiled=True)]
    reduce_sum x8 -> x0, other arithmetic: 29 us -> none  [add_block(): jnp.sum(masked[:, :, None] == local_ids[None, None, :], axis=1)]
    ppermute x0 -> x31, starting transfers between devices: none -> 26.9 us  [the longest x8 9.79 us: move_z(): return lax.ppermute(v, 'dp', [(z, z ^ k) for z in range(4)])]
    ppermute x0 -> x31, waiting for transfers between devices: none -> 24.4 us  [the longest x8 11 us: move_z(): return lax.ppermute(v, 'dp', [(z, z ^ k) for z in range(4)])]
    another operation x1 -> x0, loops' own time: 15.9 us -> none  [pool_local(): lax.scan(add_block, jnp.zeros((samples, half_width), jnp.float32), starts)]
  transfers between devices with their start and end apart: 5 -> 31, of which waited for: 5 -> 8; matrix products, arithmetic and copies ran while one was open for 7% -> 14% of each run, Pallas kernels for 0% -> 52%
where the time goes in v2:
time: 175 us; the launch traced here: 174 us
  Pallas kernels  91 us (52%)
  starting transfers between devices  26.9 us (15%)
  waiting for transfers between devices  24.4 us (14%)
  other arithmetic  16.3 us (9%)
  local copies, waits for them, and re-layouts  13.9 us (8%)
    pallas_call x4, Pallas kernels, chunk_backward(): pl.pallas_call(functools.partial(chunk_kernel, wide=wide, first=first, fe...  42 us
    pallas_call x2, Pallas kernels, mixed_blocks(): pl.pallas_call(mixed_kernel, out_shape=jax.ShapeDtypeStruct((slots, sampl...  19.2 us
    pallas_call x1, Pallas kernels, grad_out_of(): pl.pallas_call(functools.partial(grad_out_kernel, chunks=chunks), out_sha...  16.3 us
    ppermute x8, waiting for transfers between devices, move_z(): return lax.ppermute(v, 'dp', [(z, z ^ k) for z in range(4)])  11 us
    ppermute x8, starting transfers between devices, move_z(): return lax.ppermute(v, 'dp', [(z, z ^ k) for z in range(4)])  9.79 us
    ppermute x6, waiting for transfers between devices, move_a(): return lax.ppermute(v, PLANE, PERM_A)  9.67 us
    ppermute x6, starting transfers between devices, move_b(): return lax.ppermute(v, PLANE, PERM_B)  8.78 us
    pallas_call x1, Pallas kernels, hidden_of(): pl.pallas_call(functools.partial(hidden_kernel, step=512), out_shape=jax....  7.22 us
  transfers between devices with their start and end apart: 31, of which 8 were waited for; matrix products, arithmetic and copies ran while one was open for 14% of the time, Pallas kernels for 52%

profile of v2, /device:TPU:0, one launch (start us, length us, event | category | flops | bytes accessed | tf_op | source)
XLA Modules:
  0.0 173.6 jit_solution(16638945378340525067)
XLA Ops:
  0.7 3.0 %collective-permute-start = (bf16[512,512]{1,0:T(8,128)(2,1)}, bf16[512,512]{1,0:T(8,128)(2,1)S(1)}, u32[]{:S(2)}, u32[]{:S(2)}) collective-permute-start(bf16[512,512]{1,0:T(8,128)(2,1)} %param.13), channel_id=1, source_target_pairs={{0,16},{4,20},{8,12},{12,8},{16,0},{20,4},{24,28},{28,24},{1,17},{... | collective-permute-start | bytes 1572872 | tf_op jit(solution)/shard_map/ppermute | solution.py:315
  3.7 7.4 %collective-permute-done = bf16[512,512]{1,0:T(8,128)(2,1)S(1)} collective-permute-done((bf16[512,512]{1,0:T(8,128)(2,1)}, bf16[512,512]{1,0:T(8,128)(2,1)S(1)}, u32[]{:S(2)}, u32[]{:S(2)}) %collective-permute-start) | collective-permute-done | bytes 524320 | tf_op jit(solution)/shard_map/ppermute | solution.py:315
  11.0 2.2 %pad_maximum_fusion.3.refs_0_.refs_4_ = bf16[2,512,512]{2,1,0:T(8,128)(2,1)} fusion(bf16[1,512,512]{2,1,0:T(8,128)(2,1)S(1)} %bitcast.40, bf16[1,512,512]{2,1,0:T(8,128)(2,1)} %bitcast.39), kind=kLoop, calls=%fused_computation.11 | loop fusion | flops 524288 | bytes 2097152 | tf_op jit(solution)/shard_map/stack | solution.py:359
  13.2 2.0 %collective-permute-start.2 = (bf16[2,512,512]{2,1,0:T(8,128)(2,1)}, bf16[2,512,512]{2,1,0:T(8,128)(2,1)S(1)}, u32[]{:S(2)}, u32[]{:S(2)}) collective-permute-start(bf16[2,512,512]{2,1,0:T(8,128)(2,1)} %pad_maximum_fusion.3.refs_0_.refs_4_), channel_id=1, source_target_pairs={{0,4},{4,0},{8,24},{12,28},{16,20},{20,16},{24,8},{28,12},{1,5},{5... | collective-permute-start | bytes 3145736 | tf_op jit(solution)/shard_map/ppermute | solution.py:319
  15.2 1.6 collective-permute-start.7
  16.8 2.6 %collective-permute-start.6 = (bf16[512,512]{1,0:T(8,128)(2,1)S(1)}, bf16[512,512]{1,0:T(8,128)(2,1)S(1)}, u32[]{:S(2)}, u32[]{:S(2)}) collective-permute-start(bf16[512,512]{1,0:T(8,128)(2,1)S(1)} %copy-done.10), channel_id=1, source_target_pairs={{0,2},{1,3},{2,0},{3,1},{4,6},{5,7},{6,4},{7,5},{8,10},{9,11},{10,... | collective-permute-start | bytes 1572872 | tf_op jit(solution)/shard_map/ppermute | solution.py:327
  19.5 0.8 reshape.12.key_ref
  20.3 0.9 copy.13.len_ref
  21.2 0.7 stack.85.place_ref
  21.8 6.3 %pool.1 = bf16[512,128]{1,0:T(8,128)(2,1)} custom-call(s32[32,256]{1,0:T(8,128)} %reshape.12.key_ref, s32[512,1]{1,0:T(8,128)} %copy.13.len_ref, s32[4]{0:T(128)} %width_ref, bf16[4096,128]{1,0:T(8,128)(2,1)} %bitcast.41), custom_call_target="tpu_custom_call" | custom-call | flops 1073741824 | bytes 1048576 | tf_op jit(solution)/shard_map/pool/pallas_call | solution.py:69
  28.1 1.5 collective-permute-start.1
  29.6 0.4 collective-permute-start.8
  30.1 0.9 constant_dynamic-update-slice_fusion.4
  31.0 2.3 %collective-permute-done.1 = bf16[512,128]{1,0:T(8,128)(2,1)S(1)} collective-permute-done((bf16[512,128]{1,0:T(8,128)(2,1)}, bf16[512,128]{1,0:T(8,128)(2,1)S(1)}, u32[]{:S(2)}, u32[]{:S(2)}) %collective-permute-start.1) | collective-permute-done | bytes 131104 | tf_op jit(solution)/shard_map/ppermute | solution.py:315
  33.3 0.3 collective-permute-start.9
  33.6 1.0 pad_maximum_fusion.4
  34.7 0.6 collective-permute-start.3
  35.3 6.3 %collective-permute-done.7 = bf16[512,512]{1,0:T(8,128)(2,1)S(1)} collective-permute-done((bf16[512,512]{1,0:T(8,128)(2,1)S(1)}, bf16[512,512]{1,0:T(8,128)(2,1)S(1)}, u32[]{:S(2)}, u32[]{:S(2)}) %collective-permute-start.7) | collective-permute-done | bytes 524320 | tf_op jit(solution)/shard_map/ppermute | solution.py:327
  41.7 1.4 collective-permute-done.8
  43.1 0.4 collective-permute-start.10
  43.5 3.3 %collective-permute-done.9 = bf16[512,128]{1,0:T(8,128)(2,1)S(1)} collective-permute-done((bf16[512,128]{1,0:T(8,128)(2,1)}, bf16[512,128]{1,0:T(8,128)(2,1)S(1)}, u32[]{:S(2)}, u32[]{:S(2)}) %collective-permute-start.9) | collective-permute-done | bytes 131104 | tf_op jit(solution)/shard_map/ppermute | solution.py:327
  46.9 0.5 collective-permute-start.11
  47.6 0.8 collective-permute-done.5
  48.4 1.0 copy-done.7
  49.4 7.2 %hidden.1.hidden_ref = bf16[512,2048]{1,0:T(8,128)(2,1)} custom-call(s32[8]{0:T(128)} %stack.85.place_ref, bf16[8,512,128]{2,1,0:T(8,128)(2,1)} %copy-done.7, bf16[1024,2048]{1,0:T(8,128)(2,1)} %refs_9_.5), custom_call_target="tpu_custom_call" | custom-call | flops 2147483648 | bytes 4194304 | tf_op jit(solution)/shard_map/hidden/pallas_call | solution.py:120
  56.8 1.6 collective-permute-start.16
  58.4 0.6 pad_add_fusion.1.place_ref
  59.0 0.6 pad_add_fusion.place_ref
  59.6 0.4 collective-permute-start.13
  60.0 0.2 collective-permute-start.17
  60.2 0.6 collective-permute-start.14
  60.8 9.4 %mixed.2 = bf16[4,512,512]{2,1,0:T(8,128)(2,1)} custom-call(s32[4]{0:T(128)} %pad_add_fusion.1.place_ref, bf16[512,2048]{1,0:T(8,128)(2,1)} %hidden.1.hidden_ref, bf16[2048,4096]{1,0:T(8,128)(2,1)} %refs_8_.5), custom_call_target="tpu_custom_call" | custom-call | flops 4294967296 | bytes 8388608 | tf_op jit(solution)/shard_map/mixed/pallas_call | solution.py:139
  70.3 9.8 %mixed.3 = f32[4,512,512]{2,1,0:T(8,128)} custom-call(s32[4]{0:T(128)} %pad_add_fusion.place_ref, bf16[512,2048]{1,0:T(8,128)(2,1)} %hidden.1.hidden_ref, bf16[2048,4096]{1,0:T(8,128)(2,1)} %refs_8_.5), custom_call_target="tpu_custom_call" | custom-call | flops 4294967296 | bytes 8388608 | tf_op jit(solution)/shard_map/mixed/pallas_call | solution.py:139
  80.2 1.4 collective-permute-done.16.refs_1_.refs_5_.refs_9_
  81.6 1.5 collective-permute-start.21
  83.1 0.7 collective-permute-start.15
  83.9 0.6 concatenate.19.place_ref
  84.5 1.6 broadcast_in_dim.10.refs_7_
  86.0 10.5 %chunk_backward.4 = (bf16[512,512]{1,0:T(8,128)(2,1)}, f32[1024,512]{1,0:T(8,128)}) custom-call(s32[9]{0:T(128)} %concatenate.19.place_ref, bf16[2,512,512]{2,1,0:T(8,128)(2,1)} %pad_maximum_fusion.3.refs_0_.refs_4_, bf16[2,512,512]{2,1,0:T(8,128)(2,1)} %copy-done.8, bf16[2,512,512]{2,1,0:T(8,128)(2,1)} %collective-permute-done.19.refs_2_.refs_6_, ...), custom_call_target="tpu_custom_call" | custom-call | flops 3221225472 | bytes 14680064 | tf_op jit(solution)/shard_map/chunk_backward/pallas_call | solution.py:205
  96.6 10.8 %chunk_backward.5 = (bf16[512,512]{1,0:T(8,128)(2,1)}, f32[1024,512]{1,0:T(8,128)}) custom-call(s32[9]{0:T(128)} %concatenate.19.place_ref, bf16[2,512,640]{2,1,0:T(8,128)(2,1)} %copy-done.2, bf16[2,512,640]{2,1,0:T(8,128)(2,1)} %collective-permute-done.16.refs_1_.refs_5_.refs_9_, bf16[2,512,640]{2,1,0:T(8,128)(2,1)} %collective-permute-done.17.refs_2_.refs_6_.refs_10_, ...), custom_call_target="tpu_custom_call" | custom-call | flops 3221225472 | bytes 14680064 | tf_op jit(solution)/shard_map/chunk_backward/pallas_call | solution.py:205
  107.5 1.2 pad_maximum_fusion.2.refs_0_.refs_4_.refs_16_
  108.8 0.5 collective-permute-start.23
  109.3 1.5 collective-permute-start.20
  110.8 4.3 %convert_add_fusion = f32[4,512,512]{2,1,0:T(8,128)} fusion(f32[4,512,512]{2,1,0:T(8,128)S(1)} %copy-done, bf16[4,512,512]{2,1,0:T(8,128)(2,1)} %collective-permute-done.12), kind=kLoop, calls=%fused_computation | loop fusion | flops 2097152 | bytes 10485760 | tf_op jit(solution)/shard_map/add | solution.py:399
  115.2 10.3 %chunk_backward.6 = (bf16[512,512]{1,0:T(8,128)(2,1)}, f32[1024,512]{1,0:T(8,128)}) custom-call(s32[9]{0:T(128)} %concatenate.19.place_ref, bf16[2,512,640]{2,1,0:T(8,128)(2,1)} %copy-done.3, bf16[2,512,640]{2,1,0:T(8,128)(2,1)} %collective-permute-done.21.refs_1_.refs_5_.refs_13_, bf16[2,512,640]{2,1,0:T(8,128)(2,1)} %collective-permute-done.22.refs_2_.refs_6_.refs_14_, ...), custom_call_target="tpu_custom_call" | custom-call | flops 3221225472 | bytes 14680064 | tf_op jit(solution)/shard_map/chunk_backward/pallas_call | solution.py:205
  125.5 1.5 collective-permute-done.20.refs_1_.refs_5_.refs_17_
  127.0 3.0 %slice.47 = bf16[2,512,512]{2,1,0:T(8,128)(2,1)} slice(f32[4,512,512]{2,1,0:T(8,128)} %convert_add_fusion), slice={[2:4], [0:512], [0:512]} | slice | bytes 2097152 | tf_op jit(solution)/shard_map/slice | solution.py:405
  130.0 1.5 collective-permute-start.24
  131.5 1.1 copy-done.5
  132.6 10.3 %chunk_backward.7 = (bf16[512,512]{1,0:T(8,128)(2,1)}, f32[1024,512]{1,0:T(8,128)}) custom-call(s32[9]{0:T(128)} %concatenate.19.place_ref, bf16[2,512,640]{2,1,0:T(8,128)(2,1)} %copy-done.4, bf16[2,512,640]{2,1,0:T(8,128)(2,1)} %collective-permute-done.20.refs_1_.refs_5_.refs_17_, bf16[2,512,640]{2,1,0:T(8,128)(2,1)} %collective-permute-done.25.refs_2_.refs_6_.refs_18_, ...), custom_call_target="tpu_custom_call" | custom-call | flops 3221225472 | bytes 14680064 | tf_op jit(solution)/shard_map/chunk_backward/pallas_call | solution.py:205
  142.9 1.6 dynamic-slice_convert_fusion
  144.5 0.5 collective-permute-start.28
  145.0 2.6 %collective-permute-start.29 = (bf16[256,512]{1,0:T(8,128)(2,1)S(1)}, bf16[256,512]{1,0:T(8,128)(2,1)}, u32[]{:S(2)}, u32[]{:S(2)}) collective-permute-start(bf16[256,512]{1,0:T(8,128)(2,1)S(1)} %get-tuple-element.66), channel_id=1, source_target_pairs={{0,2},{1,3},{2,0},{3,1},{4,6},{5,7},{6,4},{7,5},{8,10},{9,11},{10,... | collective-permute-start | bytes 786440 | tf_op jit(solution)/shard_map/ppermute | solution.py:327
  147.6 1.4 collective-permute-start.30
  149.0 1.5 convert_element_type.38
  150.5 0.3 fusion.4
  150.8 0.6 collective-permute-start.27
  151.4 16.3 %grad_out.1 = f32[512,4096]{1,0:T(8,128)} custom-call(s32[8]{0:T(128)} %stack.85.place_ref, bf16[512,512]{1,0:T(8,128)(2,1)} %get-tuple-element.60.refs_0_, bf16[512,512]{1,0:T(8,128)(2,1)} %get-tuple-element.61.refs_1_, bf16[512,512]{1,0:T(8,128)(2,1)} %get-tuple-element.62.refs_2_, bf16[512,512]{1,0:T(8,128)(2,1)} %get-tuple-element.63.refs_3_, ...), custom_call_target="tpu_custom_call" | custom-call | flops 8589934592 | bytes 27262976 | tf_op jit(solution)/shard_map/grad_out/pallas_call | solution.py:276
  167.7 0.2 broadcast_in_dim.11
  167.9 1.1 dynamic-slice_dynamic-update-slice_fusion
  169.0 1.0 convert_dynamic-update-slice_fusion.2
  170.0 1.0 convert_dynamic-update-slice_fusion.1
  171.1 1.0 convert_dynamic-update-slice_fusion
  172.1 1.3 fusion.3
  (66 shorter events, 1.1 us)
Async XLA Ops:
  0.6 14.6 %copy-start.10 = (bf16[512,512]{1,0:T(8,128)(2,1)S(1)}, bf16[512,512]{1,0:T(8,128)(2,1)}, u32[]{:S(2)}) copy-start(bf16[512,512]{1,0:T(8,128)(2,1)} %param.13) | copy-start | bytes 1572868
  0.6 18.8 %copy-start.11 = (s32[512,1,16]{0,2,1:T(8,128)S(1)}, s32[512,1,16]{0,2,1:T(8,128)}, u32[]{:S(2)}) copy-start(s32[512,1,16]{0,2,1:T(8,128)} %param.7) | copy-start | bytes 98308
  0.7 19.7 %copy-start.12 = (s32[512,1]{0,1:T(1,128)S(1)}, s32[512,1]{0,1:T(1,128)}, u32[]{:S(2)}) copy-start(s32[512,1]{0,1:T(1,128)} %param.8) | copy-start | bytes 6148
  0.7 10.4 %collective-permute-start = (bf16[512,512]{1,0:T(8,128)(2,1)}, bf16[512,512]{1,0:T(8,128)(2,1)S(1)}, u32[]{:S(2)}, u32[]{:S(2)}) collective-permute-start(bf16[512,512]{1,0:T(8,128)(2,1)} %param.13), channel_id=1, source_target_pairs={{0,16},{4,20},{8,12},{12,8},{16,0},{20,4},{24,28},{28,24},{1,17},{... | collective-permute-start | bytes 1572872 | tf_op jit(solution)/shard_map/ppermute | solution.py:315
  13.2 20.4 %collective-permute-start.2 = (bf16[2,512,512]{2,1,0:T(8,128)(2,1)}, bf16[2,512,512]{2,1,0:T(8,128)(2,1)S(1)}, u32[]{:S(2)}, u32[]{:S(2)}) collective-permute-start(bf16[2,512,512]{2,1,0:T(8,128)(2,1)} %pad_maximum_fusion.3.refs_0_.refs_4_), channel_id=1, source_target_pairs={{0,4},{4,0},{8,24},{12,28},{16,20},{20,16},{24,8},{28,12},{1,5},{5... | collective-permute-start | bytes 3145736 | tf_op jit(solution)/shard_map/ppermute | solution.py:319
  15.2 26.4 %collective-permute-start.7 = (bf16[512,512]{1,0:T(8,128)(2,1)S(1)}, bf16[512,512]{1,0:T(8,128)(2,1)S(1)}, u32[]{:S(2)}, u32[]{:S(2)}) collective-permute-start(bf16[512,512]{1,0:T(8,128)(2,1)S(1)} %copy-done.10), channel_id=1, source_target_pairs={{0,1},{1,0},{2,3},{3,2},{4,5},{5,4},{6,7},{7,6},{8,9},{9,8},{10,11... | collective-permute-start | bytes 1572872 | tf_op jit(solution)/shard_map/ppermute | solution.py:327
  16.8 26.7 %collective-permute-start.6 = (bf16[512,512]{1,0:T(8,128)(2,1)S(1)}, bf16[512,512]{1,0:T(8,128)(2,1)S(1)}, u32[]{:S(2)}, u32[]{:S(2)}) collective-permute-start(bf16[512,512]{1,0:T(8,128)(2,1)S(1)} %copy-done.10), channel_id=1, source_target_pairs={{0,2},{1,3},{2,0},{3,1},{4,6},{5,7},{6,4},{7,5},{8,10},{9,11},{10,... | collective-permute-start | bytes 1572872 | tf_op jit(solution)/shard_map/ppermute | solution.py:327
  28.1 5.2 %collective-permute-start.1 = (bf16[512,128]{1,0:T(8,128)(2,1)}, bf16[512,128]{1,0:T(8,128)(2,1)S(1)}, u32[]{:S(2)}, u32[]{:S(2)}) collective-permute-start(bf16[512,128]{1,0:T(8,128)(2,1)} %pool.1), channel_id=1, source_target_pairs={{0,16},{4,20},{8,12},{12,8},{16,0},{20,4},{24,28},{28,24},{1,17},{... | collective-permute-start | bytes 393224 | tf_op jit(solution)/shard_map/ppermute | solution.py:315
  29.6 13.4 %collective-permute-start.8 = (bf16[512,128]{1,0:T(8,128)(2,1)}, bf16[512,128]{1,0:T(8,128)(2,1)S(1)}, u32[]{:S(2)}, u32[]{:S(2)}) collective-permute-start(bf16[512,128]{1,0:T(8,128)(2,1)} %pool.1), channel_id=1, source_target_pairs={{0,1},{1,0},{2,3},{3,2},{4,5},{5,4},{6,7},{7,6},{8,9},{9,8},{10,11... | collective-permute-start | bytes 393224 | tf_op jit(solution)/shard_map/ppermute | solution.py:327
  33.3 13.5 %collective-permute-start.9 = (bf16[512,128]{1,0:T(8,128)(2,1)}, bf16[512,128]{1,0:T(8,128)(2,1)S(1)}, u32[]{:S(2)}, u32[]{:S(2)}) collective-permute-start(bf16[512,128]{1,0:T(8,128)(2,1)} %pool.1), channel_id=1, source_target_pairs={{0,2},{1,3},{2,0},{3,1},{4,6},{5,7},{6,4},{7,5},{8,10},{9,11},{10,... | collective-permute-start | bytes 393224 | tf_op jit(solution)/shard_map/ppermute | solution.py:327
  33.6 13.9 %copy-start.8 = (bf16[2,512,512]{2,1,0:T(8,128)(2,1)}, bf16[2,512,512]{2,1,0:T(8,128)(2,1)S(1)}, u32[]{:S(2)}) copy-start(bf16[2,512,512]{2,1,0:T(8,128)(2,1)S(1)} %collective-permute-done.2.refs_1_.refs_5_) | copy-start | bytes 3145732
  34.7 12.1 %collective-permute-start.3 = (bf16[2,512,128]{2,1,0:T(8,128)(2,1)S(1)}, bf16[2,512,128]{2,1,0:T(8,128)(2,1)S(1)}, u32[]{:S(2)}, u32[]{:S(2)}) collective-permute-start(bf16[2,512,128]{2,1,0:T(8,128)(2,1)S(1)} %pad_maximum_fusion.4), channel_id=1, source_target_pairs={{0,4},{4,0},{8,24},{12,28},{16,20},{20,16},{24,8},{28,12},{1,5},{5... | collective-permute-start | bytes 786440 | tf_op jit(solution)/shard_map/ppermute | solution.py:319
  41.6 5.9 %collective-permute-start.4 = (bf16[2,512,128]{2,1,0:T(8,128)(2,1)S(1)}, bf16[2,512,128]{2,1,0:T(8,128)(2,1)S(1)}, u32[]{:S(2)}, u32[]{:S(2)}) collective-permute-start(bf16[2,512,128]{2,1,0:T(8,128)(2,1)S(1)} %pad_maximum_fusion.4), channel_id=1, source_target_pairs={{0,8},{8,0},{16,24},{24,16},{1,9},{9,1},{17,25},{25,17},{2,10},{10... | collective-permute-start | bytes 786440 | tf_op jit(solution)/shard_map/ppermute | solution.py:323
  43.1 13.6 %collective-permute-start.10 = (bf16[512,640]{1,0:T(8,128)(2,1)S(1)}, bf16[512,640]{1,0:T(8,128)(2,1)S(1)}, u32[]{:S(2)}, u32[]{:S(2)}) collective-permute-start(bf16[512,640]{1,0:T(8,128)(2,1)S(1)} %constant_dynamic-update-slice_fusion.5), channel_id=1, source_target_pairs={{0,16},{4,20},{8,12},{12,8},{16,0},{20,4},{24,28},{28,24},{1,17},{... | collective-permute-start | bytes 1966088 | tf_op jit(solution)/shard_map/ppermute | solution.py:315
  46.8 1.5 collective-permute-start.5
  46.9 13.2 %collective-permute-start.11 = (bf16[2,512,512]{2,1,0:T(8,128)(2,1)S(1)}, bf16[2,512,512]{2,1,0:T(8,128)(2,1)S(1)}, u32[]{:S(2)}, u32[]{:S(2)}) collective-permute-start(bf16[2,512,512]{2,1,0:T(8,128)(2,1)S(1)} %collective-permute-done.2.refs_1_.refs_5_), channel_id=1, source_target_pairs={{0,8},{8,0},{16,24},{24,16},{1,9},{9,1},{17,25},{25,17},{2,10},{10... | collective-permute-start | bytes 3145736 | tf_op jit(solution)/shard_map/ppermute | solution.py:323
  48.4 1.0 copy-start.7
  56.8 13.5 %copy-start.2 = (bf16[2,512,640]{2,1,0:T(8,128)(2,1)}, bf16[2,512,640]{2,1,0:T(8,128)(2,1)S(1)}, u32[]{:S(2)}) copy-start(bf16[2,512,640]{2,1,0:T(8,128)(2,1)S(1)} %pad_maximum_fusion.refs_0_.refs_4_.refs_8_) | copy-start | bytes 3932164
  56.8 24.8 %collective-permute-start.16 = (bf16[2,512,640]{2,1,0:T(8,128)(2,1)S(1)}, bf16[2,512,640]{2,1,0:T(8,128)(2,1)}, u32[]{:S(2)}, u32[]{:S(2)}) collective-permute-start(bf16[2,512,640]{2,1,0:T(8,128)(2,1)S(1)} %pad_maximum_fusion.refs_0_.refs_4_.refs_8_), channel_id=1, source_target_pairs={{0,4},{4,0},{8,24},{12,28},{16,20},{20,16},{24,8},{28,12},{1,5},{5... | collective-permute-start | bytes 3932168 | tf_op jit(solution)/shard_map/ppermute | solution.py:319
  59.6 23.6 %collective-permute-start.19 = (bf16[2,512,512]{2,1,0:T(8,128)(2,1)}, bf16[2,512,512]{2,1,0:T(8,128)(2,1)}, u32[]{:S(2)}, u32[]{:S(2)}) collective-permute-start(bf16[2,512,512]{2,1,0:T(8,128)(2,1)} %pad_maximum_fusion.3.refs_0_.refs_4_), channel_id=1, source_target_pairs={{0,8},{8,0},{16,24},{24,16},{1,9},{9,1},{17,25},{25,17},{2,10},{10... | collective-permute-start | bytes 3145736 | tf_op jit(solution)/shard_map/ppermute | solution.py:323
  59.6 23.6 %collective-permute-start.13 = (bf16[512,640]{1,0:T(8,128)(2,1)S(1)}, bf16[512,640]{1,0:T(8,128)(2,1)S(1)}, u32[]{:S(2)}, u32[]{:S(2)}) collective-permute-start(bf16[512,640]{1,0:T(8,128)(2,1)S(1)} %constant_dynamic-update-slice_fusion.7), channel_id=1, source_target_pairs={{0,1},{1,0},{2,3},{3,2},{4,5},{5,4},{6,7},{7,6},{8,9},{9,8},{10,11... | collective-permute-start | bytes 1966088 | tf_op jit(solution)/shard_map/ppermute | solution.py:327
  60.0 36.6 %collective-permute-start.17 = (bf16[2,512,640]{2,1,0:T(8,128)(2,1)S(1)}, bf16[2,512,640]{2,1,0:T(8,128)(2,1)}, u32[]{:S(2)}, u32[]{:S(2)}) collective-permute-start(bf16[2,512,640]{2,1,0:T(8,128)(2,1)S(1)} %pad_maximum_fusion.refs_0_.refs_4_.refs_8_), channel_id=1, source_target_pairs={{0,8},{8,0},{16,24},{24,16},{1,9},{9,1},{17,25},{25,17},{2,10},{10... | collective-permute-start | bytes 3932168 | tf_op jit(solution)/shard_map/ppermute | solution.py:323
  60.2 10.1 %copy-start.9 = (bf16[2,512,512]{2,1,0:T(8,128)(2,1)}, bf16[2,512,512]{2,1,0:T(8,128)(2,1)S(1)}, u32[]{:S(2)}) copy-start(bf16[2,512,512]{2,1,0:T(8,128)(2,1)S(1)} %collective-permute-done.11.refs_3_.refs_7_) | copy-start | bytes 3145732
  60.2 19.9 %collective-permute-start.14 = (bf16[512,640]{1,0:T(8,128)(2,1)S(1)}, bf16[512,640]{1,0:T(8,128)(2,1)S(1)}, u32[]{:S(2)}, u32[]{:S(2)}) collective-permute-start(bf16[512,640]{1,0:T(8,128)(2,1)S(1)} %constant_dynamic-update-slice_fusion.7), channel_id=1, source_target_pairs={{0,16},{4,20},{8,12},{12,8},{16,0},{20,4},{24,28},{28,24},{1,17},{... | collective-permute-start | bytes 1966088 | tf_op jit(solution)/shard_map/ppermute | solution.py:315
  80.2 16.3 %copy-start.3 = (bf16[2,512,640]{2,1,0:T(8,128)(2,1)}, bf16[2,512,640]{2,1,0:T(8,128)(2,1)S(1)}, u32[]{:S(2)}) copy-start(bf16[2,512,640]{2,1,0:T(8,128)(2,1)S(1)} %pad_maximum_fusion.1.refs_0_.refs_4_.refs_12_) | copy-start | bytes 3932164
  81.6 15.0 %collective-permute-start.18 = (bf16[2,512,640]{2,1,0:T(8,128)(2,1)}, bf16[2,512,640]{2,1,0:T(8,128)(2,1)}, u32[]{:S(2)}, u32[]{:S(2)}) collective-permute-start(bf16[2,512,640]{2,1,0:T(8,128)(2,1)} %collective-permute-done.16.refs_1_.refs_5_.refs_9_), channel_id=1, source_target_pairs={{0,8},{8,0},{16,24},{24,16},{1,9},{9,1},{17,25},{25,17},{2,10},{10... | collective-permute-start | bytes 3932168 | tf_op jit(solution)/shard_map/ppermute | solution.py:323
  81.6 27.1 %collective-permute-start.21 = (bf16[2,512,640]{2,1,0:T(8,128)(2,1)S(1)}, bf16[2,512,640]{2,1,0:T(8,128)(2,1)}, u32[]{:S(2)}, u32[]{:S(2)}) collective-permute-start(bf16[2,512,640]{2,1,0:T(8,128)(2,1)S(1)} %pad_maximum_fusion.1.refs_0_.refs_4_.refs_12_), channel_id=1, source_target_pairs={{0,4},{4,0},{8,24},{12,28},{16,20},{20,16},{24,8},{28,12},{1,5},{5... | collective-permute-start | bytes 3932168 | tf_op jit(solution)/shard_map/ppermute | solution.py:319
  83.1 27.7 %collective-permute-start.12 = (bf16[4,512,512]{2,1,0:T(8,128)(2,1)}, bf16[4,512,512]{2,1,0:T(8,128)(2,1)}, u32[]{:S(2)}, u32[]{:S(2)}) collective-permute-start(bf16[4,512,512]{2,1,0:T(8,128)(2,1)} %mixed.2), channel_id=1, source_target_pairs={{0,8},{8,0},{16,24},{24,16},{1,9},{9,1},{17,25},{25,17},{2,10},{10... | collective-permute-start | bytes 6291464 | tf_op jit(solution)/shard_map/ppermute | solution.py:323
  83.1 24.4 %collective-permute-start.15 = (bf16[512,640]{1,0:T(8,128)(2,1)S(1)}, bf16[512,640]{1,0:T(8,128)(2,1)}, u32[]{:S(2)}, u32[]{:S(2)}) collective-permute-start(bf16[512,640]{1,0:T(8,128)(2,1)S(1)} %collective-permute-done.13), channel_id=1, source_target_pairs={{0,16},{4,20},{8,12},{12,8},{16,0},{20,4},{24,28},{28,24},{1,17},{... | collective-permute-start | bytes 1966088 | tf_op jit(solution)/shard_map/ppermute | solution.py:315
  96.5 18.6 %collective-permute-start.22 = (bf16[2,512,640]{2,1,0:T(8,128)(2,1)S(1)}, bf16[2,512,640]{2,1,0:T(8,128)(2,1)}, u32[]{:S(2)}, u32[]{:S(2)}) collective-permute-start(bf16[2,512,640]{2,1,0:T(8,128)(2,1)S(1)} %pad_maximum_fusion.1.refs_0_.refs_4_.refs_12_), channel_id=1, source_target_pairs={{0,8},{8,0},{16,24},{24,16},{1,9},{9,1},{17,25},{25,17},{2,10},{10... | collective-permute-start | bytes 3932168 | tf_op jit(solution)/shard_map/ppermute | solution.py:323
  96.6 14.2 %copy-start = (f32[4,512,512]{2,1,0:T(8,128)S(1)}, f32[4,512,512]{2,1,0:T(8,128)}, u32[]{:S(2)}) copy-start(f32[4,512,512]{2,1,0:T(8,128)} %mixed.3) | copy-start | bytes 12582916
  108.7 6.4 %copy-start.4 = (bf16[2,512,640]{2,1,0:T(8,128)(2,1)}, bf16[2,512,640]{2,1,0:T(8,128)(2,1)S(1)}, u32[]{:S(2)}) copy-start(bf16[2,512,640]{2,1,0:T(8,128)(2,1)S(1)} %pad_maximum_fusion.2.refs_0_.refs_4_.refs_16_) | copy-start | bytes 3932164
  108.8 6.4 %collective-permute-start.23 = (bf16[2,512,640]{2,1,0:T(8,128)(2,1)}, bf16[2,512,640]{2,1,0:T(8,128)(2,1)}, u32[]{:S(2)}, u32[]{:S(2)}) collective-permute-start(bf16[2,512,640]{2,1,0:T(8,128)(2,1)} %collective-permute-done.21.refs_1_.refs_5_.refs_13_), channel_id=1, source_target_pairs={{0,8},{8,0},{16,24},{24,16},{1,9},{9,1},{17,25},{25,17},{2,10},{10... | collective-permute-start | bytes 3932168 | tf_op jit(solution)/shard_map/ppermute | solution.py:323
  109.3 17.7 %collective-permute-start.20 = (bf16[2,512,640]{2,1,0:T(8,128)(2,1)S(1)}, bf16[2,512,640]{2,1,0:T(8,128)(2,1)}, u32[]{:S(2)}, u32[]{:S(2)}) collective-permute-start(bf16[2,512,640]{2,1,0:T(8,128)(2,1)S(1)} %pad_maximum_fusion.2.refs_0_.refs_4_.refs_16_), channel_id=1, source_target_pairs={{0,4},{4,0},{8,24},{12,28},{16,20},{20,16},{24,8},{28,12},{1,5},{5... | collective-permute-start | bytes 3932168 | tf_op jit(solution)/shard_map/ppermute | solution.py:319
  110.8 20.7 %collective-permute-start.25 = (bf16[2,512,640]{2,1,0:T(8,128)(2,1)S(1)}, bf16[2,512,640]{2,1,0:T(8,128)(2,1)}, u32[]{:S(2)}, u32[]{:S(2)}) collective-permute-start(bf16[2,512,640]{2,1,0:T(8,128)(2,1)S(1)} %pad_maximum_fusion.2.refs_0_.refs_4_.refs_16_), channel_id=1, source_target_pairs={{0,8},{8,0},{16,24},{24,16},{1,9},{9,1},{17,25},{25,17},{2,10},{10... | collective-permute-start | bytes 3932168 | tf_op jit(solution)/shard_map/ppermute | solution.py:323
  127.0 4.5 %collective-permute-start.26 = (bf16[2,512,640]{2,1,0:T(8,128)(2,1)}, bf16[2,512,640]{2,1,0:T(8,128)(2,1)S(1)}, u32[]{:S(2)}, u32[]{:S(2)}) collective-permute-start(bf16[2,512,640]{2,1,0:T(8,128)(2,1)} %collective-permute-done.20.refs_1_.refs_5_.refs_17_), channel_id=1, source_target_pairs={{0,8},{8,0},{16,24},{24,16},{1,9},{9,1},{17,25},{25,17},{2,10},{10... | collective-permute-start | bytes 3932168 | tf_op jit(solution)/shard_map/ppermute | solution.py:323
  130.0 19.0 %collective-permute-start.24 = (bf16[2,512,512]{2,1,0:T(8,128)(2,1)}, bf16[2,512,512]{2,1,0:T(8,128)(2,1)}, u32[]{:S(2)}, u32[]{:S(2)}) collective-permute-start(bf16[2,512,512]{2,1,0:T(8,128)(2,1)} %slice.47), channel_id=1, source_target_pairs={{0,4},{4,0},{8,24},{12,28},{16,20},{20,16},{24,8},{28,12},{1,5},{5... | collective-permute-start | bytes 3145736 | tf_op jit(solution)/shard_map/ppermute | solution.py:319
  131.5 1.1 copy-start.5
  142.9 7.6 %copy-start.1 = (f32[4,512,512]{2,1,0:T(8,128)S(1)}, f32[4,512,512]{2,1,0:T(8,128)}, u32[]{:S(2)}) copy-start(f32[4,512,512]{2,1,0:T(8,128)} %convert_add_fusion) | copy-start | bytes 12582916
  144.5 24.5 %collective-permute-start.28 = (bf16[256,512]{1,0:T(8,128)(2,1)S(1)}, bf16[256,512]{1,0:T(8,128)(2,1)}, u32[]{:S(2)}, u32[]{:S(2)}) collective-permute-start(bf16[256,512]{1,0:T(8,128)(2,1)S(1)} %get-tuple-element.67), channel_id=1, source_target_pairs={{0,1},{1,0},{2,3},{3,2},{4,5},{5,4},{6,7},{7,6},{8,9},{9,8},{10,11... | collective-permute-start | bytes 786440 | tf_op jit(solution)/shard_map/ppermute | solution.py:327
  145.0 25.0 %collective-permute-start.29 = (bf16[256,512]{1,0:T(8,128)(2,1)S(1)}, bf16[256,512]{1,0:T(8,128)(2,1)}, u32[]{:S(2)}, u32[]{:S(2)}) collective-permute-start(bf16[256,512]{1,0:T(8,128)(2,1)S(1)} %get-tuple-element.66), channel_id=1, source_target_pairs={{0,2},{1,3},{2,0},{3,1},{4,6},{5,7},{6,4},{7,5},{8,10},{9,11},{10,... | collective-permute-start | bytes 786440 | tf_op jit(solution)/shard_map/ppermute | solution.py:327
  147.6 23.4 %collective-permute-start.30 = (bf16[256,512]{1,0:T(8,128)(2,1)S(1)}, bf16[256,512]{1,0:T(8,128)(2,1)}, u32[]{:S(2)}, u32[]{:S(2)}) collective-permute-start(bf16[256,512]{1,0:T(8,128)(2,1)S(1)} %get-tuple-element.65), channel_id=1, source_target_pairs={{0,3},{1,2},{2,1},{3,0},{4,7},{5,6},{6,5},{7,4},{8,11},{9,10},{10,... | collective-permute-start | bytes 786440 | tf_op jit(solution)/shard_map/ppermute | solution.py:327
  150.8 21.3 %collective-permute-start.27 = (bf16[512,512]{1,0:T(8,128)(2,1)S(1)}, bf16[512,512]{1,0:T(8,128)(2,1)S(1)}, u32[]{:S(2)}, u32[]{:S(2)}) collective-permute-start(bf16[512,512]{1,0:T(8,128)(2,1)S(1)} %fusion.4), channel_id=1, source_target_pairs={{0,16},{4,20},{8,12},{12,8},{16,0},{20,4},{24,28},{28,24},{1,17},{... | collective-permute-start | bytes 1572872 | tf_op jit(solution)/shard_map/ppermute | solution.py:315
  172.1 1.5 copy-start.6

commit v3 on v2

v3 whole, which is shorter than its diff:
```python
import functools

import jax
import jax.numpy as jnp
from jax import lax
from jax.experimental import pallas as pl
from jax.experimental.pallas import tpu as pltpu
from jax.sharding import PartitionSpec as P

F32 = jnp.float32
BF16 = jnp.bfloat16
PLANE = ("table", "tensor")
VMEM_MIB = 50
ROWS_TN = (((0,), (0,)), ((), ()))
COLS_NT = (((1,), (1,)), ((), ()))


def silu_slope(preact):
    sigmoid_part = jax.nn.sigmoid(preact)
    return sigmoid_part * (1.0 + preact * (1.0 - sigmoid_part))


def cost(flops, bytes_accessed, transcendentals):
    return pl.CostEstimate(flops=flops, bytes_accessed=bytes_accessed, transcendentals=transcendentals)


def params(mib):
    return pltpu.CompilerParams(vmem_limit_bytes=mib * 1024 * 1024)


def pool_kernel(key_ref, len_ref, width_ref, table_ref, out_ref, counts_ref, *, group, low):
    samples, columns = out_ref.shape
    slots = key_ref.shape[1]
    bag = slots // group
    high = table_ref.shape[0] // low
    rows = lax.broadcasted_iota(jnp.int32, (high * group, slots), 0)
    low_rows = lax.broadcasted_iota(jnp.int32, (low, slots), 0)
    lane = lax.broadcasted_iota(jnp.int32, (1, slots), 1)
    member, slot = lane // bag, lax.rem(lane, bag)
    group_rows = lax.broadcasted_iota(jnp.int32, (group, slots), 0)

    def one_group(g, carry):
        first = pl.multiple_of(g * group, group)
        lengths = jnp.where(group_rows == member, len_ref[pl.ds(first, group), :], 0)
        in_bag = slot < jnp.sum(lengths, axis=0, keepdims=True)
        key = key_ref[pl.ds(g, 1), :]
        hit_high = (rows == jnp.where(in_bag, (key // low) * group + member, -1)).astype(BF16)
        hit_low = (low_rows == lax.rem(key, low)).astype(BF16)
        counts = lax.dot_general(hit_high, hit_low, COLS_NT, preferred_element_type=F32).astype(BF16)
        for h in range(high):
            counts_ref[h, pl.ds(first, group), :] = counts[h * group : (h + 1) * group, :]
        return carry

    lax.fori_loop(0, samples // group, one_group, 0, unroll=4)
    total = jnp.zeros(out_ref.shape, F32)
    for h in range(high):
        total += jnp.dot(
            counts_ref[h], table_ref[h * low : (h + 1) * low, :], preferred_element_type=F32
        )
    pooled = total / len_ref[...].astype(F32)
    position = lax.axis_index("tensor") * columns + lax.broadcasted_iota(jnp.int32, pooled.shape, 1)
    out_ref[...] = jnp.where(position < width_ref[lax.axis_index("table")], pooled, 0.0).astype(BF16)


def pool_local(lookup_ids, bag_lengths, feature_widths, embedding):
    samples, unused, bag = lookup_ids.shape
    vocab, columns = embedding.shape
    low, group = 256, 16
    high = vocab // low
    return pl.pallas_call(
        functools.partial(pool_kernel, group=group, low=low),
        out_shape=jax.ShapeDtypeStruct((samples, columns), BF16),
        in_specs=[
            pl.BlockSpec(memory_space=pltpu.VMEM),
            pl.BlockSpec(memory_space=pltpu.VMEM),
            pl.BlockSpec(memory_space=pltpu.SMEM),
            pl.BlockSpec(memory_space=pltpu.VMEM),
        ],
        out_specs=pl.BlockSpec(memory_space=pltpu.VMEM),
        scratch_shapes=[pltpu.VMEM((high, samples, low), BF16)],
        compiler_params=params(VMEM_MIB),
        cost_estimate=cost(20 * samples * vocab * columns, 2 * vocab * columns, 0),
        name="pool",
    )(lookup_ids.reshape(samples // group, group * bag), bag_lengths, feature_widths, embedding)


def carry_kernel(block_ref, feat_ref, out_ref):
    wide = block_ref.shape[1]
    out_ref[:, :wide] = block_ref[...]
    out_ref[:, wide:] = feat_ref[...]


def carry(block, feat, weight):
    in_vmem = pl.BlockSpec(memory_space=pltpu.VMEM)
    samples, wide = block.shape
    return pl.pallas_call(
        carry_kernel,
        out_shape=jax.ShapeDtypeStruct((samples, wide + feat.shape[1]), BF16),
        in_specs=[in_vmem, in_vmem],
        out_specs=in_vmem,
        cost_estimate=cost(weight * 10**9, 0, 0),
        name="carry",
    )(block, feat)


def block_copies(place_ref, refs, first, width, buffer, sem, in_place):
    copies = []
    each = 8 // len(refs)
    for j in range(8):
        to = pl.multiple_of(place_ref[j] * width, width) if in_place else j * width
        source = refs[j // each].at[j % each, :, pl.ds(first, width)]
        copies.append(pltpu.make_async_copy(source, buffer.at[:, pl.ds(to, width)], sem.at[j]))
    return copies


def start_all(copies):
    for c in copies:
        c.start()


def wait_all(copies):
    for c in copies:
        c.wait()


def forward_kernel(
    place_ref, feat_ref, other_feat_ref, w_in_ref, w_out_ref, away_ref, near_ref,
    feat_buf, w_in_buf, hidden_buf, w_out_buf, away_buf, near_buf,
    feat_sem, w_in_sem, w_out_sem, away_sem, near_sem,
):
    pieces, samples, step = w_in_buf.shape[0], hidden_buf.shape[0], w_in_buf.shape[2]
    buffers, wide = w_out_buf.shape[0], w_out_buf.shape[2]
    half = away_ref.shape[0]
    feat_copies = block_copies(
        place_ref, [feat_ref, other_feat_ref], 0, feat_ref.shape[2], feat_buf, feat_sem, True
    )
    w_in_copies = [
        pltpu.make_async_copy(w_in_ref.at[:, pl.ds(i * step, step)], w_in_buf.at[i], w_in_sem.at[i])
        for i in range(pieces)
    ]
    slots = [*range(half, 2 * half), *range(half)]
    w_out_copies = []
    for i, slot in enumerate(slots):
        column = pl.ds(pl.multiple_of(place_ref[slot] * wide, wide), wide)
        w_out_copies.append(
            pltpu.make_async_copy(w_out_ref.at[:, column], w_out_buf.at[i % buffers], w_out_sem.at[i % buffers])
        )
    start_all(feat_copies + w_in_copies + w_out_copies[: buffers - 1])
    wait_all(feat_copies)
    for i in range(pieces):
        w_in_copies[i].wait()
        preact = jnp.dot(feat_buf[...], w_in_buf[i], preferred_element_type=F32)
        hidden_buf[:, i * step : (i + 1) * step] = jax.nn.silu(preact).astype(BF16)
    out_copies = []
    for i in range(2 * half):
        if i + buffers - 1 < 2 * half:
            w_out_copies[i + buffers - 1].start()
        w_out_copies[i].wait()
        product = jnp.dot(hidden_buf[...], w_out_buf[i % buffers], preferred_element_type=F32)
        if i < half:
            away_buf[i] = product.astype(BF16)
            out_copies.append(pltpu.make_async_copy(away_buf.at[i], away_ref.at[i], away_sem.at[i]))
        else:
            near_buf[i - half] = product
            out_copies.append(pltpu.make_async_copy(near_buf.at[i - half], near_ref.at[i - half], near_sem.at[i - half]))
        out_copies[-1].start()
    wait_all(out_copies)


def forward(place, feat_blocks, w_in, w_out, wide):
    samples = feat_blocks[0].shape[1]
    depth, units = w_in.shape
    step, buffers = units // 4, 3
    any_space = pl.BlockSpec(memory_space=pl.ANY)
    return pl.pallas_call(
        forward_kernel,
        out_shape=(
            jax.ShapeDtypeStruct((4, samples, wide), BF16),
            jax.ShapeDtypeStruct((4, samples, wide), F32),
        ),
        in_specs=[pl.BlockSpec(memory_space=pltpu.SMEM)] + [any_space] * 4,
        out_specs=(any_space, any_space),
        scratch_shapes=[
            pltpu.VMEM((samples, depth), BF16),
            pltpu.VMEM((4, depth, step), BF16),
            pltpu.VMEM((samples, units), BF16),
            pltpu.VMEM((buffers, units, wide), BF16),
            pltpu.VMEM((4, samples, wide), BF16),
            pltpu.VMEM((4, samples, wide), F32),
            pltpu.SemaphoreType.DMA((8,)),
            pltpu.SemaphoreType.DMA((4,)),
            pltpu.SemaphoreType.DMA((buffers,)),
            pltpu.SemaphoreType.DMA((4,)),
            pltpu.SemaphoreType.DMA((4,)),
        ],
        compiler_params=params(VMEM_MIB),
        cost_estimate=cost(
            2 * samples * units * (depth + 8 * wide), 2 * units * (depth + 8 * wide), samples * units
        ),
        name="forward",
    )(place, *feat_blocks, w_in, w_out)


def chunk_kernel(place_ref, *refs, wide, firsts, feat_counts, add):
    chunks = len(firsts)
    cot_refs, refs = [refs[4 * k : 4 * k + 4] for k in range(chunks)], refs[4 * chunks :]
    feat_refs = []
    for n in feat_counts:
        feat_refs.append(refs[:n])
        refs = refs[n:]
    w_out_ref, w_in_ref, refs = refs[0], refs[1], refs[2:]
    sum_ref, refs = (refs[0], refs[1:]) if add else (None, refs)
    hidden_ref, grad_in_ref, cot_buf, w_out_buf, feat_buf, w_in_buf, sum_buf, cot_sem, w_sem, feat_sem, sem = refs
    units = hidden_ref.shape[0]
    samples = cot_buf.shape[0] // chunks
    row = pl.ds(pl.multiple_of(place_ref[8] * units, units), units)
    cot_copies, feat_copies, w_copies = [], [], []
    for k in range(chunks):
        rows = pl.ds(k * samples, samples)
        cot_copies.append(block_copies(place_ref, cot_refs[k], 0, wide, cot_buf.at[rows], cot_sem.at[k], False))
        feat_copies += block_copies(
            place_ref, feat_refs[k], firsts[k], feat_buf.shape[1] // 8, feat_buf.at[rows], feat_sem.at[k], True
        )
    for j in range(8):
        column = pl.ds(pl.multiple_of(place_ref[j] * wide, wide), wide)
        w_copies.append(
            pltpu.make_async_copy(w_out_ref.at[row, column], w_out_buf.at[:, pl.ds(j * wide, wide)], w_sem.at[j])
        )
    w_in_copy = pltpu.make_async_copy(w_in_ref.at[:, row], w_in_buf, sem.at[0])
    start_all(feat_copies)
    w_in_copy.start()
    early = [c for copies in cot_copies for c in copies[:4]] + w_copies[:4]
    late = [c for copies in cot_copies for c in copies[4:]] + w_copies[4:]
    start_all(early + late)
    if add:
        sum_copy = pltpu.make_async_copy(sum_ref, sum_buf, sem.at[1])
        sum_copy.start()

    wait_all(feat_copies)
    w_in_copy.wait()
    preact = jnp.dot(feat_buf[...], w_in_buf[...], preferred_element_type=F32)
    hidden_ref[...] = jax.nn.silu(preact).astype(BF16).T
    slope = silu_slope(preact)
    middle = 4 * wide
    wait_all(early)
    grad_hidden = lax.dot_general(
        cot_buf[:, :middle], w_out_buf[:, :middle], COLS_NT, preferred_element_type=F32
    )
    wait_all(late)
    grad_hidden += lax.dot_general(
        cot_buf[:, middle:], w_out_buf[:, middle:], COLS_NT, preferred_element_type=F32
    )
    grad_preact = (grad_hidden * slope).astype(BF16)
    term = lax.dot_general(feat_buf[...], grad_preact, ROWS_TN, preferred_element_type=F32)
    if add:
        sum_copy.wait()
        term += sum_buf[...]
    grad_in_ref[...] = term


def chunk_backward(place, cot, feat, firsts, w_out, w_in, running, units, wide):
    chunks = len(cot)
    samples = chunks * cot[0][0].shape[1]
    depth = w_in.shape[0]
    add = running is not None
    feat_counts = [len(f) for f in feat]
    operands = [v for c in cot for v in c] + [v for f in feat for v in f] + [w_out, w_in]
    operands += [running] if add else []
    in_vmem = pl.BlockSpec(memory_space=pltpu.VMEM)
    return pl.pallas_call(
        functools.partial(chunk_kernel, wide=wide, firsts=firsts, feat_counts=feat_counts, add=add),
        out_shape=(
            jax.ShapeDtypeStruct((units, samples), BF16),
            jax.ShapeDtypeStruct((depth, units), F32),
        ),
        in_specs=[pl.BlockSpec(memory_space=pltpu.SMEM)] + [pl.BlockSpec(memory_space=pl.ANY)] * len(operands),
        out_specs=(in_vmem, in_vmem),
        scratch_shapes=[
            pltpu.VMEM((samples, 8 * wide), BF16),
            pltpu.VMEM((units, 8 * wide), BF16),
            pltpu.VMEM((samples, depth), BF16),
            pltpu.VMEM((depth, units), BF16),
            pltpu.VMEM((depth, units) if add else (8, 128), F32),
            pltpu.SemaphoreType.DMA((chunks, 8)),
            pltpu.SemaphoreType.DMA((8,)),
            pltpu.SemaphoreType.DMA((chunks, 8)),
            pltpu.SemaphoreType.DMA((2,)),
        ],
        compiler_params=params(VMEM_MIB),
        cost_estimate=cost(
            2 * samples * units * (8 * wide + 2 * depth),
            2 * (samples + units) * (8 * wide + depth) + 8 * depth * units,
            2 * samples * units,
        ),
        name="chunk_backward",
    )(place, *operands)


def grad_out_kernel(place_ref, *refs, chunks):
    blocks, hidden = refs[: 4 * chunks], refs[4 * chunks : -5]
    out_ref, hidden_buf, cot_buf, hidden_sem, cot_sem = refs[-5:]
    samples, wide = cot_buf.shape[1] // chunks, out_ref.shape[1]
    j = pl.program_id(0)
    rows = [slice(k * samples, (k + 1) * samples) for k in range(chunks)]

    def fetch(slot, action):
        buffer = lax.rem(slot, 2)
        for i in range(4):

            @pl.when(slot // 2 == i)
            def _():
                for k in range(chunks):
                    source = blocks[4 * k + i].at[lax.rem(slot, 2), :, pl.ds(0, wide)]
                    action(pltpu.make_async_copy(source, cot_buf.at[buffer, rows[k]], cot_sem.at[buffer, k]))

    hidden_copies, first = [], 0
    for k, ref in enumerate(hidden):
        to = hidden_buf.at[:, pl.ds(first, ref.shape[1])]
        hidden_copies.append(pltpu.make_async_copy(ref, to, hidden_sem.at[k]))
        first += ref.shape[1]

    @pl.when(j == 0)
    def _():
        start_all(hidden_copies)
        fetch(j, lambda c: c.start())

    @pl.when(j + 1 < pl.num_programs(0))
    def _():
        fetch(j + 1, lambda c: c.start())

    @pl.when(j == 0)
    def _():
        wait_all(hidden_copies)

    fetch(j, lambda c: c.wait())
    out_ref[...] = jnp.dot(hidden_buf[...], cot_buf[lax.rem(j, 2)], preferred_element_type=F32)


def grad_out_of(place, hidden, cot_blocks, wide):
    chunks = len(cot_blocks)
    units, samples = hidden[0].shape[0], cot_blocks[0][0].shape[1]
    flat = [array for blocks in cot_blocks for array in blocks]
    return pl.pallas_call(
        functools.partial(grad_out_kernel, chunks=chunks),
        out_shape=jax.ShapeDtypeStruct((units, 8 * wide), F32),
        grid_spec=pltpu.PrefetchScalarGridSpec(
            num_scalar_prefetch=1,
            grid=(8,),
            in_specs=[pl.BlockSpec(memory_space=pl.ANY)] * (4 * chunks + len(hidden)),
            out_specs=pl.BlockSpec((units, wide), lambda j, p: (0, p[j])),
            scratch_shapes=[
                pltpu.VMEM((units, chunks * samples), BF16),
                pltpu.VMEM((2, chunks * samples, wide), BF16),
                pltpu.SemaphoreType.DMA((chunks,)),
                pltpu.SemaphoreType.DMA((2, chunks)),
            ],
        ),
        compiler_params=params(VMEM_MIB),
        cost_estimate=cost(
            2 * units * chunks * samples * 8 * wide,
            2 * chunks * samples * (8 * wide + units) + 4 * units * 8 * wide,
            0,
        ),
        name="grad_out",
    )(place, *flat, *hidden)


def plane_perms():
    first, second = [], []
    for t in range(4):
        for y in range(2):
            along_x, along_y = (t ^ 2) * 2 + y, t * 2 + (y ^ 1)
            first.append((t * 2 + y, along_x if t % 2 == 0 else along_y))
            second.append((t * 2 + y, along_y if t % 2 == 0 else along_x))
    return first, second


PERM_A, PERM_B = plane_perms()


def move_a(v):
    return lax.ppermute(v, PLANE, PERM_A)


def move_b(v):
    return lax.ppermute(v, PLANE, PERM_B)


def swap(v):
    return lax.ppermute(v, "table", [(t, t ^ 1) for t in range(4)])


def move_z(v, k):
    return lax.ppermute(v, "dp", [(z, z ^ k) for z in range(4)])


def plane_blocks():
    t, y = lax.axis_index("table"), lax.axis_index("tensor")
    x, core = t // 2, t % 2
    blocks = []
    for dc in range(2):
        c = core ^ dc
        a_x, a_y = jnp.where(c == 0, 1, 0), jnp.where(c == 0, 0, 1)
        for dx, dy in ((0, 0), (a_x, a_y), (a_y, a_x), (1, 1)):
            blocks.append(((x ^ dx) * 2 + c) * 2 + (y ^ dy))
    return jnp.stack(blocks).astype(jnp.int32)


def after(v, *earlier):
    return lax.optimization_barrier((v,) + earlier)[0]


def spread_shards(lookup_ids, bag_lengths, feature_widths, tables, w_in, w_out, cotangent):
    z = lax.axis_index("dp")
    wide = cotangent.shape[1]
    units = w_in.shape[1] // 4
    blocks = plane_blocks()
    place = jnp.concatenate([blocks, z[None].astype(jnp.int32)])

    def backward(cot, feat, firsts, running, *earlier):
        return chunk_backward(after(place, *earlier), cot, feat, firsts, w_out, w_in, running, units, wide)

    s0 = cotangent
    a0, s1, s2 = move_a(s0), move_z(s0, 1), move_z(s0, 2)
    pooled = pool_local(lookup_ids, bag_lengths, feature_widths, tables[0])
    pair0 = jnp.stack([s0, after(a0, pooled)])
    both0 = move_b(pair0)
    pa, pooled1 = move_a(pooled), move_z(pooled, 1)
    pa, pooled1, s1 = lax.optimization_barrier((pa, pooled1, s1))

    feat_pair = jnp.stack([pooled, pa])
    e1 = carry(s1, pooled1, 4)
    feat_pair, e1 = lax.optimization_barrier((feat_pair, e1))
    a1, feat_both, pooled2 = move_a(e1), move_b(feat_pair), move_z(after(pooled, e1), 2)
    s2, pooled2, both0 = lax.optimization_barrier((s2, pooled2, both0))
    e2 = carry(s2, pooled2, 6)
    feat0 = jnp.concatenate([feat_pair, after(feat_both, e2)])
    feat0_ = swap(feat0)
    pair1 = jnp.stack([e1, after(a1, feat0)])
    pair0_, both0_ = swap(after(pair0, pair1)), swap(after(both0, pair1))
    both1, pair1_ = move_b(pair1), swap(pair1)
    a2, e3 = move_a(after(e2, pair1)), move_z(e2, 1)
    away, near = forward(after(place, pair1, pair0_, both0_), [feat0, feat0_], w_in, w_out, wide)

    pair2 = jnp.stack([e2, after(a2, near, e3)])
    both1, e3 = after(both1, pair2), after(e3, pair2)
    both2, a3, both1_, pair2_ = move_b(pair2), move_a(e3), swap(both1), swap(pair2)
    cot0 = [pair0, both0, pair0_, both0_]
    cot1 = [pair1, both1, pair1_, both1_]
    hidden01, running = backward([cot0, cot1], [[feat0, feat0_], cot1], [0, wide], None, e3, pair2_)

    pair3 = jnp.stack([e3, after(a3, running)])
    both2 = after(both2, pair3)
    both3, both2_, pair3_, got = move_b(pair3), swap(both2), swap(pair3), swap(after(away, pair3))
    near = near + got.astype(F32)
    cot2 = [pair2, both2, pair2_, both2_]
    hidden2, running = backward([cot2], [cot2], [wide], running, near, pair3_)
    both3 = after(both3, running)
    both3_ = swap(both3)
    moved = move_b(after(near, running)[2:].astype(BF16))
    cot3 = [pair3, both3, pair3_, both3_]
    hidden3, running = backward([cot3], [cot3], [wide], running)

    rows = w_in.shape[0] // 4
    parts = [lax.dynamic_slice_in_dim(running, (z ^ k) * rows, rows, 0) for k in range(4)]
    sent = [parts[k].astype(BF16) for k in (1, 2, 3)]
    moved_parts = [move_z(sent[k - 1], k) for k in (1, 2, 3)]
    moved = after(moved, running, *sent).astype(F32)
    first = (near[1] + moved[1]).astype(BF16)
    last = move_a(first)
    grad_out = grad_out_of(after(blocks, first), [hidden01, hidden2, hidden3], [cot0, cot1, cot2, cot3], wide)
    last, *moved_parts = lax.optimization_barrier((last, *moved_parts, grad_out))[:4]
    grad_in = jnp.zeros((rows, 4 * units), F32)
    for k, part in enumerate(parts[:1] + moved_parts):
        grad_in = lax.dynamic_update_slice_in_dim(grad_in, part.astype(F32), (z ^ k) * units, 1)
    mixed_out = (near[0] + moved[0] + last.astype(F32)).astype(BF16)
    return (mixed_out, grad_in, grad_out)


def summed_shards(lookup_ids, bag_lengths, feature_widths, tables, w_in, w_out, cotangent):
    pooled = pool_local(lookup_ids, bag_lengths, feature_widths, tables[0])
    features = lax.all_gather(pooled, PLANE, axis=1, tiled=True)
    preact = jnp.dot(features, w_in, preferred_element_type=F32)
    hidden = jax.nn.silu(preact).astype(BF16)
    partial_out = jnp.dot(hidden, w_out, preferred_element_type=F32)
    reduced = lax.psum_scatter(partial_out, PLANE, scatter_dimension=1, tiled=True)
    mixed_out = reduced.astype(BF16)
    whole_grad = lax.all_gather(cotangent, PLANE, axis=1, tiled=True)
    grad_hidden = lax.dot_general(whole_grad, w_out, COLS_NT, preferred_element_type=F32)
    grad_preact = (grad_hidden * silu_slope(preact)).astype(BF16)
    term_in = lax.dot_general(features, grad_preact, ROWS_TN, preferred_element_type=F32)
    term_out = lax.dot_general(hidden, whole_grad, ROWS_TN, preferred_element_type=F32)
    grad_in = lax.psum_scatter(term_in, "dp", scatter_dimension=0, tiled=True)
    grad_out = lax.psum_scatter(term_out, "dp", scatter_dimension=0, tiled=True)
    return (mixed_out, grad_in, grad_out)


def solution(mesh):
    sizes = (mesh.shape["table"], mesh.shape["tensor"], mesh.shape["dp"])
    return jax.shard_map(
        spread_shards if sizes == (4, 2, 4) else summed_shards,
        mesh=mesh,
        in_specs=(
            P("dp", "table", None),
            P("dp", "table"),
            P(),
            P("table", None, "tensor"),
            P(None, PLANE),
            P(PLANE, None),
            P("dp", PLANE),
        ),
        out_specs=(
            P("dp", PLANE),
            P("dp", PLANE),
            P(("table", "tensor", "dp"), None),
        ),
        check_vma=False,
    )
```

time: 175 us -> 165 us (0.943)
  Pallas kernels: 91 us -> 73.4 us
  waiting for transfers between devices: 24.4 us -> 38.8 us
  other arithmetic: 16.3 us -> 9.91 us
    pallas_call x7 -> x6, Pallas kernels: 68.4 us -> 53 us  [the longest x3 32.4 us: chunk_backward(): pl.pallas_call(functools.partial(chunk_kernel, wide=wide, firsts=firsts,...]
    ppermute x8, waiting for transfers between devices: 11 us -> 22.5 us  [move_z(): return lax.ppermute(v, 'dp', [(z, z ^ k) for z in range(4)])]
    ppermute x6, waiting for transfers between devices: 9.67 us -> 1.13 us  [move_a(): return lax.ppermute(v, PLANE, PERM_A)]
    ppermute x6, waiting for transfers between devices: 2.86 us -> 10.2 us  [move_b(): return lax.ppermute(v, PLANE, PERM_B)]
    unnamed x34 -> x47, local copies, waits for them, and re-layouts: 4.31 us -> 9.31 us
    ppermute x11 -> x10, waiting for transfers between devices: 0.85 us -> 4.95 us  [swap(): return lax.ppermute(v, 'table', [(t, t ^ 1) for t in range(4)])]
    dynamic_update_slice x3, other arithmetic: 3.01 us -> 0.16 us  [spread_shards(): lax.dynamic_update_slice_in_dim(grad_in, part.astype(F32), (z ^ k) * unit...]
    ppermute x8, starting transfers between devices: 9.79 us -> 12 us  [move_z(): return lax.ppermute(v, 'dp', [(z, z ^ k) for z in range(4)])]
  transfers between devices with their start and end apart: 31 -> 30, of which waited for: 8 -> 11; matrix products, arithmetic and copies ran while one was open for 14% -> 7% of each run, Pallas kernels for 52% -> 45%
where the time goes in v3:
time: 165 us; the launch traced here: 164 us
  Pallas kernels  73.4 us (44%)
  waiting for transfers between devices  38.8 us (24%)
  starting transfers between devices  27.2 us (16%)
  local copies, waits for them, and re-layouts  13.7 us (8%)
  other arithmetic  9.91 us (6%)
    pallas_call x3, Pallas kernels, chunk_backward(): pl.pallas_call(functools.partial(chunk_kernel, wide=wide, firsts=firsts,...  32.4 us
    ppermute x8, waiting for transfers between devices, move_z(): return lax.ppermute(v, 'dp', [(z, z ^ k) for z in range(4)])  22.5 us
    pallas_call x1, Pallas kernels, forward(): pl.pallas_call(forward_kernel, out_shape=(jax.ShapeDtypeStruct((4, sample...  16.3 us
    pallas_call x1, Pallas kernels, grad_out_of(): pl.pallas_call(functools.partial(grad_out_kernel, chunks=chunks), out_sha...  15.5 us
    ppermute x8, starting transfers between devices, move_z(): return lax.ppermute(v, 'dp', [(z, z ^ k) for z in range(4)])  12 us
    ppermute x6, waiting for transfers between devices, move_b(): return lax.ppermute(v, PLANE, PERM_B)  10.2 us
    unnamed x47, local copies, waits for them, and re-layouts  9.31 us
    ppermute x6, starting transfers between devices, move_b(): return lax.ppermute(v, PLANE, PERM_B)  8.06 us
  transfers between devices with their start and end apart: 30, of which 11 were waited for; matrix products, arithmetic and copies ran while one was open for 7% of the time, Pallas kernels for 45%

profile of v3, /device:TPU:0, one launch (start us, length us, event | category | flops | bytes accessed | tf_op | source)
XLA Modules:
  0.0 164.1 jit_solution(16902057657366293104)
XLA Ops:
  0.6 3.0 %collective-permute-start.7 = (bf16[512,512]{1,0:T(8,128)(2,1)}, bf16[512,512]{1,0:T(8,128)(2,1)S(1)}, u32[]{:S(2)}, u32[]{:S(2)}) collective-permute-start(bf16[512,512]{1,0:T(8,128)(2,1)} %param.13), channel_id=1, source_target_pairs={{0,16},{4,20},{8,12},{12,8},{16,0},{20,4},{24,28},{28,24},{1,17},{... | collective-permute-start | bytes 1572872 | tf_op jit(solution)/shard_map/ppermute | solution.py:382
  3.6 1.6 collective-permute-start.2
  5.2 0.9 copy.12
  6.2 0.8 copy.13.len_ref
  7.1 1.2 copy-done.7
  8.3 0.7 copy-done.9
  9.0 4.8 %pool.1 = bf16[512,128]{1,0:T(8,128)(2,1)S(1)} custom-call(s32[32,256]{1,0:T(8,128)S(1)} %reshape.12.key_ref, s32[512,1]{1,0:T(8,128)S(1)} %copy.13.len_ref, s32[4]{0:T(128)S(1)} %copy-done.9, bf16[4096,128]{1,0:T(8,128)(2,1)S(1)} %bitcast.31), custom_call_target="tpu_custom_call" | custom-call | flops 5368709120 | bytes 1048576 | tf_op jit(solution)/shard_map/pool/pallas_call | solution.py:70
  13.8 1.1 pad_maximum_fusion.3.refs_0_
  15.0 1.6 collective-permute-start.8
  16.6 0.5 collective-permute-start.1
  17.0 0.5 collective-permute-start
  17.6 2.6 %collective-permute-start.5 = (bf16[512,512]{1,0:T(8,128)(2,1)}, bf16[512,512]{1,0:T(8,128)(2,1)}, u32[]{:S(2)}, u32[]{:S(2)}) collective-permute-start(bf16[512,512]{1,0:T(8,128)(2,1)} %param.13), channel_id=1, source_target_pairs={{0,2},{1,3},{2,0},{3,1},{4,6},{5,7},{6,4},{7,5},{8,10},{9,11},{10,... | collective-permute-start | bytes 1572872 | tf_op jit(solution)/shard_map/ppermute | solution.py:394
  20.1 3.6 %collective-permute-done.1.feat_ref = bf16[512,128]{1,0:T(8,128)(2,1)S(1)} collective-permute-done((bf16[512,128]{1,0:T(8,128)(2,1)S(1)}, bf16[512,128]{1,0:T(8,128)(2,1)S(1)}, u32[]{:S(2)}, u32[]{:S(2)}) %collective-permute-start.1) | collective-permute-done | bytes 131104 | tf_op jit(solution)/shard_map/ppermute | solution.py:394
  23.8 0.6 copy-done.20
  24.4 0.2 copy-done.19
  24.6 2.0 %carry.2 = bf16[512,640]{1,0:T(8,128)(2,1)} custom-call(bf16[512,512]{1,0:T(8,128)(2,1)} %copy-done.19, bf16[512,128]{1,0:T(8,128)(2,1)} %copy-done.20), custom_call_target="tpu_custom_call" | custom-call | flops 4000000000 | tf_op jit(solution)/shard_map/carry/pallas_call | solution.py:96
  26.5 2.2 %collective-permute-start.6 = (bf16[512,128]{1,0:T(8,128)(2,1)S(1)}, bf16[512,128]{1,0:T(8,128)(2,1)S(1)}, u32[]{:S(2)}, u32[]{:S(2)}) collective-permute-start(bf16[512,128]{1,0:T(8,128)(2,1)S(1)} %pool.1), channel_id=1, source_target_pairs={{0,2},{1,3},{2,0},{3,1},{4,6},{5,7},{6,4},{7,5},{8,10},{9,11},{10,... | collective-permute-start | bytes 393224 | tf_op jit(solution)/shard_map/ppermute | solution.py:394
  28.8 0.5 collective-permute-start.3
  29.3 0.5 collective-permute-start.4
  29.9 16.6 %collective-permute-done.5.block_ref = bf16[512,512]{1,0:T(8,128)(2,1)} collective-permute-done((bf16[512,512]{1,0:T(8,128)(2,1)}, bf16[512,512]{1,0:T(8,128)(2,1)}, u32[]{:S(2)}, u32[]{:S(2)}) %collective-permute-start.5) | collective-permute-done | bytes 524320 | tf_op jit(solution)/shard_map/ppermute | solution.py:394
  46.5 1.3 collective-permute-done.6.feat_ref
  47.8 0.7 copy-done.21
  48.4 2.3 %carry.3 = bf16[512,640]{1,0:T(8,128)(2,1)} custom-call(bf16[512,512]{1,0:T(8,128)(2,1)} %collective-permute-done.5.block_ref, bf16[512,128]{1,0:T(8,128)(2,1)} %copy-done.21), custom_call_target="tpu_custom_call" | custom-call | flops 6000000000 | tf_op jit(solution)/shard_map/carry/pallas_call | solution.py:96
  50.8 2.5 %pad_maximum_fusion.refs_4_.refs_10_ = bf16[2,512,640]{2,1,0:T(8,128)(2,1)} fusion(bf16[1,512,640]{2,1,0:T(8,128)(2,1)} %bitcast.15, bf16[1,512,640]{2,1,0:T(8,128)(2,1)} %bitcast.34), kind=kLoop, calls=%fused_computation.2 | loop fusion | flops 655360 | bytes 2621440 | tf_op jit(solution)/shard_map/stack | solution.py:439
  53.3 0.5 collective-permute-start.10
  53.8 1.6 collective-permute-start.16
  55.4 0.7 collective-permute-start.12
  56.2 2.9 %collective-permute-done.10.refs_3_ = bf16[2,512,512]{2,1,0:T(8,128)(2,1)} collective-permute-done((bf16[2,512,512]{2,1,0:T(8,128)(2,1)S(1)}, bf16[2,512,512]{2,1,0:T(8,128)(2,1)}, u32[]{:S(2)}, u32[]{:S(2)}) %collective-permute-start.10) | collective-permute-done | bytes 1048608 | tf_op jit(solution)/shard_map/ppermute | solution.py:390
  59.1 0.5 collective-permute-start.13
  59.6 16.3 %forward.1 = (bf16[4,512,512]{2,1,0:T(8,128)(2,1)S(1)}, f32[4,512,512]{2,1,0:T(8,128)}) custom-call(s32[9]{0:T(128)S(1)} %concatenate.7.place_ref, bf16[4,512,128]{2,1,0:T(8,128)(2,1)S(1)} %constant_dynamic-update-slice_fusion.feat_ref.refs_8_, bf16[4,512,128]{2,1,0:T(8,128)(2,1)S(1)} %collective-permute-done.11.other_feat_ref.refs_9_, ...), custom_call_target="tpu_custom_call" | custom-call | flops 10737418240 | bytes 20971520 | tf_op jit(solution)/shard_map/forward/pallas_call | solution.py:175
  75.8 1.1 collective-permute-done.13
  77.2 1.6 collective-permute-done.16.refs_5_.refs_11_
  78.7 0.5 collective-permute-start.14
  79.2 1.6 collective-permute-start.21
  80.9 1.4 collective-permute-done.18.refs_7_.refs_13_
  82.3 1.1 copy-done.14
  83.4 13.3 %chunk_backward.3 = (bf16[512,1024]{1,0:T(8,128)(2,1)S(1)}, f32[1024,512]{1,0:T(8,128)}) custom-call(s32[9]{0:T(128)S(1)} %concatenate.7.place_ref, bf16[2,512,512]{2,1,0:T(8,128)(2,1)S(1)} %pad_maximum_fusion.3.refs_0_, bf16[2,512,512]{2,1,0:T(8,128)(2,1)} %copy-done.5, bf16[2,512,512]{2,1,0:T(8,128)(2,1)} %collective-permute-done.9.refs_2_, ...), custom_call_target="tpu_custom_call" | custom-call | flops 6442450944 | bytes 19922944 | tf_op jit(solution)/shard_map/chunk_backward/pallas_call | solution.py:270
  96.9 0.2 collective-permute-start.19
  97.1 0.4 collective-permute-start.20
  97.5 5.4 %collective-permute-done.21.refs_1_.refs_5_.refs_9_ = bf16[2,512,640]{2,1,0:T(8,128)(2,1)S(1)} collective-permute-done((bf16[2,512,640]{2,1,0:T(8,128)(2,1)S(1)}, bf16[2,512,640]{2,1,0:T(8,128)(2,1)S(1)}, u32[]{:S(2)}, u32[]{:S(2)}) %collective-permute-start.21) | collective-permute-done | bytes 1310752 | tf_op jit(solution)/shard_map/ppermute | solution.py:386
  102.9 0.3 collective-permute-start.22
  103.2 1.4 collective-permute-start.24
  104.6 3.0 %convert_add_fusion = f32[4,512,512]{2,1,0:T(8,128)S(1)} fusion(f32[4,512,512]{2,1,0:T(8,128)} %get-tuple-element.58, bf16[4,512,512]{2,1,0:T(8,128)(2,1)S(1)} %collective-permute-done.19), kind=kLoop, calls=%fused_computation | loop fusion | flops 2097152 | bytes 10485760 | tf_op jit(solution)/shard_map/add | solution.py:455
  107.7 10.0 %chunk_backward.4 = (bf16[512,512]{1,0:T(8,128)(2,1)S(1)}, f32[1024,512]{1,0:T(8,128)}) custom-call(s32[9]{0:T(128)S(1)} %concatenate.7.place_ref, bf16[2,512,640]{2,1,0:T(8,128)(2,1)S(1)} %pad_maximum_fusion.1.refs_0_.refs_4_.refs_8_, bf16[2,512,640]{2,1,0:T(8,128)(2,1)S(1)} %collective-permute-done.21.refs_1_.refs_5_.refs_9_, ...), custom_call_target="tpu_custom_call" | custom-call | flops 3221225472 | bytes 14680064 | tf_op jit(solution)/shard_map/chunk_backward/pallas_call | solution.py:270
  117.6 3.3 %collective-permute-done.24.refs_1_.refs_5_.refs_13_ = bf16[2,512,640]{2,1,0:T(8,128)(2,1)} collective-permute-done((bf16[2,512,640]{2,1,0:T(8,128)(2,1)S(1)}, bf16[2,512,640]{2,1,0:T(8,128)(2,1)}, u32[]{:S(2)}, u32[]{:S(2)}) %collective-permute-start.24) | collective-permute-done | bytes 1310752 | tf_op jit(solution)/shard_map/ppermute | solution.py:386
  120.9 1.1 slice.43
  122.0 1.4 collective-permute-start.23
  123.5 0.6 collective-permute-done.25.refs_3_.refs_7_.refs_15_
  124.2 1.1 copy-done.16
  125.2 9.2 %chunk_backward.5 = (bf16[512,512]{1,0:T(8,128)(2,1)S(1)}, f32[1024,512]{1,0:T(8,128)}) custom-call(s32[9]{0:T(128)S(1)} %concatenate.7.place_ref, bf16[2,512,640]{2,1,0:T(8,128)(2,1)S(1)} %pad_maximum_fusion.2.refs_0_.refs_4_.refs_12_, bf16[2,512,640]{2,1,0:T(8,128)(2,1)} %collective-permute-done.24.refs_1_.refs_5_.refs_13_, ...), custom_call_target="tpu_custom_call" | custom-call | flops 3221225472 | bytes 14680064 | tf_op jit(solution)/shard_map/chunk_backward/pallas_call | solution.py:270
  134.4 1.6 dynamic-slice_convert_fusion
  136.1 3.6 %collective-permute-start.29 = (bf16[256,512]{1,0:T(8,128)(2,1)S(1)}, bf16[256,512]{1,0:T(8,128)(2,1)S(1)}, u32[]{:S(2)}, u32[]{:S(2)}) collective-permute-start(bf16[256,512]{1,0:T(8,128)(2,1)S(1)} %get-tuple-element.83), channel_id=1, source_target_pairs={{0,3},{1,2},{2,1},{3,0},{4,7},{5,6},{6,5},{7,4},{8,11},{9,10},{10,... | collective-permute-start | bytes 786440 | tf_op jit(solution)/shard_map/ppermute | solution.py:394
  139.6 0.9 collective-permute-start.27
  140.5 1.5 convert_element_type.41
  142.0 0.3 fusion.4
  142.3 0.6 collective-permute-start.26
  142.9 0.4 copy-done.4
  143.2 0.3 copy-done.6
  143.6 15.5 %grad_out.1 = f32[512,4096]{1,0:T(8,128)} custom-call(s32[8]{0:T(128)S(1)} %stack.95.place_ref, bf16[2,512,512]{2,1,0:T(8,128)(2,1)S(1)} %copy-done.4, bf16[2,512,512]{2,1,0:T(8,128)(2,1)S(1)} %copy-done.6, bf16[2,512,512]{2,1,0:T(8,128)(2,1)} %collective-permute-done.9.refs_2_, bf16[2,512,512]{2,1,0:T(8,128)(2,1)} %collective-permute-done.10.refs_3_, ...), custom_call_target="tpu_custom_call" | custom-call | flops 8589934592 | bytes 27262976 | tf_op jit(solution)/shard_map/grad_out/pallas_call | solution.py:343
  159.1 0.2 broadcast_in_dim.7
  159.4 1.1 dynamic-slice_dynamic-update-slice_fusion
  160.5 1.0 collective-permute-done.28
  161.5 1.1 fusion.3
  162.8 1.3 copy-done.17
  (71 shorter events, 1.1 us)
Async XLA Ops:
  0.6 13.2 %collective-permute-start.7 = (bf16[512,512]{1,0:T(8,128)(2,1)}, bf16[512,512]{1,0:T(8,128)(2,1)S(1)}, u32[]{:S(2)}, u32[]{:S(2)}) collective-permute-start(bf16[512,512]{1,0:T(8,128)(2,1)} %param.13), channel_id=1, source_target_pairs={{0,16},{4,20},{8,12},{12,8},{16,0},{20,4},{24,28},{28,24},{1,17},{... | collective-permute-start | bytes 1572872 | tf_op jit(solution)/shard_map/ppermute | solution.py:382
  3.6 20.1 %collective-permute-start.2 = (bf16[512,512]{1,0:T(8,128)(2,1)}, bf16[512,512]{1,0:T(8,128)(2,1)S(1)}, u32[]{:S(2)}, u32[]{:S(2)}) collective-permute-start(bf16[512,512]{1,0:T(8,128)(2,1)} %param.13), channel_id=1, source_target_pairs={{0,1},{1,0},{2,3},{3,2},{4,5},{5,4},{6,7},{7,6},{8,9},{9,8},{10,11... | collective-permute-start | bytes 1572872 | tf_op jit(solution)/shard_map/ppermute | solution.py:394
  7.1 1.2 copy-start.7
  8.3 0.7 copy-start.9
  15.0 67.3 %copy-start.3 = (bf16[2,512,512]{2,1,0:T(8,128)(2,1)}, bf16[2,512,512]{2,1,0:T(8,128)(2,1)S(1)}, u32[]{:S(2)}) copy-start(bf16[2,512,512]{2,1,0:T(8,128)(2,1)S(1)} %pad_maximum_fusion.3.refs_0_) | copy-start | bytes 3145732
  15.0 32.8 %collective-permute-start.8 = (bf16[2,512,512]{2,1,0:T(8,128)(2,1)S(1)}, bf16[2,512,512]{2,1,0:T(8,128)(2,1)S(1)}, u32[]{:S(2)}, u32[]{:S(2)}) collective-permute-start(bf16[2,512,512]{2,1,0:T(8,128)(2,1)S(1)} %pad_maximum_fusion.3.refs_0_), channel_id=1, source_target_pairs={{0,4},{4,0},{8,24},{12,28},{16,20},{20,16},{24,8},{28,12},{1,5},{5... | collective-permute-start | bytes 3145736 | tf_op jit(solution)/shard_map/ppermute | solution.py:386
  16.6 7.2 %collective-permute-start.1 = (bf16[512,128]{1,0:T(8,128)(2,1)S(1)}, bf16[512,128]{1,0:T(8,128)(2,1)S(1)}, u32[]{:S(2)}, u32[]{:S(2)}) collective-permute-start(bf16[512,128]{1,0:T(8,128)(2,1)S(1)} %pool.1), channel_id=1, source_target_pairs={{0,1},{1,0},{2,3},{3,2},{4,5},{5,4},{6,7},{7,6},{8,9},{9,8},{10,11... | collective-permute-start | bytes 393224 | tf_op jit(solution)/shard_map/ppermute | solution.py:394
  17.0 6.7 %collective-permute-start = (bf16[512,128]{1,0:T(8,128)(2,1)S(1)}, bf16[512,128]{1,0:T(8,128)(2,1)S(1)}, u32[]{:S(2)}, u32[]{:S(2)}) collective-permute-start(bf16[512,128]{1,0:T(8,128)(2,1)S(1)} %pool.1), channel_id=1, source_target_pairs={{0,16},{4,20},{8,12},{12,8},{16,0},{20,4},{24,28},{28,24},{1,17},{... | collective-permute-start | bytes 393224 | tf_op jit(solution)/shard_map/ppermute | solution.py:382
  17.6 28.9 %collective-permute-start.5 = (bf16[512,512]{1,0:T(8,128)(2,1)}, bf16[512,512]{1,0:T(8,128)(2,1)}, u32[]{:S(2)}, u32[]{:S(2)}) collective-permute-start(bf16[512,512]{1,0:T(8,128)(2,1)} %param.13), channel_id=1, source_target_pairs={{0,2},{1,3},{2,0},{3,1},{4,6},{5,7},{6,4},{7,5},{8,10},{9,11},{10,... | collective-permute-start | bytes 1572872 | tf_op jit(solution)/shard_map/ppermute | solution.py:394
  23.8 0.7 copy-start.20
  23.8 0.8 copy-start.19
  26.5 21.2 %collective-permute-start.6 = (bf16[512,128]{1,0:T(8,128)(2,1)S(1)}, bf16[512,128]{1,0:T(8,128)(2,1)S(1)}, u32[]{:S(2)}, u32[]{:S(2)}) collective-permute-start(bf16[512,128]{1,0:T(8,128)(2,1)S(1)} %pool.1), channel_id=1, source_target_pairs={{0,2},{1,3},{2,0},{3,1},{4,6},{5,7},{6,4},{7,5},{8,10},{9,11},{10,... | collective-permute-start | bytes 393224 | tf_op jit(solution)/shard_map/ppermute | solution.py:394
  28.8 22.0 %collective-permute-start.3 = (bf16[512,640]{1,0:T(8,128)(2,1)}, bf16[512,640]{1,0:T(8,128)(2,1)}, u32[]{:S(2)}, u32[]{:S(2)}) collective-permute-start(bf16[512,640]{1,0:T(8,128)(2,1)} %carry.2), channel_id=1, source_target_pairs={{0,16},{4,20},{8,12},{12,8},{16,0},{20,4},{24,28},{28,24},{1,17},{... | collective-permute-start | bytes 1966088 | tf_op jit(solution)/shard_map/ppermute | solution.py:382
  29.3 21.4 %collective-permute-start.4 = (bf16[2,512,128]{2,1,0:T(8,128)(2,1)S(1)}, bf16[2,512,128]{2,1,0:T(8,128)(2,1)S(1)}, u32[]{:S(2)}, u32[]{:S(2)}) collective-permute-start(bf16[2,512,128]{2,1,0:T(8,128)(2,1)S(1)} %pad_maximum_fusion.4), channel_id=1, source_target_pairs={{0,4},{4,0},{8,24},{12,28},{16,20},{20,16},{24,8},{28,12},{1,5},{5... | collective-permute-start | bytes 786440 | tf_op jit(solution)/shard_map/ppermute | solution.py:386
  47.8 0.7 copy-start.21
  48.4 4.9 %copy-start.5 = (bf16[2,512,512]{2,1,0:T(8,128)(2,1)}, bf16[2,512,512]{2,1,0:T(8,128)(2,1)S(1)}, u32[]{:S(2)}) copy-start(bf16[2,512,512]{2,1,0:T(8,128)(2,1)S(1)} %collective-permute-done.8.refs_1_) | copy-start | bytes 3145732
  53.3 2.9 %collective-permute-start.9 = (bf16[2,512,512]{2,1,0:T(8,128)(2,1)S(1)}, bf16[2,512,512]{2,1,0:T(8,128)(2,1)}, u32[]{:S(2)}, u32[]{:S(2)}) collective-permute-start(bf16[2,512,512]{2,1,0:T(8,128)(2,1)S(1)} %pad_maximum_fusion.3.refs_0_), channel_id=1, source_target_pairs={{0,8},{8,0},{16,24},{24,16},{1,9},{9,1},{17,25},{25,17},{2,10},{10... | collective-permute-start | bytes 3145736 | tf_op jit(solution)/shard_map/ppermute | solution.py:390
  53.3 5.8 %collective-permute-start.10 = (bf16[2,512,512]{2,1,0:T(8,128)(2,1)S(1)}, bf16[2,512,512]{2,1,0:T(8,128)(2,1)}, u32[]{:S(2)}, u32[]{:S(2)}) collective-permute-start(bf16[2,512,512]{2,1,0:T(8,128)(2,1)S(1)} %collective-permute-done.8.refs_1_), channel_id=1, source_target_pairs={{0,8},{8,0},{16,24},{24,16},{1,9},{9,1},{17,25},{25,17},{2,10},{10... | collective-permute-start | bytes 3145736 | tf_op jit(solution)/shard_map/ppermute | solution.py:390
  53.8 5.8 %collective-permute-start.11 = (bf16[4,512,128]{2,1,0:T(8,128)(2,1)S(1)}, bf16[4,512,128]{2,1,0:T(8,128)(2,1)S(1)}, u32[]{:S(2)}, u32[]{:S(2)}) collective-permute-start(bf16[4,512,128]{2,1,0:T(8,128)(2,1)S(1)} %constant_dynamic-update-slice_fusion.feat_ref.refs_8_), channel_id=1, source_target_pairs={{0,8},{8,0},{16,24},{24,16},{1,9},{9,1},{17,25},{25,17},{2,10},{10... | collective-permute-start | bytes 1572872 | tf_op jit(solution)/shard_map/ppermute | solution.py:390
  53.8 24.9 %collective-permute-start.16 = (bf16[2,512,640]{2,1,0:T(8,128)(2,1)}, bf16[2,512,640]{2,1,0:T(8,128)(2,1)}, u32[]{:S(2)}, u32[]{:S(2)}) collective-permute-start(bf16[2,512,640]{2,1,0:T(8,128)(2,1)} %pad_maximum_fusion.refs_4_.refs_10_), channel_id=1, source_target_pairs={{0,4},{4,0},{8,24},{12,28},{16,20},{20,16},{24,8},{28,12},{1,5},{5... | collective-permute-start | bytes 3932168 | tf_op jit(solution)/shard_map/ppermute | solution.py:386
  55.4 21.5 %copy-start.18 = (bf16[512,640]{1,0:T(8,128)(2,1)S(1)}, bf16[512,640]{1,0:T(8,128)(2,1)}, u32[]{:S(2)}) copy-start(bf16[512,640]{1,0:T(8,128)(2,1)} %carry.3) | copy-start | bytes 1966084
  55.4 21.5 %collective-permute-start.12 = (bf16[512,640]{1,0:T(8,128)(2,1)}, bf16[512,640]{1,0:T(8,128)(2,1)S(1)}, u32[]{:S(2)}, u32[]{:S(2)}) collective-permute-start(bf16[512,640]{1,0:T(8,128)(2,1)} %carry.3), channel_id=1, source_target_pairs={{0,1},{1,0},{2,3},{3,2},{4,5},{5,4},{6,7},{7,6},{8,9},{9,8},{10,11... | collective-permute-start | bytes 1966088 | tf_op jit(solution)/shard_map/ppermute | solution.py:394
  56.1 24.7 %collective-permute-start.17 = (bf16[2,512,640]{2,1,0:T(8,128)(2,1)}, bf16[2,512,640]{2,1,0:T(8,128)(2,1)S(1)}, u32[]{:S(2)}, u32[]{:S(2)}) collective-permute-start(bf16[2,512,640]{2,1,0:T(8,128)(2,1)} %pad_maximum_fusion.refs_4_.refs_10_), channel_id=1, source_target_pairs={{0,8},{8,0},{16,24},{24,16},{1,9},{9,1},{17,25},{25,17},{2,10},{10... | collective-permute-start | bytes 3932168 | tf_op jit(solution)/shard_map/ppermute | solution.py:390
  59.1 17.9 %collective-permute-start.13 = (bf16[512,640]{1,0:T(8,128)(2,1)}, bf16[512,640]{1,0:T(8,128)(2,1)S(1)}, u32[]{:S(2)}, u32[]{:S(2)}) collective-permute-start(bf16[512,640]{1,0:T(8,128)(2,1)} %carry.3), channel_id=1, source_target_pairs={{0,16},{4,20},{8,12},{12,8},{16,0},{20,4},{24,28},{28,24},{1,17},{... | collective-permute-start | bytes 1966088 | tf_op jit(solution)/shard_map/ppermute | solution.py:382
  77.1 30.5 %copy-start = (bf16[2,512,640]{2,1,0:T(8,128)(2,1)}, bf16[2,512,640]{2,1,0:T(8,128)(2,1)S(1)}, u32[]{:S(2)}) copy-start(bf16[2,512,640]{2,1,0:T(8,128)(2,1)S(1)} %pad_maximum_fusion.1.refs_0_.refs_4_.refs_8_) | copy-start | bytes 3932164
  77.1 3.7 %collective-permute-start.15 = (bf16[2,512,640]{2,1,0:T(8,128)(2,1)S(1)}, bf16[2,512,640]{2,1,0:T(8,128)(2,1)S(1)}, u32[]{:S(2)}, u32[]{:S(2)}) collective-permute-start(bf16[2,512,640]{2,1,0:T(8,128)(2,1)S(1)} %pad_maximum_fusion.1.refs_0_.refs_4_.refs_8_), channel_id=1, source_target_pairs={{0,8},{8,0},{16,24},{24,16},{1,9},{9,1},{17,25},{25,17},{2,10},{10... | collective-permute-start | bytes 3932168 | tf_op jit(solution)/shard_map/ppermute | solution.py:390
  78.7 3.6 %collective-permute-start.18 = (bf16[2,512,640]{2,1,0:T(8,128)(2,1)}, bf16[2,512,640]{2,1,0:T(8,128)(2,1)S(1)}, u32[]{:S(2)}, u32[]{:S(2)}) collective-permute-start(bf16[2,512,640]{2,1,0:T(8,128)(2,1)} %collective-permute-done.16.refs_5_.refs_11_), channel_id=1, source_target_pairs={{0,8},{8,0},{16,24},{24,16},{1,9},{9,1},{17,25},{25,17},{2,10},{10... | collective-permute-start | bytes 3932168 | tf_op jit(solution)/shard_map/ppermute | solution.py:390
  78.7 18.0 %collective-permute-start.14 = (bf16[512,640]{1,0:T(8,128)(2,1)S(1)}, bf16[512,640]{1,0:T(8,128)(2,1)S(1)}, u32[]{:S(2)}, u32[]{:S(2)}) collective-permute-start(bf16[512,640]{1,0:T(8,128)(2,1)S(1)} %collective-permute-done.12), channel_id=1, source_target_pairs={{0,16},{4,20},{8,12},{12,8},{16,0},{20,4},{24,28},{28,24},{1,17},{... | collective-permute-start | bytes 1966088 | tf_op jit(solution)/shard_map/ppermute | solution.py:382
  79.2 23.7 %collective-permute-start.21 = (bf16[2,512,640]{2,1,0:T(8,128)(2,1)S(1)}, bf16[2,512,640]{2,1,0:T(8,128)(2,1)S(1)}, u32[]{:S(2)}, u32[]{:S(2)}) collective-permute-start(bf16[2,512,640]{2,1,0:T(8,128)(2,1)S(1)} %pad_maximum_fusion.1.refs_0_.refs_4_.refs_8_), channel_id=1, source_target_pairs={{0,4},{4,0},{8,24},{12,28},{16,20},{20,16},{24,8},{28,12},{1,5},{5... | collective-permute-start | bytes 3932168 | tf_op jit(solution)/shard_map/ppermute | solution.py:386
  80.8 15.9 %copy-start.13 = (bf16[2,512,640]{2,1,0:T(8,128)(2,1)}, bf16[2,512,640]{2,1,0:T(8,128)(2,1)S(1)}, u32[]{:S(2)}) copy-start(bf16[2,512,640]{2,1,0:T(8,128)(2,1)S(1)} %collective-permute-done.15.refs_2_.refs_6_.refs_10_) | copy-start | bytes 3932164
  80.9 1.4 copy-start.12
  82.3 1.1 copy-start.14
  96.7 10.9 %copy-start.8 = (bf16[512,1024]{1,0:T(8,128)(2,1)}, bf16[512,1024]{1,0:T(8,128)(2,1)S(1)}, u32[]{:S(2)}) copy-start(bf16[512,1024]{1,0:T(8,128)(2,1)S(1)} %get-tuple-element.76.refs_16_) | copy-start | bytes 3145732
  96.9 27.3 %copy-start.1 = (bf16[2,512,640]{2,1,0:T(8,128)(2,1)}, bf16[2,512,640]{2,1,0:T(8,128)(2,1)S(1)}, u32[]{:S(2)}) copy-start(bf16[2,512,640]{2,1,0:T(8,128)(2,1)S(1)} %pad_maximum_fusion.2.refs_0_.refs_4_.refs_12_) | copy-start | bytes 3932164
  96.9 7.7 %collective-permute-start.19 = (bf16[4,512,512]{2,1,0:T(8,128)(2,1)S(1)}, bf16[4,512,512]{2,1,0:T(8,128)(2,1)S(1)}, u32[]{:S(2)}, u32[]{:S(2)}) collective-permute-start(bf16[4,512,512]{2,1,0:T(8,128)(2,1)S(1)} %get-tuple-element.67), channel_id=1, source_target_pairs={{0,8},{8,0},{16,24},{24,16},{1,9},{9,1},{17,25},{25,17},{2,10},{10... | collective-permute-start | bytes 6291464 | tf_op jit(solution)/shard_map/ppermute | solution.py:390
  97.1 10.5 %collective-permute-start.20 = (bf16[2,512,640]{2,1,0:T(8,128)(2,1)S(1)}, bf16[2,512,640]{2,1,0:T(8,128)(2,1)S(1)}, u32[]{:S(2)}, u32[]{:S(2)}) collective-permute-start(bf16[2,512,640]{2,1,0:T(8,128)(2,1)S(1)} %pad_maximum_fusion.2.refs_0_.refs_4_.refs_12_), channel_id=1, source_target_pairs={{0,8},{8,0},{16,24},{24,16},{1,9},{9,1},{17,25},{25,17},{2,10},{10... | collective-permute-start | bytes 3932168 | tf_op jit(solution)/shard_map/ppermute | solution.py:390
  102.9 4.7 %copy-start.2 = (bf16[2,512,640]{2,1,0:T(8,128)(2,1)}, bf16[2,512,640]{2,1,0:T(8,128)(2,1)S(1)}, u32[]{:S(2)}) copy-start(bf16[2,512,640]{2,1,0:T(8,128)(2,1)S(1)} %collective-permute-done.21.refs_1_.refs_5_.refs_9_) | copy-start | bytes 3932164
  102.9 4.7 %collective-permute-start.22 = (bf16[2,512,640]{2,1,0:T(8,128)(2,1)S(1)}, bf16[2,512,640]{2,1,0:T(8,128)(2,1)}, u32[]{:S(2)}, u32[]{:S(2)}) collective-permute-start(bf16[2,512,640]{2,1,0:T(8,128)(2,1)S(1)} %collective-permute-done.21.refs_1_.refs_5_.refs_9_), channel_id=1, source_target_pairs={{0,8},{8,0},{16,24},{24,16},{1,9},{9,1},{17,25},{25,17},{2,10},{10... | collective-permute-start | bytes 3932168 | tf_op jit(solution)/shard_map/ppermute | solution.py:390
  103.2 17.7 %collective-permute-start.24 = (bf16[2,512,640]{2,1,0:T(8,128)(2,1)S(1)}, bf16[2,512,640]{2,1,0:T(8,128)(2,1)}, u32[]{:S(2)}, u32[]{:S(2)}) collective-permute-start(bf16[2,512,640]{2,1,0:T(8,128)(2,1)S(1)} %pad_maximum_fusion.2.refs_0_.refs_4_.refs_12_), channel_id=1, source_target_pairs={{0,4},{4,0},{8,24},{12,28},{16,20},{20,16},{24,8},{28,12},{1,5},{5... | collective-permute-start | bytes 3932168 | tf_op jit(solution)/shard_map/ppermute | solution.py:386
  107.6 13.3 %copy-start.10 = (f32[4,512,512]{2,1,0:T(8,128)}, f32[4,512,512]{2,1,0:T(8,128)S(1)}, u32[]{:S(2)}) copy-start(f32[4,512,512]{2,1,0:T(8,128)S(1)} %convert_add_fusion) | copy-start | bytes 12582916
  107.6 10.0 %copy-start.15 = (bf16[2,512,640]{2,1,0:T(8,128)(2,1)}, bf16[2,512,640]{2,1,0:T(8,128)(2,1)S(1)}, u32[]{:S(2)}) copy-start(bf16[2,512,640]{2,1,0:T(8,128)(2,1)S(1)} %collective-permute-done.20.refs_2_.refs_6_.refs_14_) | copy-start | bytes 3932164
  120.9 3.2 %collective-permute-start.25 = (bf16[2,512,640]{2,1,0:T(8,128)(2,1)}, bf16[2,512,640]{2,1,0:T(8,128)(2,1)S(1)}, u32[]{:S(2)}, u32[]{:S(2)}) collective-permute-start(bf16[2,512,640]{2,1,0:T(8,128)(2,1)} %collective-permute-done.24.refs_1_.refs_5_.refs_13_), channel_id=1, source_target_pairs={{0,8},{8,0},{16,24},{24,16},{1,9},{9,1},{17,25},{25,17},{2,10},{10... | collective-permute-start | bytes 3932168 | tf_op jit(solution)/shard_map/ppermute | solution.py:390
  122.0 18.5 %collective-permute-start.23 = (bf16[2,512,512]{2,1,0:T(8,128)(2,1)}, bf16[2,512,512]{2,1,0:T(8,128)(2,1)}, u32[]{:S(2)}, u32[]{:S(2)}) collective-permute-start(bf16[2,512,512]{2,1,0:T(8,128)(2,1)} %slice.43), channel_id=1, source_target_pairs={{0,4},{4,0},{8,24},{12,28},{16,20},{20,16},{24,8},{28,12},{1,5},{5... | collective-permute-start | bytes 3145736 | tf_op jit(solution)/shard_map/ppermute | solution.py:386
  124.2 1.1 copy-start.16
  134.4 7.6 %copy-start.11 = (f32[4,512,512]{2,1,0:T(8,128)S(1)}, f32[4,512,512]{2,1,0:T(8,128)}, u32[]{:S(2)}) copy-start(f32[4,512,512]{2,1,0:T(8,128)} %copy-done.10) | copy-start | bytes 12582916
  136.1 24.4 %collective-permute-start.29 = (bf16[256,512]{1,0:T(8,128)(2,1)S(1)}, bf16[256,512]{1,0:T(8,128)(2,1)S(1)}, u32[]{:S(2)}, u32[]{:S(2)}) collective-permute-start(bf16[256,512]{1,0:T(8,128)(2,1)S(1)} %get-tuple-element.83), channel_id=1, source_target_pairs={{0,3},{1,2},{2,1},{3,0},{4,7},{5,6},{6,5},{7,4},{8,11},{9,10},{10,... | collective-permute-start | bytes 786440 | tf_op jit(solution)/shard_map/ppermute | solution.py:394
  139.6 21.8 %collective-permute-start.28 = (bf16[256,512]{1,0:T(8,128)(2,1)S(1)}, bf16[256,512]{1,0:T(8,128)(2,1)S(1)}, u32[]{:S(2)}, u32[]{:S(2)}) collective-permute-start(bf16[256,512]{1,0:T(8,128)(2,1)S(1)} %get-tuple-element.84), channel_id=1, source_target_pairs={{0,2},{1,3},{2,0},{3,1},{4,6},{5,7},{6,4},{7,5},{8,10},{9,11},{10,... | collective-permute-start | bytes 786440 | tf_op jit(solution)/shard_map/ppermute | solution.py:394
  139.6 21.8 %collective-permute-start.27 = (bf16[256,512]{1,0:T(8,128)(2,1)S(1)}, bf16[256,512]{1,0:T(8,128)(2,1)S(1)}, u32[]{:S(2)}, u32[]{:S(2)}) collective-permute-start(bf16[256,512]{1,0:T(8,128)(2,1)S(1)} %get-tuple-element.85), channel_id=1, source_target_pairs={{0,1},{1,0},{2,3},{3,2},{4,5},{5,4},{6,7},{7,6},{8,9},{9,8},{10,11... | collective-permute-start | bytes 786440 | tf_op jit(solution)/shard_map/ppermute | solution.py:394
  142.0 1.2 copy-start.4
  142.0 1.5 copy-start.6
  142.3 19.2 %collective-permute-start.26 = (bf16[512,512]{1,0:T(8,128)(2,1)S(1)}, bf16[512,512]{1,0:T(8,128)(2,1)S(1)}, u32[]{:S(2)}, u32[]{:S(2)}) collective-permute-start(bf16[512,512]{1,0:T(8,128)(2,1)S(1)} %fusion.4), channel_id=1, source_target_pairs={{0,16},{4,20},{8,12},{12,8},{16,0},{20,4},{24,28},{28,24},{1,17},{... | collective-permute-start | bytes 1572872 | tf_op jit(solution)/shard_map/ppermute | solution.py:382
  162.7 1.3 copy-start.17

commit v4 on v3

--- a/solution.py
+++ b/solution.py
@@ -201,7 +201,7 @@
     )(place, *feat_blocks, w_in, w_out)
 
 
-def chunk_kernel(place_ref, *refs, wide, firsts, feat_counts, add):
+def chunk_kernel(place_ref, *refs, wide, firsts, feat_counts, add, split):
     chunks = len(firsts)
     cot_refs, refs = [refs[4 * k : 4 * k + 4] for k in range(chunks)], refs[4 * chunks :]
     feat_refs = []
@@ -210,7 +210,9 @@
         refs = refs[n:]
     w_out_ref, w_in_ref, refs = refs[0], refs[1], refs[2:]
     sum_ref, refs = (refs[0], refs[1:]) if add else (None, refs)
-    hidden_ref, grad_in_ref, cot_buf, w_out_buf, feat_buf, w_in_buf, sum_buf, cot_sem, w_sem, feat_sem, sem = refs
+    hidden_ref, refs = refs[0], refs[1:]
+    (sent_ref, kept_ref), refs = (refs[:2], refs[2:]) if split else ((None, None), refs)
+    grad_in_ref, cot_buf, w_out_buf, feat_buf, w_in_buf, sum_buf, cot_sem, w_sem, feat_sem, sem = refs
     units = hidden_ref.shape[0]
     samples = cot_buf.shape[0] // chunks
     row = pl.ds(pl.multiple_of(place_ref[8] * units, units), units)
@@ -256,9 +258,18 @@
         sum_copy.wait()
         term += sum_buf[...]
     grad_in_ref[...] = term
-
-
-def chunk_backward(place, cot, feat, firsts, w_out, w_in, running, units, wide):
+    if split:
+        rows = kept_ref.shape[0]
+        for k in range(split):
+            other = lax.bitwise_xor(place_ref[8], k)
+            block = grad_in_ref[pl.ds(pl.multiple_of(other * rows, rows), rows), :]
+            if k == 0:
+                kept_ref[...] = block
+            else:
+                sent_ref[k - 1] = block.astype(BF16)
+
+
+def chunk_backward(place, cot, feat, firsts, w_out, w_in, running, units, wide, split):
     chunks = len(cot)
     samples = chunks * cot[0][0].shape[1]
     depth = w_in.shape[0]
@@ -266,16 +277,18 @@
     feat_counts = [len(f) for f in feat]
     operands = [v for c in cot for v in c] + [v for f in feat for v in f] + [w_out, w_in]
     operands += [running] if add else []
+    sums, held = [jax.ShapeDtypeStruct((depth, units), F32)], []
+    if split:
+        rows = depth // split
+        sums = [jax.ShapeDtypeStruct((split - 1, rows, units), BF16), jax.ShapeDtypeStruct((rows, units), F32)]
+        held = [pltpu.VMEM((depth, units), F32)]
     in_vmem = pl.BlockSpec(memory_space=pltpu.VMEM)
     return pl.pallas_call(
-        functools.partial(chunk_kernel, wide=wide, firsts=firsts, feat_counts=feat_counts, add=add),
-        out_shape=(
-            jax.ShapeDtypeStruct((units, samples), BF16),
-            jax.ShapeDtypeStruct((depth, units), F32),
-        ),
+        functools.partial(chunk_kernel, wide=wide, firsts=firsts, feat_counts=feat_counts, add=add, split=split),
+        out_shape=(jax.ShapeDtypeStruct((units, samples), BF16), *sums),
         in_specs=[pl.BlockSpec(memory_space=pltpu.SMEM)] + [pl.BlockSpec(memory_space=pl.ANY)] * len(operands),
-        out_specs=(in_vmem, in_vmem),
-        scratch_shapes=[
+        out_specs=(in_vmem,) * (1 + len(sums)),
+        scratch_shapes=held + [
             pltpu.VMEM((samples, 8 * wide), BF16),
             pltpu.VMEM((units, 8 * wide), BF16),
             pltpu.VMEM((samples, depth), BF16),
@@ -386,6 +399,10 @@
     return lax.ppermute(v, PLANE, PERM_B)
 
 
+def move_both(v):
+    return lax.ppermute(v, PLANE, [(t * 2 + y, (t ^ 2) * 2 + (y ^ 1)) for t in range(4) for y in range(2)])
+
+
 def swap(v):
     return lax.ppermute(v, "table", [(t, t ^ 1) for t in range(4)])
 
@@ -417,63 +434,56 @@
     blocks = plane_blocks()
     place = jnp.concatenate([blocks, z[None].astype(jnp.int32)])
 
-    def backward(cot, feat, firsts, running, *earlier):
-        return chunk_backward(after(place, *earlier), cot, feat, firsts, w_out, w_in, running, units, wide)
+    def backward(cot, feat, firsts, running, *earlier, split=0):
+        return chunk_backward(after(place, *earlier), cot, feat, firsts, w_out, w_in, running, units, wide, split)
 
     s0 = cotangent
-    a0, s1, s2 = move_a(s0), move_z(s0, 1), move_z(s0, 2)
+    a0, s2 = move_a(s0), move_z(s0, 2)
     pooled = pool_local(lookup_ids, bag_lengths, feature_widths, tables[0])
     pair0 = jnp.stack([s0, after(a0, pooled)])
-    both0 = move_b(pair0)
-    pa, pooled1 = move_a(pooled), move_z(pooled, 1)
-    pa, pooled1, s1 = lax.optimization_barrier((pa, pooled1, s1))
+    both0, pair1 = move_b(pair0), move_z(pair0, 1)
+    pa, pooled2 = move_a(pooled), move_z(pooled, 2)
+    pa, pooled2, s2 = lax.optimization_barrier((pa, pooled2, s2))
 
     feat_pair = jnp.stack([pooled, pa])
-    e1 = carry(s1, pooled1, 4)
-    feat_pair, e1 = lax.optimization_barrier((feat_pair, e1))
-    a1, feat_both, pooled2 = move_a(e1), move_b(feat_pair), move_z(after(pooled, e1), 2)
-    s2, pooled2, both0 = lax.optimization_barrier((s2, pooled2, both0))
-    e2 = carry(s2, pooled2, 6)
-    feat0 = jnp.concatenate([feat_pair, after(feat_both, e2)])
-    feat0_ = swap(feat0)
-    pair1 = jnp.stack([e1, after(a1, feat0)])
-    pair0_, both0_ = swap(after(pair0, pair1)), swap(after(both0, pair1))
-    both1, pair1_ = move_b(pair1), swap(pair1)
-    a2, e3 = move_a(after(e2, pair1)), move_z(e2, 1)
-    away, near = forward(after(place, pair1, pair0_, both0_), [feat0, feat0_], w_in, w_out, wide)
-
-    pair2 = jnp.stack([e2, after(a2, near, e3)])
-    both1, e3 = after(both1, pair2), after(e3, pair2)
-    both2, a3, both1_, pair2_ = move_b(pair2), move_a(e3), swap(both1), swap(pair2)
+    e2 = carry(s2, pooled2, 5)
+    feat_pair, e2 = lax.optimization_barrier((feat_pair, e2))
+    a2, feat_both, e3 = move_a(e2), move_b(feat_pair), move_z(e2, 1)
+    feat0 = jnp.concatenate([feat_pair, feat_both])
+    feat0_, both0_ = swap(feat0), swap(after(both0, feat0))
+    pair2 = jnp.stack([e2, after(a2, feat0, pair1)])
+    both2, feat1 = move_b(pair2), move_z(after(feat0, pair2), 1)
+    pair0_ = swap(after(pair0, pair2))
+    away, near = forward(after(place, pair2, both0_, pair0_), [feat0, feat0_], w_in, w_out, wide)
+
+    e3, both2 = lax.optimization_barrier((e3, after(both2, near)))
+    a3, both2_, pair2_ = move_a(e3), swap(both2), swap(after(pair2, e3))
+    both1 = move_b(after(pair1, e3))
     cot0 = [pair0, both0, pair0_, both0_]
+    cot2 = [pair2, both2, pair2_, both2_]
+    hidden02, running = backward([cot0, cot2], [[feat0, feat0_], cot2], [0, wide], None, e3)
+
+    pair3 = jnp.stack([e3, after(a3, running, both1, feat1)])
+    both3 = move_b(pair3)
+    both1 = after(both1, pair3)
+    feat1_, both1_, pair1_, got = swap(after(feat1, pair3)), swap(both1), swap(after(pair1, pair3)), swap(after(away, pair3))
+    sums = [near[k] + got[k].astype(F32) for k in range(4)]
+    leaving = [sums[k].astype(BF16) for k in (1, 2, 3)]
     cot1 = [pair1, both1, pair1_, both1_]
-    hidden01, running = backward([cot0, cot1], [[feat0, feat0_], cot1], [0, wide], None, e3, pair2_)
-
-    pair3 = jnp.stack([e3, after(a3, running)])
-    both2 = after(both2, pair3)
-    both3, both2_, pair3_, got = move_b(pair3), swap(both2), swap(pair3), swap(after(away, pair3))
-    near = near + got.astype(F32)
-    cot2 = [pair2, both2, pair2_, both2_]
-    hidden2, running = backward([cot2], [cot2], [wide], running, near, pair3_)
+    hidden1, running = backward([cot1], [[feat1, feat1_]], [0], running, *leaving)
     both3 = after(both3, running)
-    both3_ = swap(both3)
-    moved = move_b(after(near, running)[2:].astype(BF16))
+    both3_, pair3_ = swap(both3), swap(after(pair3, running))
+    arrived = [move_a(leaving[0]), move_b(leaving[1]), move_both(leaving[2])]
     cot3 = [pair3, both3, pair3_, both3_]
-    hidden3, running = backward([cot3], [cot3], [wide], running)
-
-    rows = w_in.shape[0] // 4
-    parts = [lax.dynamic_slice_in_dim(running, (z ^ k) * rows, rows, 0) for k in range(4)]
-    sent = [parts[k].astype(BF16) for k in (1, 2, 3)]
-    moved_parts = [move_z(sent[k - 1], k) for k in (1, 2, 3)]
-    moved = after(moved, running, *sent).astype(F32)
-    first = (near[1] + moved[1]).astype(BF16)
-    last = move_a(first)
-    grad_out = grad_out_of(after(blocks, first), [hidden01, hidden2, hidden3], [cot0, cot1, cot2, cot3], wide)
-    last, *moved_parts = lax.optimization_barrier((last, *moved_parts, grad_out))[:4]
-    grad_in = jnp.zeros((rows, 4 * units), F32)
-    for k, part in enumerate(parts[:1] + moved_parts):
+    hidden3, sent, kept = backward([cot3], [cot3], [wide], running, both3_, split=4)
+
+    moved_parts = [move_z(sent[k - 1], k) for k in (3, 2, 1)]
+    grad_out = grad_out_of(after(blocks, sent), [hidden02, hidden1, hidden3], [cot0, cot2, cot1, cot3], wide)
+    late = lax.optimization_barrier((*arrived, *moved_parts, grad_out))
+    grad_in = jnp.zeros((kept.shape[0], 4 * units), F32)
+    for k, part in enumerate((kept,) + late[3:6][::-1]):
         grad_in = lax.dynamic_update_slice_in_dim(grad_in, part.astype(F32), (z ^ k) * units, 1)
-    mixed_out = (near[0] + moved[0] + last.astype(F32)).astype(BF16)
+    mixed_out = (sums[0] + late[0].astype(F32) + late[1].astype(F32) + late[2].astype(F32)).astype(BF16)
     return (mixed_out, grad_in, grad_out)
 
 

time: 165 us -> 163 us (0.988)
  waiting for transfers between devices: 38.8 us -> 45.8 us
  local copies, waits for them, and re-layouts: 13.7 us -> 7.82 us
  Pallas kernels: 73.4 us -> 69.2 us
  starting transfers between devices: 27.2 us -> 29.1 us
    ppermute x10 -> x11, waiting for transfers between devices: 4.95 us -> 9.21 us  [swap(): return lax.ppermute(v, 'table', [(t, t ^ 1) for t in range(4)])]
    add x1 -> x0, other arithmetic: 2.98 us -> none  [spread_shards(): near = near + got.astype(F32)]
    ppermute x6 -> x5, waiting for transfers between devices: 1.13 us -> 3.79 us  [move_a(): return lax.ppermute(v, PLANE, PERM_A)]
    pallas_call x2 -> x1, Pallas kernels: 4.29 us -> 1.95 us  [carry(): pl.pallas_call(carry_kernel, out_shape=jax.ShapeDtypeStruct((samples, wid...]
    convert_element_type x3 -> x2, other arithmetic: 2.84 us -> 5.13 us  [the longest x1 3.31 us: spread_shards(): (sums[0] + late[0].astype(F32) + late[1].astype(F32) + late[2].astype(F32...]
    unnamed x47 -> x37, local copies, waits for them, and re-layouts: 9.31 us -> 7.14 us
    ppermute x8, starting transfers between devices: 12 us -> 9.94 us  [move_z(): return lax.ppermute(v, 'dp', [(z, z ^ k) for z in range(4)])]
    ppermute x6 -> x5, starting transfers between devices: 5.63 us -> 7.66 us  [move_a(): return lax.ppermute(v, PLANE, PERM_A)]
  transfers between devices with their start and end apart: 30 -> 31, of which waited for: 11 -> 14; matrix products, arithmetic and copies ran while one was open for 7% -> 4% of each run, Pallas kernels for 45% -> 43%
where the time goes in v4:
time: 163 us; the launch traced here: 162 us
  Pallas kernels  69.2 us (42%)
  waiting for transfers between devices  45.8 us (28%)
  starting transfers between devices  29.1 us (18%)
  other arithmetic  9.53 us (6%)
  local copies, waits for them, and re-layouts  7.82 us (5%)
    pallas_call x3, Pallas kernels, chunk_backward(): pl.pallas_call(functools.partial(chunk_kernel, wide=wide, firsts=firsts,...  30.6 us
    ppermute x8, waiting for transfers between devices, move_z(): return lax.ppermute(v, 'dp', [(z, z ^ k) for z in range(4)])  21.6 us
    pallas_call x1, Pallas kernels, forward(): pl.pallas_call(forward_kernel, out_shape=(jax.ShapeDtypeStruct((4, sample...  16.3 us
    pallas_call x1, Pallas kernels, grad_out_of(): pl.pallas_call(functools.partial(grad_out_kernel, chunks=chunks), out_sha...  15.6 us
    ppermute x6, waiting for transfers between devices, move_b(): return lax.ppermute(v, PLANE, PERM_B)  11.2 us
    ppermute x8, starting transfers between devices, move_z(): return lax.ppermute(v, 'dp', [(z, z ^ k) for z in range(4)])  9.94 us
    ppermute x11, waiting for transfers between devices, swap(): return lax.ppermute(v, 'table', [(t, t ^ 1) for t in range(4)])  9.21 us
    ppermute x6, starting transfers between devices, move_b(): return lax.ppermute(v, PLANE, PERM_B)  8.14 us
  transfers between devices with their start and end apart: 31, of which 14 were waited for; matrix products, arithmetic and copies ran while one was open for 4% of the time, Pallas kernels for 43%

profile of v4, /device:TPU:0, one launch (start us, length us, event | category | flops | bytes accessed | tf_op | source)
XLA Modules:
  0.0 162.4 jit_solution(15986480501930025654)
XLA Ops:
  0.6 3.0 %collective-permute-start.5 = (bf16[512,512]{1,0:T(8,128)(2,1)}, bf16[512,512]{1,0:T(8,128)(2,1)S(1)}, u32[]{:S(2)}, u32[]{:S(2)}) collective-permute-start(bf16[512,512]{1,0:T(8,128)(2,1)} %param.13), channel_id=1, source_target_pairs={{0,16},{4,20},{8,12},{12,8},{16,0},{20,4},{24,28},{28,24},{1,17},{... | collective-permute-start | bytes 1572872 | tf_op jit(solution)/shard_map/ppermute | solution.py:395
  3.6 2.6 %collective-permute-start.2 = (bf16[512,512]{1,0:T(8,128)(2,1)}, bf16[512,512]{1,0:T(8,128)(2,1)}, u32[]{:S(2)}, u32[]{:S(2)}) collective-permute-start(bf16[512,512]{1,0:T(8,128)(2,1)} %param.13), channel_id=1, source_target_pairs={{0,2},{1,3},{2,0},{3,1},{4,6},{5,7},{6,4},{7,5},{8,10},{9,11},{10,... | collective-permute-start | bytes 1572872 | tf_op jit(solution)/shard_map/ppermute | solution.py:411
  6.2 0.9 copy.12
  7.1 0.1 reshape.20.key_ref
  7.3 0.8 copy.13.len_ref
  8.1 1.2 copy-done.4
  9.3 0.7 copy-done.8
  10.0 4.8 %pool.1 = bf16[512,128]{1,0:T(8,128)(2,1)S(1)} custom-call(s32[32,256]{1,0:T(8,128)S(1)} %reshape.20.key_ref, s32[512,1]{1,0:T(8,128)S(1)} %copy.13.len_ref, s32[4]{0:T(128)S(1)} %copy-done.8, bf16[4096,128]{1,0:T(8,128)(2,1)S(1)} %bitcast.41), custom_call_target="tpu_custom_call" | custom-call | flops 5368709120 | bytes 1048576 | tf_op jit(solution)/shard_map/pool/pallas_call | solution.py:70
  14.8 0.6 collective-permute-start
  15.4 0.1 pad_maximum_fusion.2.refs_0_
  15.5 2.0 %collective-permute-start.6 = (bf16[2,512,512]{2,1,0:T(8,128)(2,1)S(1)}, bf16[2,512,512]{2,1,0:T(8,128)(2,1)}, u32[]{:S(2)}, u32[]{:S(2)}) collective-permute-start(bf16[2,512,512]{2,1,0:T(8,128)(2,1)S(1)} %pad_maximum_fusion.2.refs_0_), channel_id=1, source_target_pairs={{0,1},{1,0},{2,3},{3,2},{4,5},{5,4},{6,7},{7,6},{8,9},{9,8},{10,11... | collective-permute-start | bytes 3145736 | tf_op jit(solution)/shard_map/ppermute | solution.py:411
  17.5 1.5 collective-permute-start.7
  19.0 2.1 %collective-permute-done = bf16[512,128]{1,0:T(8,128)(2,1)S(1)} collective-permute-done((bf16[512,128]{1,0:T(8,128)(2,1)S(1)}, bf16[512,128]{1,0:T(8,128)(2,1)S(1)}, u32[]{:S(2)}, u32[]{:S(2)}) %collective-permute-start) | collective-permute-done | bytes 131104 | tf_op jit(solution)/shard_map/ppermute | solution.py:395
  21.2 13.9 %collective-permute-done.1.feat_ref = bf16[512,128]{1,0:T(8,128)(2,1)S(1)} collective-permute-done((bf16[512,128]{1,0:T(8,128)(2,1)S(1)}, bf16[512,128]{1,0:T(8,128)(2,1)S(1)}, u32[]{:S(2)}, u32[]{:S(2)}) %collective-permute-start.1) | collective-permute-done | bytes 131104 | tf_op jit(solution)/shard_map/ppermute | solution.py:411
  35.1 0.7 copy-done.16
  35.7 2.0 %carry.1 = bf16[512,640]{1,0:T(8,128)(2,1)} custom-call(bf16[512,512]{1,0:T(8,128)(2,1)} %collective-permute-done.2.block_ref, bf16[512,128]{1,0:T(8,128)(2,1)} %copy-done.16), custom_call_target="tpu_custom_call" | custom-call | flops 5000000000 | tf_op jit(solution)/shard_map/carry/pallas_call | solution.py:96
  37.7 1.6 collective-permute-start.3
  39.3 0.5 collective-permute-start.4
  39.8 8.7 %collective-permute-done.4 = bf16[2,512,128]{2,1,0:T(8,128)(2,1)S(1)} collective-permute-done((bf16[2,512,128]{2,1,0:T(8,128)(2,1)S(1)}, bf16[2,512,128]{2,1,0:T(8,128)(2,1)S(1)}, u32[]{:S(2)}, u32[]{:S(2)}) %collective-permute-start.4) | collective-permute-done | bytes 262176 | tf_op jit(solution)/shard_map/ppermute | solution.py:399
  48.6 1.4 collective-permute-done.3
  50.0 2.7 %collective-permute-done.6.refs_0_.refs_8_ = bf16[2,512,512]{2,1,0:T(8,128)(2,1)} collective-permute-done((bf16[2,512,512]{2,1,0:T(8,128)(2,1)S(1)}, bf16[2,512,512]{2,1,0:T(8,128)(2,1)}, u32[]{:S(2)}, u32[]{:S(2)}) %collective-permute-start.6) | collective-permute-done | bytes 1048608 | tf_op jit(solution)/shard_map/ppermute | solution.py:411
  52.7 2.3 %pad_maximum_fusion.refs_4_.refs_10_ = bf16[2,512,640]{2,1,0:T(8,128)(2,1)} fusion(bf16[1,512,640]{2,1,0:T(8,128)(2,1)S(1)} %bitcast.43, bf16[1,512,640]{2,1,0:T(8,128)(2,1)} %bitcast.42), kind=kLoop, calls=%fused_computation | loop fusion | flops 655360 | bytes 2621440 | tf_op jit(solution)/shard_map/stack | solution.py:454
  55.0 0.5 collective-permute-start.8
  55.5 0.1 collective-permute-start.10
  55.6 1.5 collective-permute-start.12
  57.1 0.1 concatenate.7.place_ref
  57.2 0.6 collective-permute-done.9.refs_2_
  57.8 2.2 %collective-permute-done.8.refs_3_ = bf16[2,512,512]{2,1,0:T(8,128)(2,1)} collective-permute-done((bf16[2,512,512]{2,1,0:T(8,128)(2,1)S(1)}, bf16[2,512,512]{2,1,0:T(8,128)(2,1)}, u32[]{:S(2)}, u32[]{:S(2)}) %collective-permute-start.8) | collective-permute-done | bytes 1048608 | tf_op jit(solution)/shard_map/ppermute | solution.py:407
  60.1 16.3 %forward.1 = (bf16[4,512,512]{2,1,0:T(8,128)(2,1)S(1)}, f32[4,512,512]{2,1,0:T(8,128)}) custom-call(s32[9]{0:T(128)S(1)} %concatenate.7.place_ref, bf16[4,512,128]{2,1,0:T(8,128)(2,1)S(1)} %constant_dynamic-update-slice_fusion.feat_ref.refs_8_, bf16[4,512,128]{2,1,0:T(8,128)(2,1)S(1)} %collective-permute-done.10.other_feat_ref.refs_9_, ...), custom_call_target="tpu_custom_call" | custom-call | flops 10737418240 | bytes 20971520 | tf_op jit(solution)/shard_map/forward/pallas_call | solution.py:175
  76.4 0.2 collective-permute-start.14
  76.6 0.4 collective-permute-start.15
  77.0 1.5 collective-permute-start.16
  78.5 1.5 collective-permute-start.13
  80.0 1.5 collective-permute-done.15.refs_7_.refs_13_
  81.6 1.0 copy-done.10
  82.6 13.6 %chunk_backward.3 = (bf16[512,1024]{1,0:T(8,128)(2,1)S(1)}, f32[1024,512]{1,0:T(8,128)}) custom-call(s32[9]{0:T(128)S(1)} %concatenate.7.place_ref, bf16[2,512,512]{2,1,0:T(8,128)(2,1)S(1)} %pad_maximum_fusion.2.refs_0_, bf16[2,512,512]{2,1,0:T(8,128)(2,1)} %copy-done.1, bf16[2,512,512]{2,1,0:T(8,128)(2,1)} %collective-permute-done.9.refs_2_, ...), custom_call_target="tpu_custom_call" | custom-call | flops 6442450944 | bytes 19922944 | tf_op jit(solution)/shard_map/chunk_backward/pallas_call | solution.py:286
  96.3 0.2 collective-permute-done.13
  96.5 2.5 %collective-permute-done.16.refs_1_.refs_9_ = bf16[2,512,512]{2,1,0:T(8,128)(2,1)S(1)} collective-permute-done((bf16[2,512,512]{2,1,0:T(8,128)(2,1)}, bf16[2,512,512]{2,1,0:T(8,128)(2,1)S(1)}, u32[]{:S(2)}, u32[]{:S(2)}) %collective-permute-start.16) | collective-permute-done | bytes 1048608 | tf_op jit(solution)/shard_map/ppermute | solution.py:399
  99.0 1.8 %pad_maximum_fusion.1.refs_0_.refs_4_.refs_12_ = bf16[2,512,640]{2,1,0:T(8,128)(2,1)S(1)} fusion(bf16[1,512,640]{2,1,0:T(8,128)(2,1)} %bitcast.17, bf16[1,512,640]{2,1,0:T(8,128)(2,1)} %bitcast.16), kind=kLoop, calls=%fused_computation.1 | loop fusion | flops 655360 | bytes 2621440 | tf_op jit(solution)/shard_map/stack | solution.py:466
  100.8 0.1 collective-permute-start.18
  100.9 0.5 collective-permute-start.24
  101.4 0.1 collective-permute-start.23
  101.5 1.5 collective-permute-start.22
  103.0 2.0 %collective-permute-done.18 = bf16[4,512,512]{2,1,0:T(8,128)(2,1)S(1)} collective-permute-done((bf16[4,512,512]{2,1,0:T(8,128)(2,1)S(1)}, bf16[4,512,512]{2,1,0:T(8,128)(2,1)S(1)}, u32[]{:S(2)}, u32[]{:S(2)}) %collective-permute-start.18) | collective-permute-done | bytes 2097184 | tf_op jit(solution)/shard_map/ppermute | solution.py:407
  105.0 1.8 %fusion.5 = (bf16[512,512]{1,0:T(8,128)(2,1)}, bf16[512,512]{1,0:T(8,128)(2,1)}, bf16[512,512]{1,0:T(8,128)(2,1)}) fusion(f32[4,512,512]{2,1,0:T(8,128)S(1)} %copy-done.11, bf16[4,512,512]{2,1,0:T(8,128)(2,1)S(1)} %collective-permute-done.18), kind=kLoop, calls=%fused_computation.12 | loop fusion | flops 2359296 | bytes 6291456 | tf_op jit(solution)/shard_map/convert_element_type | solution.py:471
  106.9 1.9 %collective-permute-done.25.refs_5_ = bf16[4,512,128]{2,1,0:T(8,128)(2,1)S(1)} collective-permute-done((bf16[4,512,128]{2,1,0:T(8,128)(2,1)S(1)}, bf16[4,512,128]{2,1,0:T(8,128)(2,1)S(1)}, u32[]{:S(2)}, u32[]{:S(2)}) %collective-permute-start.25) | collective-permute-done | bytes 524320 | tf_op jit(solution)/shard_map/ppermute | solution.py:407
  108.8 1.0 copy-done.14
  109.8 9.0 %chunk_backward.4 = (bf16[512,512]{1,0:T(8,128)(2,1)S(1)}, f32[1024,512]{1,0:T(8,128)}) custom-call(s32[9]{0:T(128)S(1)} %concatenate.7.place_ref, bf16[2,512,512]{2,1,0:T(8,128)(2,1)} %collective-permute-done.6.refs_0_.refs_8_, bf16[2,512,512]{2,1,0:T(8,128)(2,1)S(1)} %collective-permute-done.16.refs_1_.refs_9_, ...), custom_call_target="tpu_custom_call" | custom-call | flops 3221225472 | bytes 14680064 | tf_op jit(solution)/shard_map/chunk_backward/pallas_call | solution.py:286
  118.9 0.8 copy-done.6
  119.6 0.1 collective-permute-start.26
  119.8 0.4 collective-permute-start.27
  120.2 0.1 stack.83.place_ref
  120.2 1.0 collective-permute-start.19
  121.2 1.5 collective-permute-start.20
  122.8 1.0 collective-permute-start.21
  123.8 0.9 collective-permute-done.27.refs_2_.refs_6_.refs_14_
  124.7 8.0 %chunk_backward.5 = (bf16[512,512]{1,0:T(8,128)(2,1)S(1)}, bf16[3,256,512]{2,1,0:T(8,128)(2,1)S(1)}, f32[256,512]{1,0:T(8,128)S(1)}) custom-call(s32[9]{0:T(128)S(1)} %concatenate.7.place_ref, bf16[2,512,640]{2,1,0:T(8,128)(2,1)S(1)} %pad_maximum_fusion.1.refs_0_.refs_4_.refs_12_, bf16[2,512,640]{2,1,0:T(8,128)(2,1)} %collective-permute-done.22.refs_1_.refs_5_.refs_13_, ...), custom_call_target="tpu_custom_call" | custom-call | flops 3221225472 | bytes 14680064 | tf_op jit(solution)/shard_map/chunk_backward/pallas_call | solution.py:286
  132.7 4.7 %collective-permute-start.28 = (bf16[256,512]{1,0:T(8,128)(2,1)S(1)}, bf16[256,512]{1,0:T(8,128)(2,1)S(1)}, u32[]{:S(2)}, u32[]{:S(2)}) collective-permute-start(bf16[256,512]{1,0:T(8,128)(2,1)S(1)} %get-tuple-element.92), channel_id=1, source_target_pairs={{0,3},{1,2},{2,1},{3,0},{4,7},{5,6},{6,5},{7,4},{8,11},{9,10},{10,... | collective-permute-start | bytes 786440 | tf_op jit(solution)/shard_map/ppermute | solution.py:411
  137.5 0.6 collective-permute-start.30
  138.1 15.6 %grad_out.1 = f32[512,4096]{1,0:T(8,128)} custom-call(s32[8]{0:T(128)S(1)} %stack.83.place_ref, bf16[2,512,512]{2,1,0:T(8,128)(2,1)S(1)} %pad_maximum_fusion.2.refs_0_, bf16[2,512,512]{2,1,0:T(8,128)(2,1)S(1)} %copy-done.2, bf16[2,512,512]{2,1,0:T(8,128)(2,1)} %collective-permute-done.9.refs_2_, bf16[2,512,512]{2,1,0:T(8,128)(2,1)} %collective-permute-done.8.refs_3_, ...), custom_call_target="tpu_custom_call" | custom-call | flops 8589934592 | bytes 27262976 | tf_op jit(solution)/shard_map/grad_out/pallas_call | solution.py:356
  153.7 0.2 broadcast_in_dim.7
  154.0 4.9 %collective-permute-done.29 = bf16[256,512]{1,0:T(8,128)(2,1)S(1)} collective-permute-done((bf16[256,512]{1,0:T(8,128)(2,1)S(1)}, bf16[256,512]{1,0:T(8,128)(2,1)S(1)}, u32[]{:S(2)}, u32[]{:S(2)}) %collective-permute-start.29) | collective-permute-done | bytes 262176 | tf_op jit(solution)/shard_map/ppermute | solution.py:411
  159.0 0.1 convert_dynamic-update-slice_fusion
  159.1 3.3 %fusion.2 = bf16[512,512]{1,0:T(8,128)(2,1)} fusion(bf16[512,512]{1,0:T(8,128)(2,1)S(1)} %collective-permute-done.21, bf16[512,512]{1,0:T(8,128)(2,1)S(1)} %collective-permute-done.20, bf16[512,512]{1,0:T(8,128)(2,1)S(1)} %collective-permute-done.19, f32[4,512,512]{2,1,0:T(8,128)} %get-tuple-element.55, bf16[4,512,512]{2,1,0:T(8,128)(2,1)} %copy-done.13), kind=kLoop, calls=%fused_computation.6 | loop fusion | flops 2359296 | bytes 3670016 | tf_op jit(solution)/shard_map/convert_element_type | solution.py:486
  (58 shorter events, 0.4 us)
Async XLA Ops:
  0.6 14.8 %collective-permute-start.5 = (bf16[512,512]{1,0:T(8,128)(2,1)}, bf16[512,512]{1,0:T(8,128)(2,1)S(1)}, u32[]{:S(2)}, u32[]{:S(2)}) collective-permute-start(bf16[512,512]{1,0:T(8,128)(2,1)} %param.13), channel_id=1, source_target_pairs={{0,16},{4,20},{8,12},{12,8},{16,0},{20,4},{24,28},{28,24},{1,17},{... | collective-permute-start | bytes 1572872 | tf_op jit(solution)/shard_map/ppermute | solution.py:395
  3.6 31.5 %collective-permute-start.2 = (bf16[512,512]{1,0:T(8,128)(2,1)}, bf16[512,512]{1,0:T(8,128)(2,1)}, u32[]{:S(2)}, u32[]{:S(2)}) collective-permute-start(bf16[512,512]{1,0:T(8,128)(2,1)} %param.13), channel_id=1, source_target_pairs={{0,2},{1,3},{2,0},{3,1},{4,6},{5,7},{6,4},{7,5},{8,10},{9,11},{10,... | collective-permute-start | bytes 1572872 | tf_op jit(solution)/shard_map/ppermute | solution.py:411
  8.1 1.2 copy-start.4
  9.3 0.7 copy-start.8
  10.0 5.5 %copy-start.15 = (bf16[512,512]{1,0:T(8,128)(2,1)S(1)}, bf16[512,512]{1,0:T(8,128)(2,1)}, u32[]{:S(2)}) copy-start(bf16[512,512]{1,0:T(8,128)(2,1)} %param.13) | copy-start | bytes 1572868
  14.8 6.3 %collective-permute-start = (bf16[512,128]{1,0:T(8,128)(2,1)S(1)}, bf16[512,128]{1,0:T(8,128)(2,1)S(1)}, u32[]{:S(2)}, u32[]{:S(2)}) collective-permute-start(bf16[512,128]{1,0:T(8,128)(2,1)S(1)} %pool.1), channel_id=1, source_target_pairs={{0,16},{4,20},{8,12},{12,8},{16,0},{20,4},{24,28},{28,24},{1,17},{... | collective-permute-start | bytes 393224 | tf_op jit(solution)/shard_map/ppermute | solution.py:395
  15.4 19.7 %collective-permute-start.1 = (bf16[512,128]{1,0:T(8,128)(2,1)S(1)}, bf16[512,128]{1,0:T(8,128)(2,1)S(1)}, u32[]{:S(2)}, u32[]{:S(2)}) collective-permute-start(bf16[512,128]{1,0:T(8,128)(2,1)S(1)} %pool.1), channel_id=1, source_target_pairs={{0,2},{1,3},{2,0},{3,1},{4,6},{5,7},{6,4},{7,5},{8,10},{9,11},{10,... | collective-permute-start | bytes 393224 | tf_op jit(solution)/shard_map/ppermute | solution.py:411
  15.5 37.2 %collective-permute-start.6 = (bf16[2,512,512]{2,1,0:T(8,128)(2,1)S(1)}, bf16[2,512,512]{2,1,0:T(8,128)(2,1)}, u32[]{:S(2)}, u32[]{:S(2)}) collective-permute-start(bf16[2,512,512]{2,1,0:T(8,128)(2,1)S(1)} %pad_maximum_fusion.2.refs_0_), channel_id=1, source_target_pairs={{0,1},{1,0},{2,3},{3,2},{4,5},{5,4},{6,7},{7,6},{8,9},{9,8},{10,11... | collective-permute-start | bytes 3145736 | tf_op jit(solution)/shard_map/ppermute | solution.py:411
  17.5 37.5 %collective-permute-start.7 = (bf16[2,512,512]{2,1,0:T(8,128)(2,1)S(1)}, bf16[2,512,512]{2,1,0:T(8,128)(2,1)S(1)}, u32[]{:S(2)}, u32[]{:S(2)}) collective-permute-start(bf16[2,512,512]{2,1,0:T(8,128)(2,1)S(1)} %pad_maximum_fusion.2.refs_0_), channel_id=1, source_target_pairs={{0,4},{4,0},{8,24},{12,28},{16,20},{20,16},{24,8},{28,12},{1,5},{5... | collective-permute-start | bytes 3145736 | tf_op jit(solution)/shard_map/ppermute | solution.py:399
  35.1 0.7 copy-start.16
  37.7 12.3 %collective-permute-start.3 = (bf16[512,640]{1,0:T(8,128)(2,1)}, bf16[512,640]{1,0:T(8,128)(2,1)S(1)}, u32[]{:S(2)}, u32[]{:S(2)}) collective-permute-start(bf16[512,640]{1,0:T(8,128)(2,1)} %carry.1), channel_id=1, source_target_pairs={{0,16},{4,20},{8,12},{12,8},{16,0},{20,4},{24,28},{28,24},{1,17},{... | collective-permute-start | bytes 1966088 | tf_op jit(solution)/shard_map/ppermute | solution.py:395
  39.3 9.2 %collective-permute-start.4 = (bf16[2,512,128]{2,1,0:T(8,128)(2,1)S(1)}, bf16[2,512,128]{2,1,0:T(8,128)(2,1)S(1)}, u32[]{:S(2)}, u32[]{:S(2)}) collective-permute-start(bf16[2,512,128]{2,1,0:T(8,128)(2,1)S(1)} %pad_maximum_fusion.3), channel_id=1, source_target_pairs={{0,4},{4,0},{8,24},{12,28},{16,20},{20,16},{24,8},{28,12},{1,5},{5... | collective-permute-start | bytes 786440 | tf_op jit(solution)/shard_map/ppermute | solution.py:399
  55.0 2.8 %collective-permute-start.9 = (bf16[2,512,512]{2,1,0:T(8,128)(2,1)S(1)}, bf16[2,512,512]{2,1,0:T(8,128)(2,1)}, u32[]{:S(2)}, u32[]{:S(2)}) collective-permute-start(bf16[2,512,512]{2,1,0:T(8,128)(2,1)S(1)} %pad_maximum_fusion.2.refs_0_), channel_id=1, source_target_pairs={{0,8},{8,0},{16,24},{24,16},{1,9},{9,1},{17,25},{25,17},{2,10},{10... | collective-permute-start | bytes 3145736 | tf_op jit(solution)/shard_map/ppermute | solution.py:407
  55.0 21.3 %copy-start.1 = (bf16[2,512,512]{2,1,0:T(8,128)(2,1)}, bf16[2,512,512]{2,1,0:T(8,128)(2,1)S(1)}, u32[]{:S(2)}) copy-start(bf16[2,512,512]{2,1,0:T(8,128)(2,1)S(1)} %collective-permute-done.7.refs_1_) | copy-start | bytes 3145732
  55.0 5.0 %collective-permute-start.8 = (bf16[2,512,512]{2,1,0:T(8,128)(2,1)S(1)}, bf16[2,512,512]{2,1,0:T(8,128)(2,1)}, u32[]{:S(2)}, u32[]{:S(2)}) collective-permute-start(bf16[2,512,512]{2,1,0:T(8,128)(2,1)S(1)} %collective-permute-done.7.refs_1_), channel_id=1, source_target_pairs={{0,8},{8,0},{16,24},{24,16},{1,9},{9,1},{17,25},{25,17},{2,10},{10... | collective-permute-start | bytes 3145736 | tf_op jit(solution)/shard_map/ppermute | solution.py:407
  55.5 4.5 %collective-permute-start.10 = (bf16[4,512,128]{2,1,0:T(8,128)(2,1)S(1)}, bf16[4,512,128]{2,1,0:T(8,128)(2,1)S(1)}, u32[]{:S(2)}, u32[]{:S(2)}) collective-permute-start(bf16[4,512,128]{2,1,0:T(8,128)(2,1)S(1)} %constant_dynamic-update-slice_fusion.feat_ref.refs_8_), channel_id=1, source_target_pairs={{0,8},{8,0},{16,24},{24,16},{1,9},{9,1},{17,25},{25,17},{2,10},{10... | collective-permute-start | bytes 1572872 | tf_op jit(solution)/shard_map/ppermute | solution.py:407
  55.6 20.8 %collective-permute-start.12 = (bf16[2,512,640]{2,1,0:T(8,128)(2,1)}, bf16[2,512,640]{2,1,0:T(8,128)(2,1)}, u32[]{:S(2)}, u32[]{:S(2)}) collective-permute-start(bf16[2,512,640]{2,1,0:T(8,128)(2,1)} %pad_maximum_fusion.refs_4_.refs_10_), channel_id=1, source_target_pairs={{0,4},{4,0},{8,24},{12,28},{16,20},{20,16},{24,8},{28,12},{1,5},{5... | collective-permute-start | bytes 3932168 | tf_op jit(solution)/shard_map/ppermute | solution.py:399
  57.2 19.1 %collective-permute-start.11 = (bf16[512,640]{1,0:T(8,128)(2,1)}, bf16[512,640]{1,0:T(8,128)(2,1)}, u32[]{:S(2)}, u32[]{:S(2)}) collective-permute-start(bf16[512,640]{1,0:T(8,128)(2,1)} %carry.1), channel_id=1, source_target_pairs={{0,1},{1,0},{2,3},{3,2},{4,5},{5,4},{6,7},{7,6},{8,9},{9,8},{10,11... | collective-permute-start | bytes 1966088 | tf_op jit(solution)/shard_map/ppermute | solution.py:411
  76.4 3.6 %collective-permute-start.14 = (bf16[2,512,640]{2,1,0:T(8,128)(2,1)}, bf16[2,512,640]{2,1,0:T(8,128)(2,1)S(1)}, u32[]{:S(2)}, u32[]{:S(2)}) collective-permute-start(bf16[2,512,640]{2,1,0:T(8,128)(2,1)} %pad_maximum_fusion.refs_4_.refs_10_), channel_id=1, source_target_pairs={{0,8},{8,0},{16,24},{24,16},{1,9},{9,1},{17,25},{25,17},{2,10},{10... | collective-permute-start | bytes 3932168 | tf_op jit(solution)/shard_map/ppermute | solution.py:407
  76.6 5.0 %collective-permute-start.15 = (bf16[2,512,640]{2,1,0:T(8,128)(2,1)}, bf16[2,512,640]{2,1,0:T(8,128)(2,1)S(1)}, u32[]{:S(2)}, u32[]{:S(2)}) collective-permute-start(bf16[2,512,640]{2,1,0:T(8,128)(2,1)} %collective-permute-done.12.refs_5_.refs_11_), channel_id=1, source_target_pairs={{0,8},{8,0},{16,24},{24,16},{1,9},{9,1},{17,25},{25,17},{2,10},{10... | collective-permute-start | bytes 3932168 | tf_op jit(solution)/shard_map/ppermute | solution.py:407
  77.0 22.0 %collective-permute-start.16 = (bf16[2,512,512]{2,1,0:T(8,128)(2,1)}, bf16[2,512,512]{2,1,0:T(8,128)(2,1)S(1)}, u32[]{:S(2)}, u32[]{:S(2)}) collective-permute-start(bf16[2,512,512]{2,1,0:T(8,128)(2,1)} %collective-permute-done.6.refs_0_.refs_8_), channel_id=1, source_target_pairs={{0,4},{4,0},{8,24},{12,28},{16,20},{20,16},{24,8},{28,12},{1,5},{5... | collective-permute-start | bytes 3145736 | tf_op jit(solution)/shard_map/ppermute | solution.py:399
  78.5 18.0 %collective-permute-start.13 = (bf16[512,640]{1,0:T(8,128)(2,1)}, bf16[512,640]{1,0:T(8,128)(2,1)}, u32[]{:S(2)}, u32[]{:S(2)}) collective-permute-start(bf16[512,640]{1,0:T(8,128)(2,1)} %collective-permute-done.11), channel_id=1, source_target_pairs={{0,16},{4,20},{8,12},{12,8},{16,0},{20,4},{24,28},{28,24},{1,17},{... | collective-permute-start | bytes 1966088 | tf_op jit(solution)/shard_map/ppermute | solution.py:395
  80.0 16.2 %collective-permute-start.17 = (bf16[4,512,128]{2,1,0:T(8,128)(2,1)S(1)}, bf16[4,512,128]{2,1,0:T(8,128)(2,1)S(1)}, u32[]{:S(2)}, u32[]{:S(2)}) collective-permute-start(bf16[4,512,128]{2,1,0:T(8,128)(2,1)S(1)} %constant_dynamic-update-slice_fusion.feat_ref.refs_8_), channel_id=1, source_target_pairs={{0,1},{1,0},{2,3},{3,2},{4,5},{5,4},{6,7},{7,6},{8,9},{9,8},{10,11... | collective-permute-start | bytes 1572872 | tf_op jit(solution)/shard_map/ppermute | solution.py:411
  80.0 1.5 copy-start.9
  81.6 1.0 copy-start.10
  82.6 22.4 %copy-start.11 = (f32[4,512,512]{2,1,0:T(8,128)S(1)}, f32[4,512,512]{2,1,0:T(8,128)}, u32[]{:S(2)}) copy-start(f32[4,512,512]{2,1,0:T(8,128)} %get-tuple-element.55) | copy-start | bytes 12582916
  96.2 10.6 %copy-start.5 = (bf16[512,1024]{1,0:T(8,128)(2,1)}, bf16[512,1024]{1,0:T(8,128)(2,1)S(1)}, u32[]{:S(2)}) copy-start(bf16[512,1024]{1,0:T(8,128)(2,1)S(1)} %get-tuple-element.77.refs_16_) | copy-start | bytes 3145732
  99.0 9.8 %copy-start.3 = (bf16[2,512,512]{2,1,0:T(8,128)(2,1)}, bf16[2,512,512]{2,1,0:T(8,128)(2,1)S(1)}, u32[]{:S(2)}) copy-start(bf16[2,512,512]{2,1,0:T(8,128)(2,1)S(1)} %collective-permute-done.16.refs_1_.refs_9_) | copy-start | bytes 3145732
  100.8 23.9 %copy-start = (bf16[2,512,640]{2,1,0:T(8,128)(2,1)}, bf16[2,512,640]{2,1,0:T(8,128)(2,1)S(1)}, u32[]{:S(2)}) copy-start(bf16[2,512,640]{2,1,0:T(8,128)(2,1)S(1)} %pad_maximum_fusion.1.refs_0_.refs_4_.refs_12_) | copy-start | bytes 3932164
  100.8 4.2 %collective-permute-start.18 = (bf16[4,512,512]{2,1,0:T(8,128)(2,1)S(1)}, bf16[4,512,512]{2,1,0:T(8,128)(2,1)S(1)}, u32[]{:S(2)}, u32[]{:S(2)}) collective-permute-start(bf16[4,512,512]{2,1,0:T(8,128)(2,1)S(1)} %get-tuple-element.66), channel_id=1, source_target_pairs={{0,8},{8,0},{16,24},{24,16},{1,9},{9,1},{17,25},{25,17},{2,10},{10... | collective-permute-start | bytes 6291464 | tf_op jit(solution)/shard_map/ppermute | solution.py:407
  100.9 7.9 %collective-permute-start.24 = (bf16[2,512,512]{2,1,0:T(8,128)(2,1)S(1)}, bf16[2,512,512]{2,1,0:T(8,128)(2,1)S(1)}, u32[]{:S(2)}, u32[]{:S(2)}) collective-permute-start(bf16[2,512,512]{2,1,0:T(8,128)(2,1)S(1)} %collective-permute-done.16.refs_1_.refs_9_), channel_id=1, source_target_pairs={{0,8},{8,0},{16,24},{24,16},{1,9},{9,1},{17,25},{25,17},{2,10},{10... | collective-permute-start | bytes 3145736 | tf_op jit(solution)/shard_map/ppermute | solution.py:407
  101.4 7.4 %collective-permute-start.23 = (bf16[2,512,512]{2,1,0:T(8,128)(2,1)}, bf16[2,512,512]{2,1,0:T(8,128)(2,1)}, u32[]{:S(2)}, u32[]{:S(2)}) collective-permute-start(bf16[2,512,512]{2,1,0:T(8,128)(2,1)} %collective-permute-done.6.refs_0_.refs_8_), channel_id=1, source_target_pairs={{0,8},{8,0},{16,24},{24,16},{1,9},{9,1},{17,25},{25,17},{2,10},{10... | collective-permute-start | bytes 3145736 | tf_op jit(solution)/shard_map/ppermute | solution.py:407
  101.5 18.2 %collective-permute-start.22 = (bf16[2,512,640]{2,1,0:T(8,128)(2,1)S(1)}, bf16[2,512,640]{2,1,0:T(8,128)(2,1)}, u32[]{:S(2)}, u32[]{:S(2)}) collective-permute-start(bf16[2,512,640]{2,1,0:T(8,128)(2,1)S(1)} %pad_maximum_fusion.1.refs_0_.refs_4_.refs_12_), channel_id=1, source_target_pairs={{0,4},{4,0},{8,24},{12,28},{16,20},{20,16},{24,8},{28,12},{1,5},{5... | collective-permute-start | bytes 3932168 | tf_op jit(solution)/shard_map/ppermute | solution.py:399
  103.0 5.8 %collective-permute-start.25 = (bf16[4,512,128]{2,1,0:T(8,128)(2,1)S(1)}, bf16[4,512,128]{2,1,0:T(8,128)(2,1)S(1)}, u32[]{:S(2)}, u32[]{:S(2)}) collective-permute-start(bf16[4,512,128]{2,1,0:T(8,128)(2,1)S(1)} %collective-permute-done.17.refs_4_), channel_id=1, source_target_pairs={{0,8},{8,0},{16,24},{24,16},{1,9},{9,1},{17,25},{25,17},{2,10},{10... | collective-permute-start | bytes 1572872 | tf_op jit(solution)/shard_map/ppermute | solution.py:407
  105.0 1.8 %copy-start.13 = (bf16[4,512,512]{2,1,0:T(8,128)(2,1)}, bf16[4,512,512]{2,1,0:T(8,128)(2,1)S(1)}, u32[]{:S(2)}) copy-start(bf16[4,512,512]{2,1,0:T(8,128)(2,1)S(1)} %collective-permute-done.18) | copy-start | bytes 6291460
  108.8 1.0 copy-start.14
  118.8 0.8 copy-start.6
  119.6 4.2 %collective-permute-start.26 = (bf16[2,512,640]{2,1,0:T(8,128)(2,1)}, bf16[2,512,640]{2,1,0:T(8,128)(2,1)}, u32[]{:S(2)}, u32[]{:S(2)}) collective-permute-start(bf16[2,512,640]{2,1,0:T(8,128)(2,1)} %collective-permute-done.22.refs_1_.refs_5_.refs_13_), channel_id=1, source_target_pairs={{0,8},{8,0},{16,24},{24,16},{1,9},{9,1},{17,25},{25,17},{2,10},{10... | collective-permute-start | bytes 3932168 | tf_op jit(solution)/shard_map/ppermute | solution.py:407
  119.8 4.9 %collective-permute-start.27 = (bf16[2,512,640]{2,1,0:T(8,128)(2,1)S(1)}, bf16[2,512,640]{2,1,0:T(8,128)(2,1)}, u32[]{:S(2)}, u32[]{:S(2)}) collective-permute-start(bf16[2,512,640]{2,1,0:T(8,128)(2,1)S(1)} %pad_maximum_fusion.1.refs_0_.refs_4_.refs_12_), channel_id=1, source_target_pairs={{0,8},{8,0},{16,24},{24,16},{1,9},{9,1},{17,25},{25,17},{2,10},{10... | collective-permute-start | bytes 3932168 | tf_op jit(solution)/shard_map/ppermute | solution.py:407
  120.2 17.9 %copy-start.2 = (bf16[2,512,512]{2,1,0:T(8,128)(2,1)S(1)}, bf16[2,512,512]{2,1,0:T(8,128)(2,1)}, u32[]{:S(2)}) copy-start(bf16[2,512,512]{2,1,0:T(8,128)(2,1)} %copy-done.1) | copy-start | bytes 3145732
  120.2 17.9 %copy-start.7 = (bf16[512,512]{1,0:T(8,128)(2,1)S(1)}, bf16[512,512]{1,0:T(8,128)(2,1)}, u32[]{:S(2)}) copy-start(bf16[512,512]{1,0:T(8,128)(2,1)} %copy-done.6) | copy-start | bytes 1572868
  120.2 17.2 %collective-permute-start.19 = (bf16[512,512]{1,0:T(8,128)(2,1)}, bf16[512,512]{1,0:T(8,128)(2,1)S(1)}, u32[]{:S(2)}, u32[]{:S(2)}) collective-permute-start(bf16[512,512]{1,0:T(8,128)(2,1)} %get-tuple-element.89), channel_id=1, source_target_pairs={{0,16},{4,20},{8,12},{12,8},{16,0},{20,4},{24,28},{28,24},{1,17},{... | collective-permute-start | bytes 1572872 | tf_op jit(solution)/shard_map/ppermute | solution.py:395
  121.2 32.7 %collective-permute-start.20 = (bf16[512,512]{1,0:T(8,128)(2,1)}, bf16[512,512]{1,0:T(8,128)(2,1)S(1)}, u32[]{:S(2)}, u32[]{:S(2)}) collective-permute-start(bf16[512,512]{1,0:T(8,128)(2,1)} %get-tuple-element.88), channel_id=1, source_target_pairs={{0,4},{4,0},{8,24},{12,28},{16,20},{20,16},{24,8},{28,12},{1,5},{5... | collective-permute-start | bytes 1572872 | tf_op jit(solution)/shard_map/ppermute | solution.py:399
  122.8 31.2 %collective-permute-start.21 = (bf16[512,512]{1,0:T(8,128)(2,1)}, bf16[512,512]{1,0:T(8,128)(2,1)S(1)}, u32[]{:S(2)}, u32[]{:S(2)}) collective-permute-start(bf16[512,512]{1,0:T(8,128)(2,1)} %get-tuple-element.87), channel_id=1, source_target_pairs={{0,20},{4,16},{8,28},{12,24},{16,4},{20,0},{24,12},{28,8},{1,21},{... | collective-permute-start | bytes 1572872 | tf_op jit(solution)/shard_map/ppermute | solution.py:403
  132.7 21.2 %collective-permute-start.28 = (bf16[256,512]{1,0:T(8,128)(2,1)S(1)}, bf16[256,512]{1,0:T(8,128)(2,1)S(1)}, u32[]{:S(2)}, u32[]{:S(2)}) collective-permute-start(bf16[256,512]{1,0:T(8,128)(2,1)S(1)} %get-tuple-element.92), channel_id=1, source_target_pairs={{0,3},{1,2},{2,1},{3,0},{4,7},{5,6},{6,5},{7,4},{8,11},{9,10},{10,... | collective-permute-start | bytes 786440 | tf_op jit(solution)/shard_map/ppermute | solution.py:411
  137.4 21.4 %collective-permute-start.29 = (bf16[256,512]{1,0:T(8,128)(2,1)S(1)}, bf16[256,512]{1,0:T(8,128)(2,1)S(1)}, u32[]{:S(2)}, u32[]{:S(2)}) collective-permute-start(bf16[256,512]{1,0:T(8,128)(2,1)S(1)} %get-tuple-element.91), channel_id=1, source_target_pairs={{0,2},{1,3},{2,0},{3,1},{4,6},{5,7},{6,4},{7,5},{8,10},{9,11},{10,... | collective-permute-start | bytes 786440 | tf_op jit(solution)/shard_map/ppermute | solution.py:411
  137.5 21.4 %collective-permute-start.30 = (bf16[256,512]{1,0:T(8,128)(2,1)S(1)}, bf16[256,512]{1,0:T(8,128)(2,1)S(1)}, u32[]{:S(2)}, u32[]{:S(2)}) collective-permute-start(bf16[256,512]{1,0:T(8,128)(2,1)S(1)} %get-tuple-element.90), channel_id=1, source_target_pairs={{0,1},{1,0},{2,3},{3,2},{4,5},{5,4},{6,7},{7,6},{8,9},{9,8},{10,11... | collective-permute-start | bytes 786440 | tf_op jit(solution)/shard_map/ppermute | solution.py:411
  159.1 3.3 %copy-start.12 = (f32[256,2048]{1,0:T(8,128)}, f32[256,2048]{1,0:T(8,128)S(1)}, u32[]{:S(2)}) copy-start(f32[256,2048]{1,0:T(8,128)S(1)} %convert_dynamic-update-slice_fusion) | copy-start | bytes 6291460
